TPU v7x, 32 devices: a whole 2x2x4 slice. The times are simulated.
32 devices in a mesh: br: 16 (over z, y, x), bus: 2 (over core).
Axes of the slice: x: 2, y: 2, z: 4, core: 2. Of those that a mesh axis runs over, the one named last changes fastest.
Arguments:
- shift_factors: bfloat16 [12288, 20480], P('br', 'bus'), may hold values from -0.0625 to 0.0625
- injections: bfloat16 [20480, 128], P(('bus', 'br')), may hold values from -6 to 6
- limits: float32 [12288], P(('br', 'bus')), may hold values from 0.2 to 2
- entry_row: int32 [16384], P(('br', 'bus')), may hold values from 0 to 383
- entry_owner: int32 [16384, 1], P(('br', 'bus')), may hold values from 0 to 15; in each aligned block of 512 rows (0 to 511, 512 to 1023, ...) at most 64 rows name the same one
- entry_slot: int32 [16384], P(('br', 'bus')), may hold values from 0 to 7
- outage_factor: float32 [16384], P(('br', 'bus')), may hold values from -1 to 1
- outage_row: int32 [128], P(('br', 'bus')), may hold values from 0 to 383
Outputs:
- injection_grad: float32 [20480, 128], P(('bus', 'br'))
Inputs may be any that keep to these rules, and one draw needn't show every extreme that they name: `entry_owner`: among the pairs of one device no owner appears more than 64 times, and in every draw some device names some owner exactly 64 times.
All inputs are finite; a program needn't handle non-finite values.
Results may differ from a plain program's by a relative error of at most 0.0016.
The roundings to bfloat16 on the way count: a program that leaves them out, or rounds other values in their place, can miss the bound.
Values may be sent and summed in bfloat16 or wider, within the bound.
No kernel may reach another device: no remote copies, remote signals or barrier semaphores. Data moves between devices by JAX's collectives and lax.ppermute only.
A program may use at most 64 MiB of HBM per device.

v0:
```python
import jax
import jax.numpy as jnp
from jax import lax
from jax.sharding import PartitionSpec as P

base_weight = 1.0
cont_weight = 0.25
emergency = 1.25


def on_device(
    shift_factors, injections, limits, entry_row, entry_owner, entry_slot, outage_factor, outage_row
):
    rows_group, bus_cols = shift_factors.shape
    br_count = lax.axis_size("br")
    bus_count = lax.axis_size("bus")
    rows_dev = rows_group // bus_count
    owned_conts = outage_row.shape[0]
    group_conts = owned_conts * bus_count
    factor_cols = shift_factors
    partial_flows = jnp.dot(
        factor_cols,
        lax.all_gather(injections, "br", axis=0, tiled=True),
        preferred_element_type=jnp.float32,
    )
    flows = lax.psum_scatter(partial_flows, "bus", scatter_dimension=0, tiled=True)
    limit_col = limits[:, None]
    base_adj = base_weight * (
        jnp.maximum(flows - limit_col, 0.0) + jnp.minimum(flows + limit_col, 0.0)
    )
    own_outage = jnp.take(flows, outage_row, axis=0)
    owner_ids = entry_owner[:, 0]
    all_outage = lax.all_gather(own_outage, ("br", "bus"), axis=0, tiled=True)
    contingency = owner_ids * group_conts + entry_slot
    fetched = jnp.take(all_outage, contingency, axis=0)
    post_flow = jnp.take(flows, entry_row, axis=0) + outage_factor[:, None] * fetched
    emerg_cap = emergency * jnp.take(limits, entry_row)[:, None]
    entry_adj = cont_weight * (
        jnp.maximum(post_flow - emerg_cap, 0.0) + jnp.minimum(post_flow + emerg_cap, 0.0)
    )
    weighted = outage_factor[:, None] * entry_adj
    local_rows = jnp.arange(rows_dev, dtype=jnp.int32)
    row_hot = (entry_row[:, None] == local_rows[None, :]).astype(jnp.float32)
    monitored_adj = lax.dot_general(
        row_hot,
        entry_adj,
        (((0,), (0,)), ((), ())),
        precision=lax.Precision.HIGHEST,
        preferred_element_type=jnp.float32,
    )
    every_part = jax.ops.segment_sum(
        weighted, contingency, num_segments=owned_conts * br_count * bus_count
    )
    owned_adj = lax.psum_scatter(every_part, ("br", "bus"), scatter_dimension=0, tiled=True)
    outage_hot = (outage_row[:, None] == local_rows[None, :]).astype(jnp.float32)
    outage_adj = lax.dot_general(
        outage_hot,
        owned_adj,
        (((0,), (0,)), ((), ())),
        precision=lax.Precision.HIGHEST,
        preferred_element_type=jnp.float32,
    )
    adjoint = (base_adj + monitored_adj + outage_adj).astype(jnp.bfloat16)
    group_adjoint = lax.all_gather(adjoint, "bus", axis=0, tiled=True)
    factor_cols = shift_factors
    return lax.psum_scatter(
        lax.dot_general(
            factor_cols, group_adjoint, (((0,), (0,)), ((), ())), preferred_element_type=jnp.float32
        ),
        "br",
        scatter_dimension=0,
        tiled=True,
    )


def solution(mesh):
    in_specs = (
        P("br", "bus"),
        P(("bus", "br"), None),
        P(("br", "bus")),
        P(("br", "bus")),
        P(("br", "bus"), None),
        P(("br", "bus")),
        P(("br", "bus")),
        P(("br", "bus")),
    )
    out_specs = P(("bus", "br"), None)
    return jax.shard_map(
        on_device, mesh=mesh, in_specs=in_specs, out_specs=out_specs, check_vma=False
    )
```

profile of v0, /device:TPU:0, one launch (start us, length us, event | category | flops | bytes accessed | tf_op | source)
XLA Modules:
  0.0 398.3 jit_solution(8383836613717565397)
XLA Ops:
  6.6 0.7 all-gather.3.cloned.1.call-update
  7.3 0.7 broadcast_multiply_fusion.1
  8.0 0.7 compare_and_fusion.1
  8.7 0.7 compare_select_fusion.2
  9.4 0.7 compare_select_fusion.1
  10.1 66.7 %all-gather.3.cloned.1.call-done = bf16[10240,128]{1,0:T(8,128)(2,1)} async-done(((bf16[640,128]{1,0:T(8,128)(2,1)}), bf16[10240,128]{1,0:T(8,128)(2,1)}) %all-gather.3.cloned.1.call-update) | async-done | bytes 2621456 | tf_op jit(solution)/shard_map/all_gather | solution.py:23
  76.8 11.2 %fusion.14 = f32[768,128]{1,0:T(8,128)} fusion(bf16[768,10240]{1,0:T(8,128)(2,1)} %param.8, bf16[10240,128]{1,0:T(8,128)(2,1)} %all-gather.3.cloned.1.call-done), kind=kOutput, calls=%fused_computation.37 | convolution fusion | flops 2013265920 | bytes 18743296 | tf_op jit(solution)/shard_map/dot_general | solution.py:21
  88.0 0.0 all-reduce.3.cloned.1.call-start
  88.1 3.5 gather_fusion.3
  91.7 3.2 reduce-scatter.3.cloned.1.call-done
  94.9 1.5 gather_fusion.1
  96.4 0.1 select_bitcast_fusion
  96.4 41.8 %all-gather = f32[32,4,128]{2,1,0:T(4,128)S(1)} all-gather(f32[1,4,128]{2,1,0:T(4,128)S(1)} %select_bitcast_fusion), channel_id=1, replica_groups=mesh['br'=16,'bus'=2] {'br','bus'}, dimensions={0}, use_global_device_ids=true | all-gather | bytes 67584 | tf_op jit(solution)/shard_map/all_gather | solution.py:33
  138.3 1.0 gather_fusion.2
  139.3 2.0 gather_fusion
  141.3 0.3 minimum_add_fusion
  141.6 3.0 scatter_custom_fusion
  144.6 113.7 %all-reduce.3.cloned.1.call-done = f32[128,128]{1,0:T(8,128)} async-done(((f32[128,128]{1,0:T(8,128)}), f32[128,128]{1,0:T(8,128)}) %all-reduce.3.cloned.1.call-update) | async-done | bytes 65552
  258.4 1.1 fusion.9
  259.5 1.8 fusion.1
  261.3 3.2 all_gather.11
  264.5 10.1 %convolution_bitcast_fusion = f32[10240,128]{0,1:T(8,128)} fusion(bf16[768,128]{1,0:T(8,128)(2,1)S(1)} %all_gather.11, bf16[768,10240]{1,0:T(8,128)(2,1)} %param.8), kind=kOutput, calls=%fused_computation.5 | convolution fusion | flops 2013265920 | bytes 21168128 | tf_op jit(solution)/shard_map/dot_general | solution.py:67
  274.7 115.2 %reduce-scatter.5.cloned.1.call-done = f32[640,128]{0,1:T(8,128)} async-done(((f32[10240,128]{0,1:T(8,128)}), f32[640,128]{0,1:T(8,128)}) %reduce-scatter.5.cloned.1.call-update) | async-done | bytes 327696 | tf_op jit(solution)/shard_map/reduce_scatter | solution.py:66
  389.9 1.9 copy.11
  (21 shorter events, 0.2 us)
Async XLA Ops:
  6.5 85.1 %copy-start.3 = (s32[4]{0:T(128)S(1)}, s32[4]{0:T(128)}, u32[]{:S(2)}) copy-start(s32[4]{0:T(128)} %param.15) | copy-start | bytes 52
  6.5 85.1 %copy-start.2 = (s32[512]{0:T(512)S(1)}, s32[512]{0:T(512)}, u32[]{:S(2)}) copy-start(s32[512]{0:T(512)} %param.11) | copy-start | bytes 6148
  6.5 81.5 %copy-start = (f32[384]{0:T(512)S(1)}, f32[384]{0:T(512)}, u32[]{:S(2)}) copy-start(f32[384]{0:T(512)} %param.10) | copy-start | bytes 4612
  6.5 85.1 %copy-start.1 = (f32[512]{0:T(512)S(1)}, f32[512]{0:T(512)}, u32[]{:S(2)}) copy-start(f32[512]{0:T(512)} %param.14) | copy-start | bytes 6148
  6.5 70.3 %all-gather.3.cloned.1.call-start = ((), (), s32[]{:S(2)}) async-start(), calls=%async_computation.2 | async-start | bytes 2785280 | tf_op jit(solution)/shard_map/all_gather | solution.py:23
  7.3 87.6 %reduce-scatter.3.cloned.1.call-start = ((), (), s32[]{:S(2)}) async-start(), calls=%async_computation.3 | async-start | bytes 589824 | tf_op jit(solution)/shard_map/reduce_scatter | solution.py:26
  88.0 170.4 %all-reduce.3.cloned.1.call-start = ((), (), s32[]{:S(2)}) async-start(), calls=%async_computation.5 | async-start | bytes 131072
  144.6 245.3 %reduce-scatter.5.cloned.1.call-start = ((), (), s32[]{:S(2)}) async-start(), calls=%async_computation.4 | async-start | bytes 5570560 | tf_op jit(solution)/shard_map/reduce_scatter | solution.py:66
Sparse Core Ops, SparseCore 0:
  10.1 66.6 all-gather.2
  88.1 6.6 reduce-scatter.2
  144.7 113.6 all-reduce.2
  274.8 115.0 reduce-scatter.4
where the time goes:
time: 399 us; the launch traced here: 398 us
  waiting for transfers between devices  300 us (75%)
  blocking collectives  45 us (11%)
  matrix products  24.2 us (6%)
  between operations  13.3 us (3%)
  local copies, waits for them, and re-layouts  9.84 us (2%)
  other arithmetic  6.13 us (2%)
    reduce_scatter x1, waiting for transfers between devices, on_device(): lax.psum_scatter(lax.dot_general(factor_cols, group_adjoint, (((0,), (0,)...  115 us
    unnamed x5, waiting for transfers between devices  114 us
    all_gather x1, waiting for transfers between devices, on_device(): lax.all_gather(injections, 'br', axis=0, tiled=True)  66.7 us
    all_gather x1, blocking collectives, on_device(): all_outage = lax.all_gather(own_outage, ('br', 'bus'), axis=0, tiled=True)  41.8 us
    dot_general x1, matrix products, on_device(): jnp.dot(factor_cols, lax.all_gather(injections, 'br', axis=0, tiled=True)...  11.2 us
    dot_general x1, matrix products, on_device(): lax.dot_general(factor_cols, group_adjoint, (((0,), (0,)), ((), ())), pre...  10.1 us
  transfers between devices with their start and end apart: 4, of which 4 were waited for; matrix products, arithmetic and copies ran while one was open for 2% of the time, Pallas kernels for 0%

commit v1 on v0

--- a/solution.py
+++ b/solution.py
@@ -1,11 +1,296 @@
+import functools
+
 import jax
 import jax.numpy as jnp
 from jax import lax
+from jax.experimental import pallas as pl
+from jax.experimental.pallas import tpu as pltpu
 from jax.sharding import PartitionSpec as P
 
 base_weight = 1.0
 cont_weight = 0.25
 emergency = 1.25
+
+F32 = jnp.float32
+BF16 = jnp.bfloat16
+VM = pl.BlockSpec(memory_space=pltpu.VMEM)
+SM = pl.BlockSpec(memory_space=pltpu.SMEM)
+LEVELS = 32000.0
+LANES = 128
+
+
+def call(body, out_shape, in_specs, name, scratch=(), flops=0, nbytes=0, limit=24):
+    many = isinstance(out_shape, (tuple, list))
+    return pl.pallas_call(
+        body,
+        out_shape=out_shape,
+        in_specs=in_specs,
+        out_specs=[VM] * len(out_shape) if many else VM,
+        scratch_shapes=list(scratch),
+        compiler_params=pltpu.CompilerParams(vmem_limit_bytes=limit << 20),
+        cost_estimate=pl.CostEstimate(flops=flops, bytes_accessed=nbytes, transcendentals=0),
+        name=name,
+    )
+
+
+def sds(shape, dtype):
+    return jax.ShapeDtypeStruct(shape, dtype)
+
+
+def forward(factors, shards, places, plane, total, name, rows_out=None):
+    rows = factors.shape[0]
+    width, scen = shards[0].shape
+    n = len(shards)
+    scal = jnp.stack([plane, *places]).astype(jnp.int32)
+    keep = total is not None
+
+    def body(scal_ref, f_ref, *refs):
+        ins, refs = refs[:n], refs[n:]
+        tot_ref, refs = (refs[0], refs[1:]) if keep else (None, refs)
+        out_ref, buf = refs
+        for g in range(n):
+            buf[pl.ds(pl.multiple_of(scal_ref[1 + g] * width, width), width), :] = ins[g][...]
+        start = pl.multiple_of(scal_ref[0] * width, width)
+        part = jnp.dot(f_ref[:, pl.ds(start, n * width)], buf[...], preferred_element_type=F32)
+        out_ref[...] = part + tot_ref[...] if keep else part
+
+    ops = [scal, factors, *shards] + ([total] if keep else [])
+    return call(
+        body,
+        sds((rows, scen), F32),
+        [SM] + [VM] * (len(ops) - 1),
+        name,
+        [pltpu.VMEM((n * width, scen), BF16)],
+        flops=2 * rows * n * width * scen,
+        nbytes=n * width * (rows + scen) * 2,
+    )(*ops)
+
+
+def put_coded(ref, blocks):
+    width = blocks[0].shape[1]
+    top = functools.reduce(
+        jnp.maximum, [jnp.max(jnp.abs(b), axis=1, keepdims=True) for b in blocks]
+    )
+    power = jnp.ceil(jnp.log2(jnp.maximum(top, 1e-30)))
+    scale = jnp.exp2(-power) * LEVELS
+    for n, b in enumerate(blocks):
+        ref[:, n * width : (n + 1) * width] = jnp.round(b * scale).astype(jnp.int32).astype(jnp.int16)
+    end = len(blocks) * width
+    ref[:, end:] = jnp.broadcast_to(power, (ref.shape[0], LANES)).astype(jnp.int32).astype(jnp.int16)
+
+
+def get_coded(ref, n, width):
+    power = ref[:, ref.shape[1] - LANES :].astype(jnp.int32).astype(F32)[:, :1]
+    scale = jnp.exp2(power) * (1.0 / LEVELS)
+    return ref[:, n * width : (n + 1) * width].astype(jnp.int32).astype(F32) * scale
+
+
+def three(x):
+    high = x.astype(BF16)
+    rest = x - high.astype(F32)
+    middle = rest.astype(BF16)
+    low = (rest - middle.astype(F32)).astype(BF16)
+    return jnp.concatenate([high, middle, low], axis=1)
+
+
+def pick(hot, x):
+    n = x.shape[1]
+    y = jnp.dot(hot, three(x), preferred_element_type=F32)
+    return y[:, :n] + y[:, n : 2 * n] + y[:, 2 * n :]
+
+
+def one_hot(hit):
+    return jnp.where(hit, 1.0, 0.0).astype(BF16)
+
+
+def overload(x, cap):
+    return jnp.maximum(x - cap, 0.0) + jnp.minimum(x + cap, 0.0)
+
+
+def on_slice(
+    shift_factors, injections, limits, entry_row, entry_owner, entry_slot, outage_factor, outage_row
+):
+    rows, cols = shift_factors.shape
+    width, scen = injections.shape
+    half = rows // 2
+    pairs = entry_row.shape[0]
+    owned = outage_row.shape[0]
+    me = lax.axis_index("br")
+    core = lax.axis_index("bus")
+    zz, spot = me // 4, me % 4
+    mid = (zz == 1) | (zz == 2)
+
+    def index(z, y, x):
+        return z * 4 + y * 2 + x
+
+    chips = [(z, y, x) for z in range(4) for y in range(2) for x in range(2)]
+    to_x = [(index(z, y, x), index(z, y, 1 - x)) for z, y, x in chips]
+    to_y = [(index(z, y, x), index(z, 1 - y, x)) for z, y, x in chips]
+    to_z = {k: [(index(z, y, x), index(z ^ k, y, x)) for z, y, x in chips] for k in (1, 2, 3)}
+    inner = [(index(z, y, x), index(3 - z, y, x)) for z, y, x in chips if z in (1, 2)]
+    outward = [(index(z, y, x), index(z ^ 1, y, x)) for z, y, x in chips if z in (1, 2)]
+
+    def send(v, perm):
+        return lax.ppermute(v, "br", perm)
+
+    def swap(v):
+        return lax.ppermute(v, "bus", [(0, 1), (1, 0)])
+
+    own = injections
+    pair = send(own, to_z[1])
+    third_mid = send(own, inner)
+    own_x, own_y = send(own, to_x), send(own, to_y)
+    fourth_mid = send(pair, inner)
+    third_end = send(third_mid, outward)
+    pair_x, pair_y = send(pair, to_x), send(pair, to_y)
+    fourth_end = send(fourth_mid, outward)
+    third = jnp.where(mid, third_mid, third_end)
+    fourth = jnp.where(mid, fourth_mid, fourth_end)
+    third_x, third_y = send(third, to_x), send(third, to_y)
+    own_d = send(own_y, to_x)
+    pair_d = send(pair_x, to_y)
+    third_d = send(third_y, to_x)
+    fourth_x, fourth_y = send(fourth, to_x), send(fourth, to_y)
+    fourth_d = send(fourth_x, to_y)
+    low = zz < 2
+    z_third = jnp.where(low, 2, 1)
+    z_fourth = jnp.where(low, 3, 0)
+    places = [spot, spot ^ 1, spot ^ 2, spot ^ 3]
+
+    factors = pltpu.with_memory_space_constraint(shift_factors, pltpu.VMEM)
+    part = forward(factors, [own, own_x, own_y, own_d], places, zz * 4, None, "forward_own")
+    part = forward(factors, [pair, pair_x, pair_y, pair_d], places, (zz ^ 1) * 4, part, "forward_pair")
+    part = forward(factors, [third, third_x, third_y, third_d], places, z_third * 4, part, "forward_third")
+    part = forward(factors, [fourth, fourth_x, fourth_y, fourth_d], places, z_fourth * 4, part, "forward_fourth")
+
+    mine = lax.dynamic_slice_in_dim(part, core * half, half, 0)
+    theirs = lax.dynamic_slice_in_dim(part, (1 - core) * half, half, 0)
+    flows = mine + swap(theirs)
+
+    group = jnp.concatenate([lax.dynamic_slice_in_dim(flows, outage_row[t], 1, 0) for t in range(owned)], axis=0)
+    group = jnp.concatenate([group, swap(group)], axis=0)
+    group = jnp.concatenate([group, send(group, to_x)], axis=0)
+    group = jnp.concatenate([group, send(group, to_y)], axis=0)
+    outage = jnp.concatenate([group] + [send(group, to_z[k]) for k in (1, 2, 3)], axis=0)
+    conts = outage.shape[0]
+    own_first = (me * 2 + core) * owned
+    contingency = jnp.bitwise_xor(entry_owner[:, 0] * (2 * owned) + entry_slot, own_first)
+
+    def middle(flows_ref, out_ref, lim_ref, er_ref, ert_ref, ct_ref, ctt_ref, f_ref, limr_ref, adj_ref, every_ref):
+        flows = flows_ref[...]
+        hit = er_ref[...] == lax.broadcasted_iota(jnp.int32, (pairs, half), 1)
+        cap = emergency * jnp.sum(jnp.where(hit, limr_ref[...], 0.0), axis=1, keepdims=True)
+        cont = one_hot(ct_ref[...] == lax.broadcasted_iota(jnp.int32, (pairs, conts), 1))
+        factor = f_ref[...]
+        post = pick(one_hot(hit), flows) + factor * pick(cont, out_ref[...])
+        adj = cont_weight * overload(post, cap)
+        hot_t = one_hot(ert_ref[...] == lax.broadcasted_iota(jnp.int32, (half, pairs), 0))
+        cont_t = one_hot(ctt_ref[...] == lax.broadcasted_iota(jnp.int32, (conts, pairs), 0))
+        every_ref[...] = pick(cont_t, factor * adj)
+        adj_ref[...] = base_weight * overload(flows, lim_ref[...]) + pick(hot_t, adj)
+
+    adjoint, every = call(
+        middle, [sds((half, scen), F32), sds((conts, scen), F32)], [VM] * 9, "penalty"
+    )(
+        flows, outage, limits[:, None], entry_row[:, None], entry_row[None, :],
+        contingency[:, None], contingency[None, :], outage_factor[:, None], limits[None, :],
+    )
+
+    per_plane = conts // 4
+    got = [send(every[k * per_plane : (k + 1) * per_plane], to_z[k]) for k in (1, 2, 3)]
+    every = every[:per_plane] + got[0] + got[1] + got[2]
+    for step in (lambda v: send(v, to_y), lambda v: send(v, to_x), swap):
+        n = every.shape[0] // 2
+        every = every[:n] + step(every[n:])
+
+    def finish(row_ref, adj_ref, own_ref, out_ref):
+        place = lax.broadcasted_iota(jnp.int32, (half, scen), 0)
+        total = adj_ref[...]
+        for t in range(owned):
+            total = total + jnp.where(place == row_ref[t], own_ref[t : t + 1, :], 0.0)
+        out_ref[...] = total.T.astype(BF16)
+
+    adj_t = call(finish, sds((scen, half), BF16), [SM, VM, VM], "round")(outage_row, adjoint, every)
+    other_t = swap(adj_t)
+
+    scal = jnp.stack([core, *[((zz ^ k) * 4 + (spot ^ l)) for k in range(4) for l in range(4)]]).astype(jnp.int32)
+
+    def message(n):
+        return sds((scen, n * width + LANES), jnp.int16)
+
+    block = sds((scen, width), F32)
+
+    def backward(wanted, name, shapes, store):
+        def body(scal_ref, f_ref, a_ref, b_ref, *refs):
+            outs, adj = refs[:-1], refs[-1]
+            adj[:, pl.ds(pl.multiple_of(scal_ref[0] * half, half), half)] = a_ref[...]
+            adj[:, pl.ds(pl.multiple_of((1 - scal_ref[0]) * half, half), half)] = b_ref[...]
+
+            def grad(k, line):
+                first = pl.multiple_of(scal_ref[1 + 4 * k + line] * width, width)
+                return jnp.dot(adj[...], f_ref[:, pl.ds(first, width)], preferred_element_type=F32)
+
+            store(grad, outs)
+
+        return call(
+            body, shapes, [SM, VM, VM, VM], name, [pltpu.VMEM((scen, rows), BF16)],
+            flops=2 * rows * wanted * width * scen, nbytes=wanted * width * rows * 2,
+        )(scal, factors, adj_t, other_t)
+
+    def store_1(grad, outs):
+        put_coded(outs[0], [grad(3, 3), grad(3, 1)])
+        put_coded(outs[1], [grad(2, 3), grad(2, 2)])
+
+    x1, y1 = backward(4, "backward_first", [message(2), message(2)], store_1)
+    x1, y1 = send(x1, to_x), send(y1, to_y)
+
+    def store_2(grad, outs):
+        put_coded(outs[0], [grad(1, 3), grad(1, 1)])
+        put_coded(outs[1], [grad(0, 3), grad(0, 2)])
+        for ref, (k, line) in zip(outs[2:], ((2, 1), (3, 2), (0, 1), (1, 2), (0, 0), (1, 0), (2, 0), (3, 0))):
+            ref[...] = grad(k, line)
+
+    x2b, y2b, p2x, p3y, p0x, p1y, p0, p1, p2, p3 = backward(
+        12, "backward_rest", [message(2), message(2)] + [block] * 8, store_2
+    )
+
+    def add(name, *terms_of):
+        flat, plan = [], []
+        for terms in terms_of:
+            plan.append([])
+            for t in terms:
+                array, which = t if isinstance(t, tuple) else (t, None)
+                plan[-1].append((len(flat), which))
+                flat.append(array)
+
+        def body(*refs):
+            ins, outs = refs[: len(flat)], refs[len(flat) :]
+            for out, terms in zip(outs, plan):
+                total = None
+                for place, which in terms:
+                    v = ins[place][...] if which is None else get_coded(ins[place], which, width)
+                    total = v if total is None else total + v
+                put_coded(out, [total])
+
+        return call(body, [message(1)] * len(plan), [VM] * len(flat), name)(*flat)
+
+    x2a, y2a = add("sum_2", [p2x, (y1, 0)], [p3y, (x1, 0)])
+    x2a, y2a = send(x2a, to_x), send(y2a, to_y)
+    x2b, y2b = send(x2b, to_x), send(y2b, to_y)
+    z2, z3 = add("sum_z", [p2, (y1, 1), (x2a, 0)], [p3, (x1, 1), (y2a, 0)])
+    z3, z2 = send(z3, to_z[3]), send(z2, to_z[2])
+    x3, y3 = add("sum_3", [p0x, (y2b, 0)], [p1y, (x2b, 0)])
+    x3, y3 = send(x3, to_x), send(y3, to_y)
+    (z1,) = add("sum_z1", [p1, (x2b, 1), (y3, 0)])
+    z1 = send(z1, to_z[1])
+
+    def last(p_ref, y2b_ref, x3_ref, z1_ref, z2_ref, z3_ref, out_ref):
+        total = p_ref[...] + get_coded(y2b_ref, 1, width)
+        for ref in (x3_ref, z2_ref, z3_ref, z1_ref):
+            total = total + get_coded(ref, 0, width)
+        out_ref[...] = total.T
+
+    return call(last, sds((width, scen), F32), [VM] * 6, "gradient")(p0, y2b, x3, z1, z2, z3)
 
 
 def on_device(
@@ -62,7 +347,6 @@
     )
     adjoint = (base_adj + monitored_adj + outage_adj).astype(jnp.bfloat16)
     group_adjoint = lax.all_gather(adjoint, "bus", axis=0, tiled=True)
-    factor_cols = shift_factors
     return lax.psum_scatter(
         lax.dot_general(
             factor_cols, group_adjoint, (((0,), (0,)), ((), ())), preferred_element_type=jnp.float32
@@ -85,6 +369,5 @@
         P(("br", "bus")),
     )
     out_specs = P(("bus", "br"), None)
-    return jax.shard_map(
-        on_device, mesh=mesh, in_specs=in_specs, out_specs=out_specs, check_vma=False
-    )
+    local = on_slice if (mesh.shape["br"], mesh.shape["bus"]) == (16, 2) else on_device
+    return jax.shard_map(local, mesh=mesh, in_specs=in_specs, out_specs=out_specs, check_vma=False)

time: 399 us -> 150 us (0.38)
  waiting for transfers between devices: 300 us -> 57.9 us
  starting transfers between devices: 0.15 us -> 49.7 us
  blocking collectives: 45 us -> 0 us
  matrix products: 24.2 us -> 0 us
  Pallas kernels: 0 us -> 15.7 us
  local copies, waits for them, and re-layouts: 9.84 us -> 17.4 us
  other arithmetic: 6.13 us -> 0.11 us
  between operations: 13.3 us -> 7.75 us
    reduce_scatter x2 -> x0, waiting for transfers between devices: 118 us -> none  [the longest x1 115 us: on_device(): lax.psum_scatter(lax.dot_general(factor_cols, group_adjoint, (((0,), (0,)...]
    unnamed x5 -> x0, waiting for transfers between devices: 114 us -> none
    all_gather x1 -> x0, waiting for transfers between devices: 66.7 us -> none  [on_device(): lax.all_gather(injections, 'br', axis=0, tiled=True)]
    ppermute x0 -> x42, waiting for transfers between devices: none -> 57.9 us  [the longest x38 54.9 us: send(): return lax.ppermute(v, 'br', perm)]
    ppermute x0 -> x42, starting transfers between devices: none -> 49.7 us  [the longest x38 48.8 us: send(): return lax.ppermute(v, 'br', perm)]
    all_gather x2 -> x0, blocking collectives: 45 us -> none  [the longest x1 41.8 us: on_device(): all_outage = lax.all_gather(own_outage, ('br', 'bus'), axis=0, tiled=True)]
    dot_general x4 -> x0, matrix products: 24.2 us -> none  [the longest x1 11.2 us: on_device(): jnp.dot(factor_cols, lax.all_gather(injections, 'br', axis=0, tiled=True)...]
    pallas_call x0 -> x13, Pallas kernels: none -> 15.7 us  [the longest x4 7.06 us: forward(): call(body, sds((rows, scen), F32), [SM] + [VM] * (len(ops) - 1), name, [p...]
  transfers between devices with their start and end apart: 4 -> 42, of which waited for: 4 -> 21; matrix products, arithmetic and copies ran while one was open for 2% -> 1% of each run, Pallas kernels for 0% -> 5%
where the time goes in v1:
time: 150 us; the launch traced here: 149 us
  waiting for transfers between devices  57.9 us (39%)
  starting transfers between devices  49.7 us (33%)
  local copies, waits for them, and re-layouts  17.4 us (12%)
  Pallas kernels  15.7 us (10%)
  between operations  7.75 us (5%)
    ppermute x38, waiting for transfers between devices, send(): return lax.ppermute(v, 'br', perm)  54.9 us
    ppermute x38, starting transfers between devices, send(): return lax.ppermute(v, 'br', perm)  48.8 us
    unnamed x20, local copies, waits for them, and re-layouts  15.6 us
    pallas_call x4, Pallas kernels, forward(): call(body, sds((rows, scen), F32), [SM] + [VM] * (len(ops) - 1), name, [p...  7.06 us
    pallas_call x2, Pallas kernels, backward(): call(body, shapes, [SM, VM, VM, VM], name, [pltpu.VMEM((scen, rows), BF16...  4.59 us
    ppermute x4, waiting for transfers between devices, swap(): return lax.ppermute(v, 'bus', [(0, 1), (1, 0)])  3.01 us
  transfers between devices with their start and end apart: 42, of which 21 were waited for; matrix products, arithmetic and copies ran while one was open for 1% of the time, Pallas kernels for 5%

profile of v1, /device:TPU:0, one launch (start us, length us, event | category | flops | bytes accessed | tf_op | source)
XLA Modules:
  0.0 148.5 jit_solution(8895245975806751312)
XLA Ops:
  0.0 3.0 %collective-permute-start = (bf16[640,128]{1,0:T(8,128)(2,1)}, bf16[640,128]{1,0:T(8,128)(2,1)S(1)}, u32[]{:S(2)}, u32[]{:S(2)}) collective-permute-start(bf16[640,128]{1,0:T(8,128)(2,1)} %refs_0_.1), channel_id=1, source_target_pairs={{0,8},{2,10},{4,12},{6,14},{8,0},{10,2},{12,4},{14,6},{16,24},{18,... | collective-permute-start | bytes 491528 | tf_op jit(solution)/shard_map/ppermute | solution.py:134
  5.3 2.2 %collective-permute-done.refs_0_ = bf16[640,128]{1,0:T(8,128)(2,1)S(1)} collective-permute-done((bf16[640,128]{1,0:T(8,128)(2,1)}, bf16[640,128]{1,0:T(8,128)(2,1)S(1)}, u32[]{:S(2)}, u32[]{:S(2)}) %collective-permute-start) | collective-permute-done | bytes 163872 | tf_op jit(solution)/shard_map/ppermute | solution.py:134
  14.7 2.6 %collective-permute-done.7 = bf16[640,128]{1,0:T(8,128)(2,1)S(1)} collective-permute-done((bf16[640,128]{1,0:T(8,128)(2,1)S(1)}, bf16[640,128]{1,0:T(8,128)(2,1)S(1)}, u32[]{:S(2)}, u32[]{:S(2)}) %collective-permute-start.7) | collective-permute-done | bytes 163872 | tf_op jit(solution)/shard_map/ppermute | solution.py:134
  18.6 5.9 %collective-permute-done.2 = bf16[640,128]{1,0:T(8,128)(2,1)S(1)} collective-permute-done((bf16[640,128]{1,0:T(8,128)(2,1)S(1)}, bf16[640,128]{1,0:T(8,128)(2,1)S(1)}, u32[]{:S(2)}, u32[]{:S(2)}) %collective-permute-start.2) | collective-permute-done | bytes 163872 | tf_op jit(solution)/shard_map/ppermute | solution.py:134
  28.6 2.4 %collective-permute-done.9.refs_2_ = bf16[640,128]{1,0:T(8,128)(2,1)S(1)} collective-permute-done((bf16[640,128]{1,0:T(8,128)(2,1)S(1)}, bf16[640,128]{1,0:T(8,128)(2,1)S(1)}, u32[]{:S(2)}, u32[]{:S(2)}) %collective-permute-start.9) | collective-permute-done | bytes 163872 | tf_op jit(solution)/shard_map/ppermute | solution.py:134
  34.7 5.5 %copy-done = bf16[768,10240]{1,0:T(8,128)(2,1)S(1)} copy-done((bf16[768,10240]{1,0:T(8,128)(2,1)S(1)}, bf16[768,10240]{1,0:T(8,128)(2,1)}, u32[]{:S(2)}) %copy-start) | copy-done | bytes 15728664
  42.9 3.7 %copy-done.1 = bf16[768,10240]{1,0:T(8,128)(2,1)S(1)} copy-done((bf16[768,10240]{1,0:T(8,128)(2,1)S(1)}, bf16[768,10240]{1,0:T(8,128)(2,1)}, u32[]{:S(2)}) %copy-start.1) | copy-done | bytes 15728664
  50.2 1.8 %forward_fourth.1 = f32[768,128]{1,0:T(8,128)S(1)} custom-call(s32[5]{0:T(128)S(1)} %stack.125.scal_ref, bf16[768,10240]{1,0:T(8,128)(2,1)S(1)} %copy-done.1, bf16[640,128]{1,0:T(8,128)(2,1)S(1)} %broadcast_select_fusion.1.refs_0_, bf16[640,128]{1,0:T(8,128)(2,1)S(1)} %collective-permute-done.3.refs_1_, bf16[640,128]{1,0:T(8,128)(2,1)S(1)} %collective-permute-done.4.refs_2_, ...), custom_call_target="tpu_custom_call" | custom-call | flops 503316480 | bytes 4587520 | tf_op jit(solution)/shard_map/forward_fourth/pallas_call | solution.py:58
  62.3 3.0 %collective-permute-done.19 = f32[8,128]{1,0:T(8,128)S(1)} collective-permute-done((f32[8,128]{1,0:T(8,128)S(1)}, f32[8,128]{1,0:T(8,128)S(1)}, u32[]{:S(2)}, u32[]{:S(2)}) %collective-permute-start.19) | collective-permute-done | bytes 4128 | tf_op jit(solution)/shard_map/ppermute | solution.py:134
  66.9 2.1 %collective-permute-done.20 = f32[16,128]{1,0:T(8,128)S(1)} collective-permute-done((f32[16,128]{1,0:T(8,128)S(1)}, f32[16,128]{1,0:T(8,128)S(1)}, u32[]{:S(2)}, u32[]{:S(2)}) %collective-permute-start.20) | collective-permute-done | bytes 8224 | tf_op jit(solution)/shard_map/ppermute | solution.py:134
  69.1 2.7 %collective-permute-start.22 = (f32[32,128]{1,0:T(8,128)S(1)}, f32[32,128]{1,0:T(8,128)S(1)}, u32[]{:S(2)}, u32[]{:S(2)}) collective-permute-start(f32[32,128]{1,0:T(8,128)S(1)} %concatenate.22), channel_id=1, source_target_pairs={{0,16},{2,18},{4,20},{6,22},{8,24},{10,26},{12,28},{14,30},{16,0},... | collective-permute-start | bytes 49160 | tf_op jit(solution)/shard_map/ppermute | solution.py:134
  74.1 3.3 %collective-permute-done.23 = f32[32,128]{1,0:T(8,128)S(1)} collective-permute-done((f32[32,128]{1,0:T(8,128)S(1)}, f32[32,128]{1,0:T(8,128)S(1)}, u32[]{:S(2)}, u32[]{:S(2)}) %collective-permute-start.23) | collective-permute-done | bytes 16416 | tf_op jit(solution)/shard_map/ppermute | solution.py:134
  80.2 2.7 %collective-permute-start.24 = (f32[32,128]{1,0:T(8,128)S(1)}, f32[32,128]{1,0:T(8,128)S(1)}, u32[]{:S(2)}, u32[]{:S(2)}) collective-permute-start(f32[32,128]{1,0:T(8,128)S(1)} %get-tuple-element.49), channel_id=1, source_target_pairs={{0,8},{2,10},{4,12},{6,14},{8,0},{10,2},{12,4},{14,6},{16,24},{18,... | collective-permute-start | bytes 49160 | tf_op jit(solution)/shard_map/ppermute | solution.py:134
  86.4 2.1 %collective-permute-done.27 = f32[16,128]{1,0:T(8,128)S(1)} collective-permute-done((f32[16,128]{1,0:T(8,128)S(1)}, f32[16,128]{1,0:T(8,128)S(1)}, u32[]{:S(2)}, u32[]{:S(2)}) %collective-permute-start.27) | collective-permute-done | bytes 8224 | tf_op jit(solution)/shard_map/ppermute | solution.py:134
  89.2 3.0 %collective-permute-done.28 = f32[8,128]{1,0:T(8,128)S(1)} collective-permute-done((f32[8,128]{1,0:T(8,128)S(1)}, f32[8,128]{1,0:T(8,128)S(1)}, u32[]{:S(2)}, u32[]{:S(2)}) %collective-permute-start.28) | collective-permute-done | bytes 4128 | tf_op jit(solution)/shard_map/ppermute | solution.py:134
  95.4 5.5 %copy-done.2 = bf16[768,10240]{1,0:T(8,128)(2,1)S(1)} copy-done((bf16[768,10240]{1,0:T(8,128)(2,1)S(1)}, bf16[768,10240]{1,0:T(8,128)(2,1)}, u32[]{:S(2)}) %copy-start.2) | copy-done | bytes 15728664
  100.9 2.9 %backward_rest.1 = (s16[128,1408]{1,0:T(8,128)(2,1)S(1)}, s16[128,1408]{1,0:T(8,128)(2,1)S(1)}, f32[128,640]{1,0:T(8,128)S(1)}, f32[128,640]{1,0:T(8,128)S(1)}, ...) custom-call(s32[17]{0:T(128)S(1)} %stack.119.scal_ref, ...), custom_call_target="tpu_custom_call" | custom-call | flops 1509949440 | bytes 11796480 | tf_op jit(solution)/shard_map/backward_rest/pallas_call | solution.py:235
  109.7 5.5 %collective-permute-done.31.refs_1_.y2b_ref = s16[128,1408]{1,0:T(8,128)(2,1)S(1)} collective-permute-done((s16[128,1408]{1,0:T(8,128)(2,1)S(1)}, s16[128,1408]{1,0:T(8,128)(2,1)S(1)}, u32[]{:S(2)}, u32[]{:S(2)}) %collective-permute-start.31) | collective-permute-done | bytes 360480 | tf_op jit(solution)/shard_map/ppermute | solution.py:134
  117.6 5.3 %collective-permute-done.36.refs_1_ = s16[128,1408]{1,0:T(8,128)(2,1)S(1)} collective-permute-done((s16[128,1408]{1,0:T(8,128)(2,1)S(1)}, s16[128,1408]{1,0:T(8,128)(2,1)S(1)}, u32[]{:S(2)}, u32[]{:S(2)}) %collective-permute-start.36) | collective-permute-done | bytes 360480 | tf_op jit(solution)/shard_map/ppermute | solution.py:134
  127.4 1.9 %collective-permute-start.35 = (s16[128,768]{1,0:T(8,128)(2,1)S(1)}, s16[128,768]{1,0:T(8,128)(2,1)S(1)}, u32[]{:S(2)}, u32[]{:S(2)}) collective-permute-start(s16[128,768]{1,0:T(8,128)(2,1)S(1)} %sum_z1.1), channel_id=1, source_target_pairs={{0,8},{2,10},{4,12},{6,14},{8,0},{10,2},{12,4},{14,6},{16,24},{18,... | collective-permute-start | bytes 589832 | tf_op jit(solution)/shard_map/ppermute | solution.py:134
  129.3 2.3 %collective-permute-done.38.refs_2_ = s16[128,768]{1,0:T(8,128)(2,1)S(1)} collective-permute-done((s16[128,768]{1,0:T(8,128)(2,1)S(1)}, s16[128,768]{1,0:T(8,128)(2,1)S(1)}, u32[]{:S(2)}, u32[]{:S(2)}) %collective-permute-start.38) | collective-permute-done | bytes 196640 | tf_op jit(solution)/shard_map/ppermute | solution.py:134
  132.0 2.1 %collective-permute-start.40 = (s16[128,768]{1,0:T(8,128)(2,1)S(1)}, s16[128,768]{1,0:T(8,128)(2,1)S(1)}, u32[]{:S(2)}, u32[]{:S(2)}) collective-permute-start(s16[128,768]{1,0:T(8,128)(2,1)S(1)} %get-tuple-element.43), channel_id=1, source_target_pairs={{0,16},{2,18},{4,20},{6,22},{8,24},{10,26},{12,28},{14,30},{16,0},... | collective-permute-start | bytes 589832 | tf_op jit(solution)/shard_map/ppermute | solution.py:134
  134.0 2.2 %collective-permute-start.41 = (s16[128,768]{1,0:T(8,128)(2,1)S(1)}, s16[128,768]{1,0:T(8,128)(2,1)S(1)}, u32[]{:S(2)}, u32[]{:S(2)}) collective-permute-start(s16[128,768]{1,0:T(8,128)(2,1)S(1)} %get-tuple-element.44), channel_id=1, source_target_pairs={{0,24},{2,26},{4,28},{6,30},{8,16},{10,18},{12,20},{14,22},{16,8},... | collective-permute-start | bytes 589832 | tf_op jit(solution)/shard_map/ppermute | solution.py:134
  136.2 11.2 %collective-permute-done.40.z2_ref = s16[128,768]{1,0:T(8,128)(2,1)S(1)} collective-permute-done((s16[128,768]{1,0:T(8,128)(2,1)S(1)}, s16[128,768]{1,0:T(8,128)(2,1)S(1)}, u32[]{:S(2)}, u32[]{:S(2)}) %collective-permute-start.40) | collective-permute-done | bytes 196640 | tf_op jit(solution)/shard_map/ppermute | solution.py:134
  (124 shorter events, 56.1 us)
Async XLA Ops:
  3.7 7.8 %collective-permute-start.15 = (bf16[640,128]{1,0:T(8,128)(2,1)}, bf16[640,128]{1,0:T(8,128)(2,1)S(1)}, u32[]{:S(2)}, u32[]{:S(2)}) collective-permute-start(bf16[640,128]{1,0:T(8,128)(2,1)} %refs_0_.1), channel_id=1, source_target_pairs={{0,4},{2,6},{4,0},{6,2},{8,12},{10,14},{12,8},{14,10},{16,20},{18,... | collective-permute-start | bytes 491528 | tf_op jit(solution)/shard_map/ppermute | solution.py:134
  8.1 9.1 %collective-permute-start.7 = (bf16[640,128]{1,0:T(8,128)(2,1)S(1)}, bf16[640,128]{1,0:T(8,128)(2,1)S(1)}, u32[]{:S(2)}, u32[]{:S(2)}) collective-permute-start(bf16[640,128]{1,0:T(8,128)(2,1)S(1)} %collective-permute-done.6), channel_id=1, source_target_pairs={{8,0},{10,2},{12,4},{14,6},{16,24},{18,26},{20,28},{22,30},{9,1},{... | collective-permute-start | bytes 491528 | tf_op jit(solution)/shard_map/ppermute | solution.py:134
  9.4 16.6 %collective-permute-start.14 = (bf16[640,128]{1,0:T(8,128)(2,1)}, bf16[640,128]{1,0:T(8,128)(2,1)S(1)}, u32[]{:S(2)}, u32[]{:S(2)}) collective-permute-start(bf16[640,128]{1,0:T(8,128)(2,1)} %refs_0_.1), channel_id=1, source_target_pairs={{0,2},{2,0},{4,6},{6,4},{8,10},{10,8},{12,14},{14,12},{16,18},{18,... | collective-permute-start | bytes 491528 | tf_op jit(solution)/shard_map/ppermute | solution.py:134
  11.1 16.4 %collective-permute-start.11 = (bf16[640,128]{1,0:T(8,128)(2,1)S(1)}, bf16[640,128]{1,0:T(8,128)(2,1)S(1)}, u32[]{:S(2)}, u32[]{:S(2)}) collective-permute-start(bf16[640,128]{1,0:T(8,128)(2,1)S(1)} %collective-permute-done.refs_0_), channel_id=1, source_target_pairs={{0,2},{2,0},{4,6},{6,4},{8,10},{10,8},{12,14},{14,12},{16,18},{18,... | collective-permute-start | bytes 491528 | tf_op jit(solution)/shard_map/ppermute | solution.py:134
  11.5 16.6 %collective-permute-start.12 = (bf16[640,128]{1,0:T(8,128)(2,1)S(1)}, bf16[640,128]{1,0:T(8,128)(2,1)S(1)}, u32[]{:S(2)}, u32[]{:S(2)}) collective-permute-start(bf16[640,128]{1,0:T(8,128)(2,1)S(1)} %collective-permute-done.refs_0_), channel_id=1, source_target_pairs={{0,4},{2,6},{4,0},{6,2},{8,12},{10,14},{12,8},{14,10},{16,20},{18,... | collective-permute-start | bytes 491528 | tf_op jit(solution)/shard_map/ppermute | solution.py:134
  13.2 19.1 %collective-permute-start.16 = (bf16[640,128]{1,0:T(8,128)(2,1)S(1)}, bf16[640,128]{1,0:T(8,128)(2,1)S(1)}, u32[]{:S(2)}, u32[]{:S(2)}) collective-permute-start(bf16[640,128]{1,0:T(8,128)(2,1)S(1)} %collective-permute-done.15.refs_2_), channel_id=1, source_target_pairs={{0,2},{2,0},{4,6},{6,4},{8,10},{10,8},{12,14},{14,12},{16,18},{18,... | collective-permute-start | bytes 491528 | tf_op jit(solution)/shard_map/ppermute | solution.py:134
  26.0 7.9 %collective-permute-start.3 = (bf16[640,128]{1,0:T(8,128)(2,1)S(1)}, bf16[640,128]{1,0:T(8,128)(2,1)S(1)}, u32[]{:S(2)}, u32[]{:S(2)}) collective-permute-start(bf16[640,128]{1,0:T(8,128)(2,1)S(1)} %broadcast_select_fusion.1.refs_0_), channel_id=1, source_target_pairs={{0,2},{2,0},{4,6},{6,4},{8,10},{10,8},{12,14},{14,12},{16,18},{18,... | collective-permute-start | bytes 491528 | tf_op jit(solution)/shard_map/ppermute | solution.py:134
  27.6 15.3 %collective-permute-start.13 = (bf16[640,128]{1,0:T(8,128)(2,1)S(1)}, bf16[640,128]{1,0:T(8,128)(2,1)S(1)}, u32[]{:S(2)}, u32[]{:S(2)}) collective-permute-start(bf16[640,128]{1,0:T(8,128)(2,1)S(1)} %collective-permute-done.11.refs_1_), channel_id=1, source_target_pairs={{0,4},{2,6},{4,0},{6,2},{8,12},{10,14},{12,8},{14,10},{16,20},{18,... | collective-permute-start | bytes 491528 | tf_op jit(solution)/shard_map/ppermute | solution.py:134
  28.1 20.4 %collective-permute-start.8 = (bf16[640,128]{1,0:T(8,128)(2,1)S(1)}, bf16[640,128]{1,0:T(8,128)(2,1)S(1)}, u32[]{:S(2)}, u32[]{:S(2)}) collective-permute-start(bf16[640,128]{1,0:T(8,128)(2,1)S(1)} %broadcast_select_fusion.refs_0_), channel_id=1, source_target_pairs={{0,2},{2,0},{4,6},{6,4},{8,10},{10,8},{12,14},{14,12},{16,18},{18,... | collective-permute-start | bytes 491528 | tf_op jit(solution)/shard_map/ppermute | solution.py:134
  31.0 17.5 %collective-permute-start.10 = (bf16[640,128]{1,0:T(8,128)(2,1)S(1)}, bf16[640,128]{1,0:T(8,128)(2,1)S(1)}, u32[]{:S(2)}, u32[]{:S(2)}) collective-permute-start(bf16[640,128]{1,0:T(8,128)(2,1)S(1)} %collective-permute-done.9.refs_2_), channel_id=1, source_target_pairs={{0,2},{2,0},{4,6},{6,4},{8,10},{10,8},{12,14},{14,12},{16,18},{18,... | collective-permute-start | bytes 491528 | tf_op jit(solution)/shard_map/ppermute | solution.py:134
  32.3 17.9 %collective-permute-start.4 = (bf16[640,128]{1,0:T(8,128)(2,1)S(1)}, bf16[640,128]{1,0:T(8,128)(2,1)S(1)}, u32[]{:S(2)}, u32[]{:S(2)}) collective-permute-start(bf16[640,128]{1,0:T(8,128)(2,1)S(1)} %broadcast_select_fusion.1.refs_0_), channel_id=1, source_target_pairs={{0,4},{2,6},{4,0},{6,2},{8,12},{10,14},{12,8},{14,10},{16,20},{18,... | collective-permute-start | bytes 491528 | tf_op jit(solution)/shard_map/ppermute | solution.py:134
  33.9 16.4 %collective-permute-start.5 = (bf16[640,128]{1,0:T(8,128)(2,1)S(1)}, bf16[640,128]{1,0:T(8,128)(2,1)S(1)}, u32[]{:S(2)}, u32[]{:S(2)}) collective-permute-start(bf16[640,128]{1,0:T(8,128)(2,1)S(1)} %collective-permute-done.3.refs_1_), channel_id=1, source_target_pairs={{0,4},{2,6},{4,0},{6,2},{8,12},{10,14},{12,8},{14,10},{16,20},{18,... | collective-permute-start | bytes 491528 | tf_op jit(solution)/shard_map/ppermute | solution.py:134
  52.0 8.1 %collective-permute-start.17 = (f32[384,128]{1,0:T(8,128)S(1)}, f32[384,128]{1,0:T(8,128)S(1)}, u32[]{:S(2)}, u32[]{:S(2)}) collective-permute-start(f32[384,128]{1,0:T(8,128)S(1)} %constant_dynamic-slice_fusion.4), channel_id=1, source_target_pairs={{0,1},{1,0},{2,3},{3,2},{4,5},{5,4},{6,7},{7,6},{8,9},{9,8},{10,11... | collective-permute-start | bytes 589832 | tf_op jit(solution)/shard_map/ppermute | solution.py:137
  103.8 11.3 %collective-permute-start.31 = (s16[128,1408]{1,0:T(8,128)(2,1)S(1)}, s16[128,1408]{1,0:T(8,128)(2,1)S(1)}, u32[]{:S(2)}, u32[]{:S(2)}) collective-permute-start(s16[128,1408]{1,0:T(8,128)(2,1)S(1)} %get-tuple-element.28), channel_id=1, source_target_pairs={{0,4},{2,6},{4,0},{6,2},{8,12},{10,14},{12,8},{14,10},{16,20},{18,... | collective-permute-start | bytes 1081352 | tf_op jit(solution)/shard_map/ppermute | solution.py:134
  105.4 11.3 %collective-permute-start.32 = (s16[128,1408]{1,0:T(8,128)(2,1)S(1)}, s16[128,1408]{1,0:T(8,128)(2,1)S(1)}, u32[]{:S(2)}, u32[]{:S(2)}) collective-permute-start(s16[128,1408]{1,0:T(8,128)(2,1)S(1)} %get-tuple-element.31), channel_id=1, source_target_pairs={{0,2},{2,0},{4,6},{6,4},{8,10},{10,8},{12,14},{14,12},{16,18},{18,... | collective-permute-start | bytes 1081352 | tf_op jit(solution)/shard_map/ppermute | solution.py:134
  107.4 15.5 %collective-permute-start.36 = (s16[128,1408]{1,0:T(8,128)(2,1)S(1)}, s16[128,1408]{1,0:T(8,128)(2,1)S(1)}, u32[]{:S(2)}, u32[]{:S(2)}) collective-permute-start(s16[128,1408]{1,0:T(8,128)(2,1)S(1)} %get-tuple-element.36), channel_id=1, source_target_pairs={{0,4},{2,6},{4,0},{6,2},{8,12},{10,14},{12,8},{14,10},{16,20},{18,... | collective-permute-start | bytes 1081352 | tf_op jit(solution)/shard_map/ppermute | solution.py:134
  108.3 15.0 %collective-permute-start.37 = (s16[128,1408]{1,0:T(8,128)(2,1)S(1)}, s16[128,1408]{1,0:T(8,128)(2,1)S(1)}, u32[]{:S(2)}, u32[]{:S(2)}) collective-permute-start(s16[128,1408]{1,0:T(8,128)(2,1)S(1)} %get-tuple-element.39), channel_id=1, source_target_pairs={{0,2},{2,0},{4,6},{6,4},{8,10},{10,8},{12,14},{14,12},{16,18},{18,... | collective-permute-start | bytes 1081352 | tf_op jit(solution)/shard_map/ppermute | solution.py:134
  117.0 10.1 %collective-permute-start.34 = (s16[128,768]{1,0:T(8,128)(2,1)S(1)}, s16[128,768]{1,0:T(8,128)(2,1)S(1)}, u32[]{:S(2)}, u32[]{:S(2)}) collective-permute-start(s16[128,768]{1,0:T(8,128)(2,1)S(1)} %get-tuple-element.34), channel_id=1, source_target_pairs={{0,4},{2,6},{4,0},{6,2},{8,12},{10,14},{12,8},{14,10},{16,20},{18,... | collective-permute-start | bytes 589832 | tf_op jit(solution)/shard_map/ppermute | solution.py:134
  123.7 7.9 %collective-permute-start.38 = (s16[128,768]{1,0:T(8,128)(2,1)S(1)}, s16[128,768]{1,0:T(8,128)(2,1)S(1)}, u32[]{:S(2)}, u32[]{:S(2)}) collective-permute-start(s16[128,768]{1,0:T(8,128)(2,1)S(1)} %get-tuple-element.40), channel_id=1, source_target_pairs={{0,2},{2,0},{4,6},{6,4},{8,10},{10,8},{12,14},{14,12},{16,18},{18,... | collective-permute-start | bytes 589832 | tf_op jit(solution)/shard_map/ppermute | solution.py:134
  124.0 7.6 %collective-permute-start.39 = (s16[128,768]{1,0:T(8,128)(2,1)S(1)}, s16[128,768]{1,0:T(8,128)(2,1)S(1)}, u32[]{:S(2)}, u32[]{:S(2)}) collective-permute-start(s16[128,768]{1,0:T(8,128)(2,1)S(1)} %get-tuple-element.42), channel_id=1, source_target_pairs={{0,4},{2,6},{4,0},{6,2},{8,12},{10,14},{12,8},{14,10},{16,20},{18,... | collective-permute-start | bytes 589832 | tf_op jit(solution)/shard_map/ppermute | solution.py:134
  125.1 11.2 %collective-permute-start.33 = (s16[128,768]{1,0:T(8,128)(2,1)S(1)}, s16[128,768]{1,0:T(8,128)(2,1)S(1)}, u32[]{:S(2)}, u32[]{:S(2)}) collective-permute-start(s16[128,768]{1,0:T(8,128)(2,1)S(1)} %get-tuple-element.32), channel_id=1, source_target_pairs={{0,2},{2,0},{4,6},{6,4},{8,10},{10,8},{12,14},{14,12},{16,18},{18,... | collective-permute-start | bytes 589832 | tf_op jit(solution)/shard_map/ppermute | solution.py:134
  127.4 8.9 %collective-permute-start.35 = (s16[128,768]{1,0:T(8,128)(2,1)S(1)}, s16[128,768]{1,0:T(8,128)(2,1)S(1)}, u32[]{:S(2)}, u32[]{:S(2)}) collective-permute-start(s16[128,768]{1,0:T(8,128)(2,1)S(1)} %sum_z1.1), channel_id=1, source_target_pairs={{0,8},{2,10},{4,12},{6,14},{8,0},{10,2},{12,4},{14,6},{16,24},{18,... | collective-permute-start | bytes 589832 | tf_op jit(solution)/shard_map/ppermute | solution.py:134
  132.0 15.5 %collective-permute-start.40 = (s16[128,768]{1,0:T(8,128)(2,1)S(1)}, s16[128,768]{1,0:T(8,128)(2,1)S(1)}, u32[]{:S(2)}, u32[]{:S(2)}) collective-permute-start(s16[128,768]{1,0:T(8,128)(2,1)S(1)} %get-tuple-element.43), channel_id=1, source_target_pairs={{0,16},{2,18},{4,20},{6,22},{8,24},{10,26},{12,28},{14,30},{16,0},... | collective-permute-start | bytes 589832 | tf_op jit(solution)/shard_map/ppermute | solution.py:134
  134.0 13.4 %collective-permute-start.41 = (s16[128,768]{1,0:T(8,128)(2,1)S(1)}, s16[128,768]{1,0:T(8,128)(2,1)S(1)}, u32[]{:S(2)}, u32[]{:S(2)}) collective-permute-start(s16[128,768]{1,0:T(8,128)(2,1)S(1)} %get-tuple-element.44), channel_id=1, source_target_pairs={{0,24},{2,26},{4,28},{6,30},{8,16},{10,18},{12,20},{14,22},{16,8},... | collective-permute-start | bytes 589832 | tf_op jit(solution)/shard_map/ppermute | solution.py:134
  (28 other events, 221.7 us)

commit v2 on v0

--- a/solution.py
+++ b/solution.py
@@ -1,11 +1,472 @@
+import functools
+
 import jax
 import jax.numpy as jnp
 from jax import lax
+from jax.experimental import pallas as pl
+from jax.experimental.pallas import tpu as pltpu
 from jax.sharding import PartitionSpec as P
 
 base_weight = 1.0
 cont_weight = 0.25
 emergency = 1.25
+
+F32 = jnp.float32
+BF16 = jnp.bfloat16
+VM = pl.BlockSpec(memory_space=pltpu.VMEM)
+SM = pl.BlockSpec(memory_space=pltpu.SMEM)
+LEVELS = 32000.0
+LANES = 128
+
+
+def call(body, out_shape, in_specs, name, scratch=(), us=0.5, limit=24):
+    many = isinstance(out_shape, (tuple, list))
+    return pl.pallas_call(
+        body,
+        out_shape=out_shape,
+        in_specs=in_specs,
+        out_specs=[VM] * len(out_shape) if many else VM,
+        scratch_shapes=list(scratch),
+        compiler_params=pltpu.CompilerParams(vmem_limit_bytes=limit << 20),
+        cost_estimate=pl.CostEstimate(flops=int(us * 1.15e9), bytes_accessed=1, transcendentals=0),
+        name=name,
+    )
+
+
+def sds(shape, dtype):
+    return jax.ShapeDtypeStruct(shape, dtype)
+
+
+def scaled(blocks):
+    top = functools.reduce(
+        jnp.maximum, [jnp.max(jnp.abs(b), axis=1, keepdims=True) for b in blocks]
+    )
+    power = jnp.ceil(jnp.log2(jnp.maximum(top, 1e-30)))
+    return power, jnp.exp2(-power) * LEVELS
+
+
+def whole(x):
+    return x.astype(jnp.int32).astype(jnp.int16)
+
+
+def put_coded(ref, blocks, fine=None):
+    width = blocks[0].shape[1]
+    power, scale = scaled(blocks)
+    for n, b in enumerate(blocks):
+        ref[:, n * width : (n + 1) * width] = whole(jnp.round(b * scale))
+    power = jnp.broadcast_to(power, (ref.shape[0], LANES))
+    if fine is not None:
+        end = len(blocks) * width
+        fine_power, scale = scaled([fine])
+        scaled_fine = fine * scale
+        high = jnp.round(scaled_fine)
+        ref[:, end : end + LANES] = whole(high)
+        ref[:, end + LANES : end + 2 * LANES] = whole(jnp.round((scaled_fine - high) * (2 * LEVELS)))
+        lane = lax.broadcasted_iota(jnp.int32, power.shape, 1)
+        power = jnp.where(lane < LANES // 2, power, fine_power)
+    ref[:, ref.shape[1] - LANES :] = whole(power)
+
+
+def number(x):
+    return x.astype(jnp.int32).astype(F32)
+
+
+def get_coded(ref, n, width):
+    power = number(ref[:, ref.shape[1] - LANES :])[:, :1]
+    return number(ref[:, n * width : (n + 1) * width]) * (jnp.exp2(power) * (1.0 / LEVELS))
+
+
+def get_fine(ref):
+    end = ref.shape[1] - 3 * LANES
+    power = number(ref[:, ref.shape[1] - LANES :])[:, LANES // 2 : LANES // 2 + 1]
+    value = number(ref[:, end : end + LANES]) + number(ref[:, end + LANES : end + 2 * LANES]) * (0.5 / LEVELS)
+    return value * (jnp.exp2(power) * (1.0 / LEVELS))
+
+
+def three(x):
+    high = x.astype(BF16)
+    rest = x - high.astype(F32)
+    middle = rest.astype(BF16)
+    low = (rest - middle.astype(F32)).astype(BF16)
+    return jnp.concatenate([high, middle, low], axis=1)
+
+
+def pick(hot, x):
+    n = x.shape[1]
+    y = jnp.dot(hot, three(x), preferred_element_type=F32)
+    return y[:, :n] + y[:, n : 2 * n] + y[:, 2 * n :]
+
+
+def one_hot(hit):
+    return jnp.where(hit, 1.0, 0.0).astype(BF16)
+
+
+def overload(x, cap):
+    return jnp.maximum(x - cap, 0.0) + jnp.minimum(x + cap, 0.0)
+
+
+HB = pl.BlockSpec(memory_space=pl.ANY)
+DMA = pltpu.SemaphoreType.DMA
+
+
+def tie(value, *others):
+    return lax.optimization_barrier((value, *others))[0]
+
+
+def columns(f_ref, buf, sem, scal_ref, firsts, width):
+    copies = []
+    for g, place in enumerate(firsts):
+        start = pl.multiple_of(scal_ref[place] * width, width)
+        copies.append(pltpu.make_async_copy(f_ref.at[:, pl.ds(start, width)], buf.at[g], sem.at[g]))
+        copies[-1].start()
+    return copies
+
+
+def forward(factors, shards, blocks, total, name, core=None, us=1.0):
+    rows = factors.shape[0]
+    width, scen = factors.shape[1] // (4 * 4), shards[0].shape[1]
+    n, half = len(blocks), rows // 2
+    keep = total is not None
+    spots = [(i, r) for i, v in enumerate(shards) for r in range(0, v.shape[0], width)]
+    scal = jnp.stack([*blocks, 0 if core is None else core]).astype(jnp.int32)
+
+    def body(scal_ref, f_ref, *refs):
+        ins, refs = refs[: len(shards)], refs[len(shards) :]
+        tot_ref, refs = (refs[0], refs[1:]) if keep else (None, refs)
+        outs, (buf, acc, sem) = refs[:-3], refs[-3:]
+        copies = columns(f_ref, buf, sem, scal_ref, range(n), width)
+        dst = outs[0] if core is None else acc
+        for g in range(n):
+            copies[g].wait()
+            i, r = spots[g]
+            part = jnp.dot(buf[g], ins[i][r : r + width, :], preferred_element_type=F32)
+            if g:
+                dst[...] += part
+            else:
+                dst[...] = part + tot_ref[...] if keep else part
+        if core is not None:
+            outs[0][...] = acc[pl.ds(pl.multiple_of(scal_ref[n] * half, half), half), :]
+            outs[1][...] = acc[pl.ds(pl.multiple_of((1 - scal_ref[n]) * half, half), half), :]
+
+    ops = [scal, factors, *shards] + ([total] if keep else [])
+    return call(
+        body,
+        sds((rows, scen), F32) if core is None else [sds((half, scen), F32)] * 2,
+        [SM, HB] + [VM] * (len(ops) - 2),
+        name,
+        [pltpu.VMEM((n, rows, width), BF16), pltpu.VMEM((rows if core is not None else 8, scen), F32), DMA((n,))],
+        us=us,
+    )(*ops)
+
+
+def on_slice(
+    shift_factors, injections, limits, entry_row, entry_owner, entry_slot, outage_factor, outage_row
+):
+    rows, cols = shift_factors.shape
+    width, scen = injections.shape
+    half = rows // 2
+    pairs = entry_row.shape[0]
+    owned = outage_row.shape[0]
+    group = 2 * owned
+    line_conts = 4 * group
+    conts = 4 * line_conts
+    plane = 4 * width
+    me = lax.axis_index("br")
+    core = lax.axis_index("bus")
+    zz, spot = me // 4, me % 4
+    first = 1 + core
+    second = 2 - core
+
+    chips = [(z, s) for z in range(4) for s in range(4)]
+    both = ("br", "bus")
+
+    def to(dz, ds):
+        return [(z * 4 + s, (z ^ dz) * 4 + (s ^ ds)) for z, s in chips]
+
+    def split(ds):
+        return [(2 * a + c, 2 * b + c) for c in range(2) for a, b in to(0, ds[c])]
+
+    def send(v, dz=0, ds=0):
+        return lax.ppermute(v, "br", to(dz, ds))
+
+    def swap(v):
+        return lax.ppermute(v, "bus", [(0, 1), (1, 0)])
+
+    def send_first(v):
+        return lax.ppermute(v, both, split((1, 2)))
+
+    def send_second(v):
+        return lax.ppermute(v, both, split((2, 1)))
+
+    factors = pltpu.with_memory_space_constraint(shift_factors, pltpu.HBM)
+
+    planes = {0: injections}
+    planes[1] = send(injections, 1)
+    shards = {}
+
+    def spread(k, *after):
+        a = send_first(planes[k])
+        shards[k] = [planes[k], a, send_second(tie(jnp.concatenate([planes[k], a], axis=0), *after))]
+
+    spread(0)
+
+    def block(k, line):
+        return (zz ^ k) * 4 + (spot ^ line)
+
+    lines = [0, first, second, 3]
+
+    other_row = swap(outage_row)
+    ext = plane + LANES
+
+    def take_rows(scal_ref, own_ref, other_ref, f_ref, *refs):
+        outs, (buf, picked, sem) = refs[:4], refs[4:]
+        mine = 1 - scal_ref[1]
+        numbers = [own_ref[t] * mine + other_ref[t] * (1 - mine) for t in range(owned)]
+        numbers += [own_ref[t] * (1 - mine) + other_ref[t] * mine + half for t in range(owned)]
+        copies = []
+        for c in range(group):
+            start = pl.multiple_of((numbers[c] // 16) * 16, 16)
+            copies.append(
+                pltpu.make_async_copy(f_ref.at[pl.ds(start, 16), :], buf.at[pl.ds(16 * c, 16), :], sem.at[c])
+            )
+            copies[-1].start()
+        lane = lax.broadcasted_iota(jnp.int32, (group, LANES), 1)
+        line = lax.broadcasted_iota(jnp.int32, (group, LANES), 0)
+        mark = jnp.zeros((group, LANES), F32)
+        hot = jnp.zeros((group, LANES), F32)
+        for c in range(group):
+            high, low = numbers[c] // 16, numbers[c] % 16
+            hot = hot + jnp.where((line == c) & (lane == 16 * c + low), 1.0, 0.0)
+            mark = mark + jnp.where((line == c) & (lane == 0), high.astype(F32), 0.0)
+            mark = mark + jnp.where((line == c) & (lane == 1), low.astype(F32), 0.0)
+        for copy in copies:
+            copy.wait()
+        picked[...] = jnp.dot(hot.astype(BF16), buf[...], preferred_element_type=F32)
+        for k in range(4):
+            start = pl.multiple_of((scal_ref[0] ^ k) * plane, plane)
+            outs[k][:, :plane] = picked[:, pl.ds(start, plane)].astype(BF16)
+            outs[k][:, plane:] = mark.astype(BF16)
+
+    taken = call(
+        take_rows, [sds((group, ext), BF16)] * 4, [SM, SM, SM, HB], "outage_rows",
+        [pltpu.VMEM((group * 16, cols), BF16), pltpu.VMEM((group, cols), F32), DMA((group,))], us=3,
+    )(jnp.stack([zz, core]).astype(jnp.int32), outage_row, other_row, factors)
+    planes[1] = tie(planes[1], taken[0])
+    taken = [taken[0]] + [send(taken[k], k) for k in (1, 2, 3)]
+    for k in (3, 2):
+        planes[k] = send(tie(injections, taken[0]), k)
+    spread(1)
+    spread(3)
+
+    part = forward(factors, shards[0], [block(0, line) for line in lines], None, "forward_own", us=3.5)
+    planes[2] = tie(planes[2], part)
+    spread(2)
+
+    scal = jnp.stack([zz, *[spot ^ line for line in lines]]).astype(jnp.int32)
+
+    def outage_part(scal_ref, *refs):
+        rows_in, (own, one, two), (so_ref, po_ref, stack, inj) = refs[:4], refs[4:7], refs[7:]
+        ins = [own[...], one[...], two[:width, :], two[width:, :]]
+        for k in range(4):
+            stack[pl.ds(pl.multiple_of((scal_ref[0] ^ k) * group, group), group), :] = rows_in[k][...].astype(F32)
+            inj[pl.ds(pl.multiple_of(scal_ref[1 + k] * width, width), width), :] = ins[k]
+        so = stack[...].astype(BF16)
+        so_ref[...] = so
+        po_ref[...] = jnp.dot(so[:, :plane], inj[...], preferred_element_type=F32)
+
+    out_factors, outage = call(
+        outage_part, [sds((line_conts, ext), BF16), sds((line_conts, scen), F32)], [SM] + [VM] * 7, "outage_flows",
+        [pltpu.VMEM((line_conts, ext), F32), pltpu.VMEM((plane, scen), BF16)],
+    )(tie(scal, part), *taken, *shards[0])
+    outage = outage + send(outage, 1)
+    outage = outage + send(outage, 2)
+    part = forward(factors, shards[1], [block(1, line) for line in lines], part, "forward_pair", us=3.5)
+    outage = tie(outage, part)
+    outage = outage + swap(outage)
+    outage = jnp.concatenate([outage, send(outage, 0, 1)], axis=0)
+    part = forward(factors, shards[2][:2], [block(2, line) for line in lines[:2]], part, "forward_2a", us=2.9)
+    outage = tie(outage, part)
+    outage = jnp.concatenate([outage, send(outage, 0, 2)], axis=0)
+    owner = entry_owner[:, 0]
+    contingency = jnp.bitwise_xor(owner % 4, spot) * line_conts + (owner // 4) * group + entry_slot
+
+    part = forward(factors, shards[3], [block(3, line) for line in lines], part, "forward_3", us=4)
+    mine, theirs = forward(factors, shards[2][2:], [block(2, line) for line in lines[2:]], part, "forward_2b", core, us=2.9)
+    theirs = swap(theirs)
+
+    scal = jnp.concatenate([jnp.stack([zz * group + core * owned]), outage_row]).astype(jnp.int32)
+
+    def middle(scal_ref, mine_ref, theirs_ref, out_ref, lim_ref, er_ref, ert_ref, ct_ref, ctt_ref, f_ref, limr_ref,
+               adj_ref, every_t_ref, every_ref, total):
+        flows = mine_ref[...] + theirs_ref[...]
+        hit = er_ref[...] == lax.broadcasted_iota(jnp.int32, (pairs, half), 1)
+        cap = emergency * jnp.sum(jnp.where(hit, limr_ref[...], 0.0), axis=1, keepdims=True)
+        cont = one_hot(ct_ref[...] == lax.broadcasted_iota(jnp.int32, (pairs, conts), 1))
+        factor = f_ref[...]
+        post = pick(one_hot(hit), flows) + factor * pick(cont, out_ref[...])
+        adj = cont_weight * overload(post, cap)
+        hot_t = one_hot(ert_ref[...] == lax.broadcasted_iota(jnp.int32, (half, pairs), 0))
+        cont_t = one_hot(ctt_ref[...] == lax.broadcasted_iota(jnp.int32, (conts, pairs), 0))
+        every_ref[...] = pick(cont_t, factor * adj)
+        summed = base_weight * overload(flows, lim_ref[...]) + pick(hot_t, adj)
+        total[...] = summed
+        place = lax.broadcasted_iota(jnp.int32, (half, scen), 0)
+        out = place < 0
+        for t in range(owned):
+            r = scal_ref[1 + t]
+            fresh = 1.0
+            for u in range(t):
+                fresh = fresh * jnp.where(scal_ref[1 + u] == r, 0.0, 1.0)
+            own = pl.ds(scal_ref[0] + t, 1)
+            every_ref[own, :] = every_ref[own, :] + fresh * total[pl.ds(r, 1), :]
+            out = out | (place == r)
+        adj_ref[...] = jnp.where(out, 0.0, summed).T.astype(BF16)
+        every_t_ref[...] = every_ref[...].T
+
+    adj_t, every = call(
+        middle, [sds((scen, half), BF16), sds((scen, conts), F32)], [SM] + [VM] * 10, "penalty",
+        [pltpu.VMEM((conts, scen), F32), pltpu.VMEM((half, scen), F32)],
+    )(
+        scal, mine, theirs, outage, limits[:, None], entry_row[:, None], entry_row[None, :],
+        contingency[:, None], contingency[None, :], outage_factor[:, None], limits[None, :],
+    )
+    other_t = swap(adj_t)
+
+    def message(n, fine=False):
+        return sds((scen, n * width + (3 if fine else 1) * LANES), jnp.int16)
+
+    grad_block = sds((scen, width), F32)
+
+    def backward(name, adj, messages, plain, us=3.0, fine=None):
+        wanted = [b for m in messages for b in m] + plain
+        n = len(wanted)
+        scal = jnp.stack([core, *[block(k, line) for k, line in wanted]]).astype(jnp.int32)
+
+        def body(scal_ref, f_ref, a_ref, b_ref, *refs):
+            outs, (buf, adj, sem) = refs[:-3], refs[-3:]
+            more, outs = (outs[0][...], outs[1:]) if fine is not None else (None, outs)
+            copies = columns(f_ref, buf, sem, scal_ref, range(1, n + 1), width)
+            adj[:, pl.ds(pl.multiple_of(scal_ref[0] * half, half), half)] = a_ref[...]
+            adj[:, pl.ds(pl.multiple_of((1 - scal_ref[0]) * half, half), half)] = b_ref[...]
+
+            def grad(g):
+                copies[g].wait()
+                return jnp.dot(adj[...], buf[g], preferred_element_type=F32)
+
+            g = 0
+            for ref, m in zip(outs, messages):
+                put_coded(ref, [grad(g + i) for i in range(len(m))], more)
+                g += len(m)
+            for ref in outs[len(messages) :]:
+                ref[...] = grad(g)
+                g += 1
+
+        return call(
+            body, [message(len(m), fine is not None) for m in messages] + [grad_block] * len(plain),
+            [SM, HB] + [VM] * (2 if fine is None else 3), name,
+            [pltpu.VMEM((n, rows, width), BF16), pltpu.VMEM((scen, rows), BF16), DMA((n,))],
+            us=us,
+        )(scal, factors, *adj, *([] if fine is None else [fine]))
+
+    def add(name, *terms):
+        flat = [t[0] if isinstance(t, tuple) else t for t in terms]
+
+        def body(*refs):
+            total = None
+            for t, ref in zip(terms, refs):
+                v = get_coded(ref, t[1], width) if isinstance(t, tuple) else ref[...]
+                total = v if total is None else total + v
+            put_coded(refs[-1], [total])
+
+        return call(body, message(1), [VM] * len(flat), name, us=0.01)(*flat)
+
+    def shifted(v, core_ref, on_0, on_1):
+        return jnp.where(
+            jnp.full(v.shape, core_ref[0]) == 0,
+            pltpu.roll(v, LANES - on_0 * line_conts, 1),
+            pltpu.roll(v, LANES - on_1 * line_conts, 1),
+        )
+
+    def sum_3(core_ref, p_ref, a_ref, e_ref, b_ref, t_ref):
+        t_ref[...] = e_ref[...] + shifted(get_fine(a_ref), core_ref, 1, 2)
+        put_coded(b_ref, [p_ref[...] + get_coded(a_ref, 0, width)], t_ref[...])
+
+    def sum_z3(core_ref, p_ref, a_ref, b_ref, t_ref, z_ref, e_ref):
+        e_ref[...] = (t_ref[...] + shifted(get_fine(b_ref), core_ref, 2, 1)).T[:line_conts, :]
+        put_coded(z_ref, [p_ref[...] + get_coded(a_ref, 1, width) + get_coded(b_ref, 0, width)])
+
+    core_1 = core[None].astype(jnp.int32)
+    adj = (adj_t, other_t)
+    (a3,) = backward("backward_3a", adj, [[(3, 3), (3, first)]], [], us=2.6, fine=every)
+    a3_got = send_first(a3)
+    adj = (tie(adj_t, a3), other_t)
+    a2, p3s, p3 = backward("backward_3b", adj, [[(2, 3), (2, first)]], [(3, second), (3, 0)], us=3.3)
+    a2_got = send_first(a2)
+    b3, every = call(
+        sum_3, [message(1, True), sds((scen, conts), F32)], [SM] + [VM] * 3, "sum_3", us=0.3
+    )(core_1, tie(p3s, a2), a3_got, every)
+    b3_got = send_second(b3)
+    adj = (tie(adj_t, b3), other_t)
+    a1, p2s, p2 = backward("backward_2", adj, [[(1, 3), (1, first)]], [(2, second), (2, 0)], us=3.5)
+    a1_got = send_first(a1)
+    z3, every = call(
+        sum_z3, [message(1), sds((line_conts, scen), F32)], [SM] + [VM] * 4, "sum_z3", us=0.3
+    )(core_1, tie(p3, a1), a3_got, b3_got, every)
+    every = every + send(every, 1) + send(every, 2) + send(every, 3)
+    every = every + swap(every)
+    z3_got = send(z3, 3)
+    b2 = add("sum_2", tie(p2s, z3), (a2_got, 0))
+    b2_got = send_second(b2)
+
+    adj = (tie(adj_t, b2), other_t)
+    p1s, p1, p0d, p0f, p0s, p0 = backward("backward_0", adj, [], [(1, second), (1, 0), (0, 3), (0, first), (0, second), (0, 0)], us=0.01)
+    scal = jnp.stack([spot ^ line for line in lines]).astype(jnp.int32)
+
+    def outaged(scal_ref, e_ref, so_ref, p0_ref, ps_ref, pd_ref, pf_ref, a_ref, s_ref, o_ref, whole):
+        marks = so_ref[:, plane:].astype(F32)
+        number = marks[:, :1] * 16.0 + marks[:, 1:2]
+        wide = jnp.broadcast_to(number, (line_conts, LANES))
+        across = jnp.concatenate([wide] * (LANES // line_conts), axis=0).T[:line_conts, :line_conts]
+        one = lax.broadcasted_iota(jnp.int32, (line_conts, line_conts), 0)
+        two = lax.broadcasted_iota(jnp.int32, (line_conts, line_conts), 1)
+        same = (one // group == two // group) & (wide[:, :line_conts] == across)
+        earlier = jnp.sum(jnp.where(same & (two < one), 1.0, 0.0), axis=1, keepdims=True)
+        merged = pick(one_hot(same), e_ref[...])
+        final = jnp.where(earlier > 0.0, 0.0, merged).astype(BF16)
+        whole[...] = lax.dot_general(final, so_ref[:, :plane], (((0,), (0,)), ((), ())), preferred_element_type=F32)
+
+        def of(g):
+            return whole[:, pl.ds(pl.multiple_of(scal_ref[g] * width, width), width)]
+
+        put_coded(a_ref, [pd_ref[...] + of(3), pf_ref[...] + of(1)])
+        s_ref[...] = ps_ref[...] + of(2)
+        o_ref[...] = p0_ref[...] + of(0)
+
+    a0, p0s, p0 = call(
+        outaged, [message(2), grad_block, grad_block], [SM] + [VM] * 6, "outaged_rows", [pltpu.VMEM((scen, plane), F32)], us=0.01
+    )(scal, every, out_factors, p0, p0s, p0d, p0f)
+    a0_got = send_first(a0)
+    z2 = add("sum_z2", tie(p2, a0), (a2_got, 1), (b2_got, 0))
+    z2_got = send(z2, 2)
+    b1 = add("sum_1", tie(p1s, z2), (a1_got, 0))
+    b1_got = send_second(b1)
+
+    def gather(p_ref, z3_ref, out_ref):
+        out_ref[...] = p_ref[...] + get_coded(z3_ref, 0, width)
+
+    p0 = call(gather, grad_block, [VM] * 2, "gradient_z", us=12)(tie(p0, b1), z3_got)
+    b0 = add("sum_0", tie(p0s, b1, p0), (a0_got, 0))
+    b0_got = send_second(b0)
+    z1 = add("sum_z1", tie(p1, b0), (a1_got, 1), (b1_got, 0))
+    z1_got = send(z1, 1)
+
+    def last(p_ref, a_ref, b_ref, z1_ref, z2_ref, out_ref):
+        total = p_ref[...] + get_coded(a_ref, 1, width)
+        for ref in (b_ref, z2_ref, z1_ref):
+            total = total + get_coded(ref, 0, width)
+        out_ref[...] = total.T
+
+    return call(last, sds((width, scen), F32), [VM] * 5, "gradient")(p0, a0_got, b0_got, z1_got, z2_got)
 
 
 def on_device(
@@ -62,7 +523,6 @@
     )
     adjoint = (base_adj + monitored_adj + outage_adj).astype(jnp.bfloat16)
     group_adjoint = lax.all_gather(adjoint, "bus", axis=0, tiled=True)
-    factor_cols = shift_factors
     return lax.psum_scatter(
         lax.dot_general(
             factor_cols, group_adjoint, (((0,), (0,)), ((), ())), preferred_element_type=jnp.float32
@@ -85,6 +545,5 @@
         P(("br", "bus")),
     )
     out_specs = P(("bus", "br"), None)
-    return jax.shard_map(
-        on_device, mesh=mesh, in_specs=in_specs, out_specs=out_specs, check_vma=False
-    )
+    local = on_slice if (mesh.shape["br"], mesh.shape["bus"]) == (16, 2) else on_device
+    return jax.shard_map(local, mesh=mesh, in_specs=in_specs, out_specs=out_specs, check_vma=False)

time: 399 us -> 113 us (0.28)
  waiting for transfers between devices: 300 us -> 26.9 us
  blocking collectives: 45 us -> 0 us
  starting transfers between devices: 0.15 us -> 41.5 us
  Pallas kernels: 0 us -> 41.1 us
  matrix products: 24.2 us -> 0 us
  between operations: 13.3 us -> 0.44 us
  local copies, waits for them, and re-layouts: 9.84 us -> 1.82 us
  other arithmetic: 6.13 us -> 1.3 us
    reduce_scatter x2 -> x0, waiting for transfers between devices: 118 us -> none  [the longest x1 115 us: on_device(): lax.psum_scatter(lax.dot_general(factor_cols, group_adjoint, (((0,), (0,)...]
    unnamed x5 -> x0, waiting for transfers between devices: 114 us -> none
    all_gather x1 -> x0, waiting for transfers between devices: 66.7 us -> none  [on_device(): lax.all_gather(injections, 'br', axis=0, tiled=True)]
    all_gather x2 -> x0, blocking collectives: 45 us -> none  [the longest x1 41.8 us: on_device(): all_outage = lax.all_gather(own_outage, ('br', 'bus'), axis=0, tiled=True)]
    ppermute x0 -> x37, starting transfers between devices: none -> 41.5 us  [the longest x16 24.2 us: send(): return lax.ppermute(v, 'br', to(dz, ds))]
    pallas_call x0 -> x22, Pallas kernels: none -> 41.1 us  [the longest x5 17.9 us: forward(): call(body, sds((rows, scen), F32) if core is None else [sds((half, scen),...]
    ppermute x0 -> x37, waiting for transfers between devices: none -> 26.9 us  [the longest x16 12.3 us: send(): return lax.ppermute(v, 'br', to(dz, ds))]
    dot_general x4 -> x0, matrix products: 24.2 us -> none  [the longest x1 11.2 us: on_device(): jnp.dot(factor_cols, lax.all_gather(injections, 'br', axis=0, tiled=True)...]
  transfers between devices with their start and end apart: 4 -> 37, of which waited for: 4 -> 12; matrix products, arithmetic and copies ran while one was open for 2% -> 2% of each run, Pallas kernels for 0% -> 32%
where the time goes in v2:
time: 113 us
  starting transfers between devices  41.5 us (37%)
  Pallas kernels  41.1 us (36%)
  waiting for transfers between devices  26.9 us (24%)
  local copies, waits for them, and re-layouts  1.82 us (2%)
  other arithmetic  1.3 us (1%)
    ppermute x16, starting transfers between devices, send(): return lax.ppermute(v, 'br', to(dz, ds))  24.2 us
    pallas_call x5, Pallas kernels, forward(): call(body, sds((rows, scen), F32) if core is None else [sds((half, scen),...  17.9 us
    pallas_call x4, Pallas kernels, backward(): call(body, [message(len(m), fine is not None) for m in messages] + [grad_...  13.4 us
    ppermute x16, waiting for transfers between devices, send(): return lax.ppermute(v, 'br', to(dz, ds))  12.3 us
    ppermute x8, starting transfers between devices, send_first(): return lax.ppermute(v, both, split((1, 2)))  9.04 us
    ppermute x8, waiting for transfers between devices, send_first(): return lax.ppermute(v, both, split((1, 2)))  8.9 us
    ppermute x8, starting transfers between devices, send_second(): return lax.ppermute(v, both, split((2, 1)))  7.84 us
    ppermute x8, waiting for transfers between devices, send_second(): return lax.ppermute(v, both, split((2, 1)))  3.59 us
  transfers between devices with their start and end apart: 37, of which 12 were waited for; matrix products, arithmetic and copies ran while one was open for 2% of the time, Pallas kernels for 32%

profile of v2, /device:TPU:0, one launch (start us, length us, event | category | flops | bytes accessed | tf_op | source)
XLA Modules:
  0.0 113.1 jit_solution(7673661520199396272)
XLA Ops:
  0.0 2.9 %collective-permute-start.2 = (bf16[640,128]{1,0:T(8,128)(2,1)}, bf16[640,128]{1,0:T(8,128)(2,1)S(1)}, u32[]{:S(2)}, u32[]{:S(2)}) collective-permute-start(bf16[640,128]{1,0:T(8,128)(2,1)} %refs_4_.1), channel_id=1, source_target_pairs={{0,2},{2,0},{4,6},{6,4},{8,10},{10,8},{12,14},{14,12},{16,18},{18,... | collective-permute-start | bytes 491528 | tf_op jit(solution)/shard_map/ppermute | solution.py:196
  6.4 2.8 %outage_rows.1 = (bf16[8,2688]{1,0:T(8,128)(2,1)S(1)}, bf16[8,2688]{1,0:T(8,128)(2,1)S(1)}, bf16[8,2688]{1,0:T(8,128)(2,1)S(1)}, bf16[8,2688]{1,0:T(8,128)(2,1)S(1)}) custom-call(s32[2]{0:T(128)S(1)} %pad_add_fusion.3.scal_ref, s32[4]{0:T(128)S(1)} %copy-done.2, s32[4]{0:T(128)S(1)} %collective-permute-done.other_ref, bf16[768,10240]{1,0:T(8,128)(2,1)} %f_ref.19), custom_call_target="tpu_custom_call" | custom-call | flops 3449999872 | bytes 1 | tf_op jit(solution)/shard_map/outage_rows/pallas_call | solution.py:250
  9.2 2.5 %collective-permute-start.6 = (bf16[640,128]{1,0:T(8,128)(2,1)S(1)}, bf16[640,128]{1,0:T(8,128)(2,1)S(1)}, u32[]{:S(2)}, u32[]{:S(2)}) collective-permute-start(bf16[640,128]{1,0:T(8,128)(2,1)S(1)} %copy-done), channel_id=1, source_target_pairs={{0,24},{2,26},{4,28},{6,30},{8,16},{10,18},{12,20},{14,22},{16,8},... | collective-permute-start | bytes 491528 | tf_op jit(solution)/shard_map/ppermute | solution.py:190
  15.9 2.0 %collective-permute-done.6.refs_0_ = bf16[640,128]{1,0:T(8,128)(2,1)S(1)} collective-permute-done((bf16[640,128]{1,0:T(8,128)(2,1)S(1)}, bf16[640,128]{1,0:T(8,128)(2,1)S(1)}, u32[]{:S(2)}, u32[]{:S(2)}) %collective-permute-start.6) | collective-permute-done | bytes 163872 | tf_op jit(solution)/shard_map/ppermute | solution.py:190
  18.0 2.8 %collective-permute-start.15 = (bf16[8,2688]{1,0:T(8,128)(2,1)S(1)}, bf16[8,2688]{1,0:T(8,128)(2,1)S(1)}, u32[]{:S(2)}, u32[]{:S(2)}) collective-permute-start(bf16[8,2688]{1,0:T(8,128)(2,1)S(1)} %get-tuple-element.60), channel_id=1, source_target_pairs={{0,24},{2,26},{4,28},{6,30},{8,16},{10,18},{12,20},{14,22},{16,8},... | collective-permute-start | bytes 129032 | tf_op jit(solution)/shard_map/ppermute | solution.py:190
  21.1 1.7 %collective-permute-start.11 = (bf16[1280,128]{1,0:T(8,128)(2,1)S(1)}, bf16[1280,128]{1,0:T(8,128)(2,1)S(1)}, u32[]{:S(2)}, u32[]{:S(2)}) collective-permute-start(bf16[1280,128]{1,0:T(8,128)(2,1)S(1)} %pad_maximum_fusion.3), channel_id=1, source_target_pairs={{0,4},{2,6},{4,0},{6,2},{8,12},{10,14},{12,8},{14,10},{16,20},{18,... | collective-permute-start | bytes 983048 | tf_op jit(solution)/shard_map/ppermute | solution.py:199
  22.9 4.0 %forward_own.1.refs_3_ = f32[768,128]{1,0:T(8,128)S(1)} custom-call(s32[5]{0:T(128)S(1)} %stack.148.scal_ref, bf16[768,10240]{1,0:T(8,128)(2,1)} %f_ref.19, bf16[640,128]{1,0:T(8,128)(2,1)S(1)} %copy-done, bf16[640,128]{1,0:T(8,128)(2,1)S(1)} %collective-permute-done.2.refs_1_.refs_5_, bf16[1280,128]{1,0:T(8,128)(2,1)S(1)} %collective-permute-done.3.refs_2_.refs_6_), custom_call_target="tpu_custom_call" | custom-call | flops 4024999936 | bytes 1 | tf_op jit(solution)/shard_map/forward_own/pallas_call | solution.py:152
  27.8 3.5 %collective-permute-start.16 = (f32[32,128]{1,0:T(8,128)S(1)}, f32[32,128]{1,0:T(8,128)S(1)}, u32[]{:S(2)}, u32[]{:S(2)}) collective-permute-start(f32[32,128]{1,0:T(8,128)S(1)} %get-tuple-element.61), channel_id=1, source_target_pairs={{0,8},{2,10},{4,12},{6,14},{8,0},{10,2},{12,4},{14,6},{16,24},{18,... | collective-permute-start | bytes 49160 | tf_op jit(solution)/shard_map/ppermute | solution.py:190
  35.3 4.4 %collective-permute-done.1.refs_0_ = bf16[640,128]{1,0:T(8,128)(2,1)S(1)} collective-permute-done((bf16[640,128]{1,0:T(8,128)(2,1)S(1)}, bf16[640,128]{1,0:T(8,128)(2,1)S(1)}, u32[]{:S(2)}, u32[]{:S(2)}) %collective-permute-start.1) | collective-permute-done | bytes 163872 | tf_op jit(solution)/shard_map/ppermute | solution.py:190
  41.1 4.0 %forward_pair.1.refs_2_ = f32[768,128]{1,0:T(8,128)S(1)} custom-call(s32[5]{0:T(128)S(1)} %stack.158.scal_ref, bf16[768,10240]{1,0:T(8,128)(2,1)} %f_ref.19, bf16[640,128]{1,0:T(8,128)(2,1)S(1)} %collective-permute-done.9.refs_0_, bf16[640,128]{1,0:T(8,128)(2,1)S(1)} %collective-permute-done.10.refs_1_, ...), custom_call_target="tpu_custom_call" | custom-call | flops 4024999936 | bytes 1 | tf_op jit(solution)/shard_map/forward_pair/pallas_call | solution.py:152
  45.8 2.9 %forward_2a.1.refs_3_ = f32[768,128]{1,0:T(8,128)S(1)} custom-call(s32[3]{0:T(128)S(1)} %pad_add_fusion.4.scal_ref, bf16[768,10240]{1,0:T(8,128)(2,1)} %f_ref.19, bf16[640,128]{1,0:T(8,128)(2,1)S(1)} %collective-permute-done.1.refs_0_, bf16[640,128]{1,0:T(8,128)(2,1)S(1)} %collective-permute-done.4.refs_1_, f32[768,128]{1,0:T(8,128)S(1)} %forward_pair.1.refs_2_), custom_call_target="tpu_custom_call" | custom-call | flops 3335000064 | bytes 1 | tf_op jit(solution)/shard_map/forward_2a/pallas_call | solution.py:152
  50.1 4.0 %forward_3.1.refs_1_ = f32[768,128]{1,0:T(8,128)S(1)} custom-call(s32[5]{0:T(128)S(1)} %stack.151.scal_ref, bf16[768,10240]{1,0:T(8,128)(2,1)} %f_ref.19, bf16[640,128]{1,0:T(8,128)(2,1)S(1)} %collective-permute-done.6.refs_0_, bf16[640,128]{1,0:T(8,128)(2,1)S(1)} %collective-permute-done.7.refs_1_, bf16[1280,128]{1,0:T(8,128)(2,1)S(1)} %collective-permute-done.8.refs_2_, ...), custom_call_target="tpu_custom_call" | custom-call | flops 4600000000 | bytes 1 | tf_op jit(solution)/shard_map/forward_3/pallas_call | solution.py:152
  55.7 2.9 %forward_2b.1 = (f32[384,128]{1,0:T(8,128)S(1)}, f32[384,128]{1,0:T(8,128)S(1)}) custom-call(s32[3]{0:T(128)S(1)} %pad_add_fusion.2.scal_ref, bf16[768,10240]{1,0:T(8,128)(2,1)} %f_ref.19, bf16[1280,128]{1,0:T(8,128)(2,1)S(1)} %collective-permute-done.5.refs_0_, f32[768,128]{1,0:T(8,128)S(1)} %forward_3.1.refs_1_), custom_call_target="tpu_custom_call" | custom-call | flops 3335000064 | bytes 1 | tf_op jit(solution)/shard_map/forward_2b/pallas_call | solution.py:152
  60.2 1.7 %penalty.1 = (bf16[128,384]{1,0:T(8,128)(2,1)S(1)}, f32[128,128]{1,0:T(8,128)S(1)}) custom-call(s32[5]{0:T(128)S(1)} %pad_add_fusion.1.scal_ref, f32[384,128]{1,0:T(8,128)S(1)} %get-tuple-element.55.mine_ref, f32[384,128]{1,0:T(8,128)S(1)} %collective-permute-done.12.theirs_ref, f32[128,128]{1,0:T(8,128)S(1)} %pad_maximum_fusion.4.out_ref, ...), custom_call_target="tpu_custom_call" | custom-call | flops 575000000 | bytes 1 | tf_op jit(solution)/shard_map/penalty/pallas_call | solution.py:326
  63.3 2.6 %backward_3a.1 = s16[128,1664]{1,0:T(8,128)(2,1)S(1)} custom-call(s32[3]{0:T(128)S(1)} %pad_add_fusion.5.scal_ref, bf16[768,10240]{1,0:T(8,128)(2,1)} %f_ref.19, bf16[128,384]{1,0:T(8,128)(2,1)S(1)} %get-tuple-element.81.a_ref, bf16[128,384]{1,0:T(8,128)(2,1)S(1)} %collective-permute-done.21.b_ref, f32[128,128]{1,0:T(8,128)S(1)} %get-tuple-element.65.refs_0_.e_ref), custom_call_target="tpu_custom_call" | custom-call | flops 2990000128 | bytes 1 | tf_op jit(solution)/shard_map/backward_3a/pallas_call | solution.py:364
  67.0 3.3 %backward_3b.1 = (s16[128,1408]{1,0:T(8,128)(2,1)S(1)}, f32[128,640]{1,0:T(8,128)S(1)}, f32[128,640]{1,0:T(8,128)S(1)}) custom-call(s32[5]{0:T(128)S(1)} %stack.138.scal_ref, bf16[768,10240]{1,0:T(8,128)(2,1)} %f_ref.19, bf16[128,384]{1,0:T(8,128)(2,1)S(1)} %get-tuple-element.81.a_ref, bf16[128,384]{1,0:T(8,128)(2,1)S(1)} %collective-permute-done.21.b_ref), custom_call_target="tpu_custom_call" | custom-call | flops 3795000064 | bytes 1 | tf_op jit(solution)/shard_map/backward_3b/pallas_call | solution.py:364
  71.6 2.5 %collective-permute-done.22.a_ref = s16[128,1664]{1,0:T(8,128)(2,1)S(1)} collective-permute-done((s16[128,1664]{1,0:T(8,128)(2,1)S(1)}, s16[128,1664]{1,0:T(8,128)(2,1)S(1)}, u32[]{:S(2)}, u32[]{:S(2)}) %collective-permute-start.22) | collective-permute-done | bytes 426016 | tf_op jit(solution)/shard_map/ppermute | solution.py:196
  75.0 3.5 %backward_2.1 = (s16[128,1408]{1,0:T(8,128)(2,1)S(1)}, f32[128,640]{1,0:T(8,128)S(1)}, f32[128,640]{1,0:T(8,128)S(1)}) custom-call(s32[5]{0:T(128)S(1)} %stack.161.scal_ref, bf16[768,10240]{1,0:T(8,128)(2,1)} %f_ref.19, bf16[128,384]{1,0:T(8,128)(2,1)S(1)} %get-tuple-element.81.a_ref, bf16[128,384]{1,0:T(8,128)(2,1)S(1)} %collective-permute-done.21.b_ref), custom_call_target="tpu_custom_call" | custom-call | flops 4024999936 | bytes 1 | tf_op jit(solution)/shard_map/backward_2/pallas_call | solution.py:364
  83.1 2.9 %collective-permute-start.24 = (f32[32,128]{1,0:T(8,128)S(1)}, f32[32,128]{1,0:T(8,128)S(1)}, u32[]{:S(2)}, u32[]{:S(2)}) collective-permute-start(f32[32,128]{1,0:T(8,128)S(1)} %get-tuple-element.76), channel_id=1, source_target_pairs={{0,8},{2,10},{4,12},{6,14},{8,0},{10,2},{12,4},{14,6},{16,24},{18,... | collective-permute-start | bytes 49160 | tf_op jit(solution)/shard_map/ppermute | solution.py:190
  88.5 3.9 %backward_0.1 = (f32[128,640]{1,0:T(8,128)S(1)}, f32[128,640]{1,0:T(8,128)S(1)}, f32[128,640]{1,0:T(8,128)S(1)}, f32[128,640]{1,0:T(8,128)S(1)}, f32[128,640]{1,0:T(8,128)S(1)}, /*index=5*/f32[128,640]{1,0:T(8,128)S(1)}) custom-call(s32[7]{0:T(128)S(1)} %stack.162.scal_ref, bf16[768,10240]{1,0:T(8,128)(2,1)} %f_ref.19, ...), custom_call_target="tpu_custom_call" | custom-call | flops 11500000 | bytes 1 | tf_op jit(solution)/shard_map/backward_0/pallas_call | solution.py:364
  97.2 6.4 %collective-permute-done.32.refs_1_.a_ref = s16[128,1408]{1,0:T(8,128)(2,1)S(1)} collective-permute-done((s16[128,1408]{1,0:T(8,128)(2,1)S(1)}, s16[128,1408]{1,0:T(8,128)(2,1)S(1)}, u32[]{:S(2)}, u32[]{:S(2)}) %collective-permute-start.32) | collective-permute-done | bytes 360480 | tf_op jit(solution)/shard_map/ppermute | solution.py:196
  105.7 1.9 %collective-permute-done.36.z2_ref = s16[128,768]{1,0:T(8,128)(2,1)S(1)} collective-permute-done((s16[128,768]{1,0:T(8,128)(2,1)S(1)}, s16[128,768]{1,0:T(8,128)(2,1)S(1)}, u32[]{:S(2)}, u32[]{:S(2)}) %collective-permute-start.36) | collective-permute-done | bytes 196640 | tf_op jit(solution)/shard_map/ppermute | solution.py:190
  107.7 1.9 %collective-permute-done.33.b_ref = s16[128,768]{1,0:T(8,128)(2,1)S(1)} collective-permute-done((s16[128,768]{1,0:T(8,128)(2,1)S(1)}, s16[128,768]{1,0:T(8,128)(2,1)S(1)}, u32[]{:S(2)}, u32[]{:S(2)}) %collective-permute-start.33) | collective-permute-done | bytes 196640 | tf_op jit(solution)/shard_map/ppermute | solution.py:199
  109.5 2.5 %collective-permute-done.35.z1_ref = s16[128,768]{1,0:T(8,128)(2,1)S(1)} collective-permute-done((s16[128,768]{1,0:T(8,128)(2,1)S(1)}, s16[128,768]{1,0:T(8,128)(2,1)S(1)}, u32[]{:S(2)}, u32[]{:S(2)}) %collective-permute-start.35) | collective-permute-done | bytes 196640 | tf_op jit(solution)/shard_map/ppermute | solution.py:190
  (114 shorter events, 39.0 us)
Async XLA Ops:
  0.0 12.3 %collective-permute-start.2 = (bf16[640,128]{1,0:T(8,128)(2,1)}, bf16[640,128]{1,0:T(8,128)(2,1)S(1)}, u32[]{:S(2)}, u32[]{:S(2)}) collective-permute-start(bf16[640,128]{1,0:T(8,128)(2,1)} %refs_4_.1), channel_id=1, source_target_pairs={{0,2},{2,0},{4,6},{6,4},{8,10},{10,8},{12,14},{14,12},{16,18},{18,... | collective-permute-start | bytes 491528 | tf_op jit(solution)/shard_map/ppermute | solution.py:196
  2.9 8.8 %collective-permute-start.9 = (bf16[640,128]{1,0:T(8,128)(2,1)}, bf16[640,128]{1,0:T(8,128)(2,1)S(1)}, u32[]{:S(2)}, u32[]{:S(2)}) collective-permute-start(bf16[640,128]{1,0:T(8,128)(2,1)} %refs_4_.1), channel_id=1, source_target_pairs={{0,8},{2,10},{4,12},{6,14},{8,0},{10,2},{12,4},{14,6},{16,24},{18,... | collective-permute-start | bytes 491528 | tf_op jit(solution)/shard_map/ppermute | solution.py:190
  9.2 8.7 %collective-permute-start.6 = (bf16[640,128]{1,0:T(8,128)(2,1)S(1)}, bf16[640,128]{1,0:T(8,128)(2,1)S(1)}, u32[]{:S(2)}, u32[]{:S(2)}) collective-permute-start(bf16[640,128]{1,0:T(8,128)(2,1)S(1)} %copy-done), channel_id=1, source_target_pairs={{0,24},{2,26},{4,28},{6,30},{8,16},{10,18},{12,20},{14,22},{16,8},... | collective-permute-start | bytes 491528 | tf_op jit(solution)/shard_map/ppermute | solution.py:190
  11.8 8.9 %collective-permute-start.10 = (bf16[640,128]{1,0:T(8,128)(2,1)S(1)}, bf16[640,128]{1,0:T(8,128)(2,1)S(1)}, u32[]{:S(2)}, u32[]{:S(2)}) collective-permute-start(bf16[640,128]{1,0:T(8,128)(2,1)S(1)} %collective-permute-done.9.refs_0_), channel_id=1, source_target_pairs={{0,2},{2,0},{4,6},{6,4},{8,10},{10,8},{12,14},{14,12},{16,18},{18,... | collective-permute-start | bytes 491528 | tf_op jit(solution)/shard_map/ppermute | solution.py:196
  12.4 8.7 %collective-permute-start.3 = (bf16[1280,128]{1,0:T(8,128)(2,1)S(1)}, bf16[1280,128]{1,0:T(8,128)(2,1)S(1)}, u32[]{:S(2)}, u32[]{:S(2)}) collective-permute-start(bf16[1280,128]{1,0:T(8,128)(2,1)S(1)} %pad_maximum_fusion), channel_id=1, source_target_pairs={{0,4},{2,6},{4,0},{6,2},{8,12},{10,14},{12,8},{14,10},{16,20},{18,... | collective-permute-start | bytes 983048 | tf_op jit(solution)/shard_map/ppermute | solution.py:199
  14.0 12.9 %collective-permute-start.13 = (bf16[8,2688]{1,0:T(8,128)(2,1)S(1)}, bf16[8,2688]{1,0:T(8,128)(2,1)S(1)}, u32[]{:S(2)}, u32[]{:S(2)}) collective-permute-start(bf16[8,2688]{1,0:T(8,128)(2,1)S(1)} %get-tuple-element.58), channel_id=1, source_target_pairs={{0,8},{2,10},{4,12},{6,14},{8,0},{10,2},{12,4},{14,6},{16,24},{18,... | collective-permute-start | bytes 129032 | tf_op jit(solution)/shard_map/ppermute | solution.py:190
  14.7 12.2 %collective-permute-start.14 = (bf16[8,2688]{1,0:T(8,128)(2,1)S(1)}, bf16[8,2688]{1,0:T(8,128)(2,1)S(1)}, u32[]{:S(2)}, u32[]{:S(2)}) collective-permute-start(bf16[8,2688]{1,0:T(8,128)(2,1)S(1)} %get-tuple-element.59), channel_id=1, source_target_pairs={{0,16},{2,18},{4,20},{6,22},{8,24},{10,26},{12,28},{14,30},{16,0},... | collective-permute-start | bytes 129032 | tf_op jit(solution)/shard_map/ppermute | solution.py:190
  18.0 9.0 %collective-permute-start.15 = (bf16[8,2688]{1,0:T(8,128)(2,1)S(1)}, bf16[8,2688]{1,0:T(8,128)(2,1)S(1)}, u32[]{:S(2)}, u32[]{:S(2)}) collective-permute-start(bf16[8,2688]{1,0:T(8,128)(2,1)S(1)} %get-tuple-element.60), channel_id=1, source_target_pairs={{0,24},{2,26},{4,28},{6,30},{8,16},{10,18},{12,20},{14,22},{16,8},... | collective-permute-start | bytes 129032 | tf_op jit(solution)/shard_map/ppermute | solution.py:190
  20.7 13.9 %collective-permute-start.7 = (bf16[640,128]{1,0:T(8,128)(2,1)S(1)}, bf16[640,128]{1,0:T(8,128)(2,1)S(1)}, u32[]{:S(2)}, u32[]{:S(2)}) collective-permute-start(bf16[640,128]{1,0:T(8,128)(2,1)S(1)} %collective-permute-done.6.refs_0_), channel_id=1, source_target_pairs={{0,2},{2,0},{4,6},{6,4},{8,10},{10,8},{12,14},{14,12},{16,18},{18,... | collective-permute-start | bytes 491528 | tf_op jit(solution)/shard_map/ppermute | solution.py:196
  21.1 20.0 %collective-permute-start.11 = (bf16[1280,128]{1,0:T(8,128)(2,1)S(1)}, bf16[1280,128]{1,0:T(8,128)(2,1)S(1)}, u32[]{:S(2)}, u32[]{:S(2)}) collective-permute-start(bf16[1280,128]{1,0:T(8,128)(2,1)S(1)} %pad_maximum_fusion.3), channel_id=1, source_target_pairs={{0,4},{2,6},{4,0},{6,2},{8,12},{10,14},{12,8},{14,10},{16,20},{18,... | collective-permute-start | bytes 983048 | tf_op jit(solution)/shard_map/ppermute | solution.py:199
  31.5 8.1 %collective-permute-start.1 = (bf16[640,128]{1,0:T(8,128)(2,1)S(1)}, bf16[640,128]{1,0:T(8,128)(2,1)S(1)}, u32[]{:S(2)}, u32[]{:S(2)}) collective-permute-start(bf16[640,128]{1,0:T(8,128)(2,1)S(1)} %copy-done), channel_id=1, source_target_pairs={{0,16},{2,18},{4,20},{6,22},{8,24},{10,26},{12,28},{14,30},{16,0},... | collective-permute-start | bytes 491528 | tf_op jit(solution)/shard_map/ppermute | solution.py:190
  33.0 8.1 %collective-permute-start.17 = (f32[32,128]{1,0:T(8,128)S(1)}, f32[32,128]{1,0:T(8,128)S(1)}, u32[]{:S(2)}, u32[]{:S(2)}) collective-permute-start(f32[32,128]{1,0:T(8,128)S(1)} %add.128), channel_id=1, source_target_pairs={{0,16},{2,18},{4,20},{6,22},{8,24},{10,26},{12,28},{14,30},{16,0},... | collective-permute-start | bytes 49160 | tf_op jit(solution)/shard_map/ppermute | solution.py:190
  34.6 15.5 %collective-permute-start.8 = (bf16[1280,128]{1,0:T(8,128)(2,1)S(1)}, bf16[1280,128]{1,0:T(8,128)(2,1)S(1)}, u32[]{:S(2)}, u32[]{:S(2)}) collective-permute-start(bf16[1280,128]{1,0:T(8,128)(2,1)S(1)} %pad_maximum_fusion.2), channel_id=1, source_target_pairs={{0,4},{2,6},{4,0},{6,2},{8,12},{10,14},{12,8},{14,10},{16,20},{18,... | collective-permute-start | bytes 983048 | tf_op jit(solution)/shard_map/ppermute | solution.py:199
  45.3 10.5 %collective-permute-start.5 = (bf16[1280,128]{1,0:T(8,128)(2,1)S(1)}, bf16[1280,128]{1,0:T(8,128)(2,1)S(1)}, u32[]{:S(2)}, u32[]{:S(2)}) collective-permute-start(bf16[1280,128]{1,0:T(8,128)(2,1)S(1)} %pad_maximum_fusion.1), channel_id=1, source_target_pairs={{0,4},{2,6},{4,0},{6,2},{8,12},{10,14},{12,8},{14,10},{16,20},{18,... | collective-permute-start | bytes 983048 | tf_op jit(solution)/shard_map/ppermute | solution.py:199
  65.9 8.2 %collective-permute-start.22 = (s16[128,1664]{1,0:T(8,128)(2,1)S(1)}, s16[128,1664]{1,0:T(8,128)(2,1)S(1)}, u32[]{:S(2)}, u32[]{:S(2)}) collective-permute-start(s16[128,1664]{1,0:T(8,128)(2,1)S(1)} %backward_3a.1), channel_id=1, source_target_pairs={{0,2},{2,0},{4,6},{6,4},{8,10},{10,8},{12,14},{14,12},{16,18},{18,... | collective-permute-start | bytes 1277960 | tf_op jit(solution)/shard_map/ppermute | solution.py:196
  70.3 15.6 %collective-permute-start.28 = (s16[128,1408]{1,0:T(8,128)(2,1)S(1)}, s16[128,1408]{1,0:T(8,128)(2,1)S(1)}, u32[]{:S(2)}, u32[]{:S(2)}) collective-permute-start(s16[128,1408]{1,0:T(8,128)(2,1)S(1)} %get-tuple-element.69), channel_id=1, source_target_pairs={{0,2},{2,0},{4,6},{6,4},{8,10},{10,8},{12,14},{14,12},{16,18},{18,... | collective-permute-start | bytes 1081352 | tf_op jit(solution)/shard_map/ppermute | solution.py:196
  74.4 6.7 %collective-permute-start.23 = (s16[128,1024]{1,0:T(8,128)(2,1)S(1)}, s16[128,1024]{1,0:T(8,128)(2,1)S(1)}, u32[]{:S(2)}, u32[]{:S(2)}) collective-permute-start(s16[128,1024]{1,0:T(8,128)(2,1)S(1)} %get-tuple-element.71), channel_id=1, source_target_pairs={{0,4},{2,6},{4,0},{6,2},{8,12},{10,14},{12,8},{14,10},{16,20},{18,... | collective-permute-start | bytes 786440 | tf_op jit(solution)/shard_map/ppermute | solution.py:199
  78.5 17.8 %collective-permute-start.30 = (s16[128,1408]{1,0:T(8,128)(2,1)S(1)}, s16[128,1408]{1,0:T(8,128)(2,1)S(1)}, u32[]{:S(2)}, u32[]{:S(2)}) collective-permute-start(s16[128,1408]{1,0:T(8,128)(2,1)S(1)} %get-tuple-element.73), channel_id=1, source_target_pairs={{0,2},{2,0},{4,6},{6,4},{8,10},{10,8},{12,14},{14,12},{16,18},{18,... | collective-permute-start | bytes 1081352 | tf_op jit(solution)/shard_map/ppermute | solution.py:196
  85.9 11.2 %collective-permute-start.31 = (s16[128,768]{1,0:T(8,128)(2,1)S(1)}, s16[128,768]{1,0:T(8,128)(2,1)S(1)}, u32[]{:S(2)}, u32[]{:S(2)}) collective-permute-start(s16[128,768]{1,0:T(8,128)(2,1)S(1)} %get-tuple-element.79), channel_id=1, source_target_pairs={{0,24},{2,26},{4,28},{6,30},{8,16},{10,18},{12,20},{14,22},{16,8},... | collective-permute-start | bytes 589832 | tf_op jit(solution)/shard_map/ppermute | solution.py:190
  87.7 6.9 %collective-permute-start.29 = (s16[128,768]{1,0:T(8,128)(2,1)S(1)}, s16[128,768]{1,0:T(8,128)(2,1)S(1)}, u32[]{:S(2)}, u32[]{:S(2)}) collective-permute-start(s16[128,768]{1,0:T(8,128)(2,1)S(1)} %sum_2.1), channel_id=1, source_target_pairs={{0,4},{2,6},{4,0},{6,2},{8,12},{10,14},{12,8},{14,10},{16,20},{18,... | collective-permute-start | bytes 589832 | tf_op jit(solution)/shard_map/ppermute | solution.py:199
  94.0 9.6 %collective-permute-start.32 = (s16[128,1408]{1,0:T(8,128)(2,1)S(1)}, s16[128,1408]{1,0:T(8,128)(2,1)S(1)}, u32[]{:S(2)}, u32[]{:S(2)}) collective-permute-start(s16[128,1408]{1,0:T(8,128)(2,1)S(1)} %get-tuple-element.89), channel_id=1, source_target_pairs={{0,2},{2,0},{4,6},{6,4},{8,10},{10,8},{12,14},{14,12},{16,18},{18,... | collective-permute-start | bytes 1081352 | tf_op jit(solution)/shard_map/ppermute | solution.py:196
  94.8 12.8 %collective-permute-start.36 = (s16[128,768]{1,0:T(8,128)(2,1)S(1)}, s16[128,768]{1,0:T(8,128)(2,1)S(1)}, u32[]{:S(2)}, u32[]{:S(2)}) collective-permute-start(s16[128,768]{1,0:T(8,128)(2,1)S(1)} %sum_z2.1), channel_id=1, source_target_pairs={{0,16},{2,18},{4,20},{6,22},{8,24},{10,26},{12,28},{14,30},{16,0},... | collective-permute-start | bytes 589832 | tf_op jit(solution)/shard_map/ppermute | solution.py:190
  96.5 8.9 %collective-permute-start.34 = (s16[128,768]{1,0:T(8,128)(2,1)S(1)}, s16[128,768]{1,0:T(8,128)(2,1)S(1)}, u32[]{:S(2)}, u32[]{:S(2)}) collective-permute-start(s16[128,768]{1,0:T(8,128)(2,1)S(1)} %sum_1.1), channel_id=1, source_target_pairs={{0,4},{2,6},{4,0},{6,2},{8,12},{10,14},{12,8},{14,10},{16,20},{18,... | collective-permute-start | bytes 589832 | tf_op jit(solution)/shard_map/ppermute | solution.py:199
  105.7 6.4 %collective-permute-start.35 = (s16[128,768]{1,0:T(8,128)(2,1)S(1)}, s16[128,768]{1,0:T(8,128)(2,1)S(1)}, u32[]{:S(2)}, u32[]{:S(2)}) collective-permute-start(s16[128,768]{1,0:T(8,128)(2,1)S(1)} %sum_z1.1), channel_id=1, source_target_pairs={{0,8},{2,10},{4,12},{6,14},{8,0},{10,2},{12,4},{14,6},{16,24},{18,... | collective-permute-start | bytes 589832 | tf_op jit(solution)/shard_map/ppermute | solution.py:190
  (19 other events, 106.4 us)

commit v3 on v2

--- a/solution.py
+++ b/solution.py
@@ -113,29 +113,42 @@
     return lax.optimization_barrier((value, *others))[0]
 
 
-def columns(f_ref, buf, sem, scal_ref, firsts, width):
+def here():
+    me = lax.axis_index("br")
+    return me // 4, me % 4, lax.axis_index("bus")
+
+
+def spot_of(line):
+    _, spot, core = here()
+    return spot ^ {0: 0, "a": 1 + core, "b": 2 - core, 3: 3}[line]
+
+
+def at(index, size):
+    return pl.ds(pl.multiple_of(index * size, size), size)
+
+
+def columns(f_ref, buf, sem, wanted, width):
     copies = []
-    for g, place in enumerate(firsts):
-        start = pl.multiple_of(scal_ref[place] * width, width)
-        copies.append(pltpu.make_async_copy(f_ref.at[:, pl.ds(start, width)], buf.at[g], sem.at[g]))
+    for g, (k, line) in enumerate(wanted):
+        place = (here()[0] ^ k) * 4 + spot_of(line)
+        copies.append(pltpu.make_async_copy(f_ref.at[:, at(place, width)], buf.at[g], sem.at[g]))
         copies[-1].start()
     return copies
 
 
-def forward(factors, shards, blocks, total, name, core=None, us=1.0):
+def forward(factors, shards, wanted, total, name, parted=False, us=1.0):
     rows = factors.shape[0]
     width, scen = factors.shape[1] // (4 * 4), shards[0].shape[1]
-    n, half = len(blocks), rows // 2
+    n, half = len(wanted), rows // 2
     keep = total is not None
     spots = [(i, r) for i, v in enumerate(shards) for r in range(0, v.shape[0], width)]
-    scal = jnp.stack([*blocks, 0 if core is None else core]).astype(jnp.int32)
-
-    def body(scal_ref, f_ref, *refs):
+
+    def body(f_ref, *refs):
         ins, refs = refs[: len(shards)], refs[len(shards) :]
         tot_ref, refs = (refs[0], refs[1:]) if keep else (None, refs)
         outs, (buf, acc, sem) = refs[:-3], refs[-3:]
-        copies = columns(f_ref, buf, sem, scal_ref, range(n), width)
-        dst = outs[0] if core is None else acc
+        copies = columns(f_ref, buf, sem, wanted, width)
+        dst = acc if parted else outs[0]
         for g in range(n):
             copies[g].wait()
             i, r = spots[g]
@@ -144,17 +157,18 @@
                 dst[...] += part
             else:
                 dst[...] = part + tot_ref[...] if keep else part
-        if core is not None:
-            outs[0][...] = acc[pl.ds(pl.multiple_of(scal_ref[n] * half, half), half), :]
-            outs[1][...] = acc[pl.ds(pl.multiple_of((1 - scal_ref[n]) * half, half), half), :]
-
-    ops = [scal, factors, *shards] + ([total] if keep else [])
+        if parted:
+            core = here()[2]
+            outs[0][...] = acc[at(core, half), :]
+            outs[1][...] = acc[at(1 - core, half), :]
+
+    ops = [factors, *shards] + ([total] if keep else [])
     return call(
         body,
-        sds((rows, scen), F32) if core is None else [sds((half, scen), F32)] * 2,
-        [SM, HB] + [VM] * (len(ops) - 2),
+        [sds((half, scen), F32)] * 2 if parted else sds((rows, scen), F32),
+        [HB] + [VM] * (len(ops) - 1),
         name,
-        [pltpu.VMEM((n, rows, width), BF16), pltpu.VMEM((rows if core is not None else 8, scen), F32), DMA((n,))],
+        [pltpu.VMEM((n, rows, width), BF16), pltpu.VMEM((rows if parted else 8, scen), F32), DMA((n,))],
         us=us,
     )(*ops)
 
@@ -174,8 +188,6 @@
     me = lax.axis_index("br")
     core = lax.axis_index("bus")
     zz, spot = me // 4, me % 4
-    first = 1 + core
-    second = 2 - core
 
     chips = [(z, s) for z in range(4) for s in range(4)]
     both = ("br", "bus")
@@ -208,19 +220,18 @@
         a = send_first(planes[k])
         shards[k] = [planes[k], a, send_second(tie(jnp.concatenate([planes[k], a], axis=0), *after))]
 
-    spread(0)
-
-    def block(k, line):
-        return (zz ^ k) * 4 + (spot ^ line)
-
-    lines = [0, first, second, 3]
+    a = send_first(injections)
+    shards[0] = [injections, a, send_second(injections), send_second(a)]
+
+    lines = [0, "a", "b", 3]
 
     other_row = swap(outage_row)
     ext = plane + LANES
 
-    def take_rows(scal_ref, own_ref, other_ref, f_ref, *refs):
+    def take_rows(own_ref, other_ref, f_ref, *refs):
         outs, (buf, picked, sem) = refs[:4], refs[4:]
-        mine = 1 - scal_ref[1]
+        plane_at, _, core = here()
+        mine = 1 - core
         numbers = [own_ref[t] * mine + other_ref[t] * (1 - mine) for t in range(owned)]
         numbers += [own_ref[t] * (1 - mine) + other_ref[t] * mine + half for t in range(owned)]
         copies = []
@@ -243,60 +254,55 @@
             copy.wait()
         picked[...] = jnp.dot(hot.astype(BF16), buf[...], preferred_element_type=F32)
         for k in range(4):
-            start = pl.multiple_of((scal_ref[0] ^ k) * plane, plane)
-            outs[k][:, :plane] = picked[:, pl.ds(start, plane)].astype(BF16)
+            outs[k][:, :plane] = picked[:, at(plane_at ^ k, plane)].astype(BF16)
             outs[k][:, plane:] = mark.astype(BF16)
 
     taken = call(
-        take_rows, [sds((group, ext), BF16)] * 4, [SM, SM, SM, HB], "outage_rows",
+        take_rows, [sds((group, ext), BF16)] * 4, [SM, SM, HB], "outage_rows",
         [pltpu.VMEM((group * 16, cols), BF16), pltpu.VMEM((group, cols), F32), DMA((group,))], us=3,
-    )(jnp.stack([zz, core]).astype(jnp.int32), outage_row, other_row, factors)
-    planes[1] = tie(planes[1], taken[0])
+    )(outage_row, other_row, factors)
+    for k in (3, 2):
+        planes[k] = send(tie(injections, other_row), k)
     taken = [taken[0]] + [send(taken[k], k) for k in (1, 2, 3)]
-    for k in (3, 2):
-        planes[k] = send(tie(injections, taken[0]), k)
-    spread(1)
-    spread(3)
-
-    part = forward(factors, shards[0], [block(0, line) for line in lines], None, "forward_own", us=3.5)
+
+    part = forward(factors, shards[0], [(0, line) for line in lines], None, "forward_own", us=3.5)
     planes[2] = tie(planes[2], part)
-    spread(2)
-
-    scal = jnp.stack([zz, *[spot ^ line for line in lines]]).astype(jnp.int32)
-
-    def outage_part(scal_ref, *refs):
-        rows_in, (own, one, two), (so_ref, po_ref, stack, inj) = refs[:4], refs[4:7], refs[7:]
-        ins = [own[...], one[...], two[:width, :], two[width:, :]]
+    for k in (1, 3, 2):
+        spread(k)
+
+    def outage_part(*refs):
+        rows_in, ins, (so_ref, po_ref, stack, inj) = refs[:4], refs[4:8], refs[8:]
         for k in range(4):
-            stack[pl.ds(pl.multiple_of((scal_ref[0] ^ k) * group, group), group), :] = rows_in[k][...].astype(F32)
-            inj[pl.ds(pl.multiple_of(scal_ref[1 + k] * width, width), width), :] = ins[k]
+            stack[at(here()[0] ^ k, group), :] = rows_in[k][...].astype(F32)
+            inj[at(spot_of(lines[k]), width), :] = ins[k][...]
         so = stack[...].astype(BF16)
         so_ref[...] = so
         po_ref[...] = jnp.dot(so[:, :plane], inj[...], preferred_element_type=F32)
 
     out_factors, outage = call(
-        outage_part, [sds((line_conts, ext), BF16), sds((line_conts, scen), F32)], [SM] + [VM] * 7, "outage_flows",
+        outage_part, [sds((line_conts, ext), BF16), sds((line_conts, scen), F32)], [VM] * 8, "outage_flows",
         [pltpu.VMEM((line_conts, ext), F32), pltpu.VMEM((plane, scen), BF16)],
-    )(tie(scal, part), *taken, *shards[0])
+    )(tie(taken[0], part, planes[2]), *taken[1:], *shards[0])
     outage = outage + send(outage, 1)
+    outage = tie(outage, shards[1][1], shards[3][1])
     outage = outage + send(outage, 2)
-    part = forward(factors, shards[1], [block(1, line) for line in lines], part, "forward_pair", us=3.5)
-    outage = tie(outage, part)
+    outage = tie(outage, shards[2][1], shards[1][2])
     outage = outage + swap(outage)
+    summed = outage
+    outage = tie(outage, shards[3][2])
     outage = jnp.concatenate([outage, send(outage, 0, 1)], axis=0)
-    part = forward(factors, shards[2][:2], [block(2, line) for line in lines[:2]], part, "forward_2a", us=2.9)
+    wanted = [(k, line) for k in (1, 3) for line in lines] + [(2, line) for line in lines[:2]]
+    part = forward(tie(factors, summed), shards[1] + shards[3] + shards[2][:2], wanted, part, "forward_most", us=6)
     outage = tie(outage, part)
     outage = jnp.concatenate([outage, send(outage, 0, 2)], axis=0)
     owner = entry_owner[:, 0]
     contingency = jnp.bitwise_xor(owner % 4, spot) * line_conts + (owner // 4) * group + entry_slot
 
-    part = forward(factors, shards[3], [block(3, line) for line in lines], part, "forward_3", us=4)
-    mine, theirs = forward(factors, shards[2][2:], [block(2, line) for line in lines[2:]], part, "forward_2b", core, us=2.9)
+    wanted = [(2, line) for line in lines[2:]]
+    mine, theirs = forward(factors, shards[2][2:], wanted, part, "forward_last", True, us=2.4)
     theirs = swap(theirs)
 
-    scal = jnp.concatenate([jnp.stack([zz * group + core * owned]), outage_row]).astype(jnp.int32)
-
-    def middle(scal_ref, mine_ref, theirs_ref, out_ref, lim_ref, er_ref, ert_ref, ct_ref, ctt_ref, f_ref, limr_ref,
+    def middle(row_ref, mine_ref, theirs_ref, out_ref, lim_ref, er_ref, ert_ref, ct_ref, ctt_ref, f_ref, limr_ref,
                adj_ref, every_t_ref, every_ref, total):
         flows = mine_ref[...] + theirs_ref[...]
         hit = er_ref[...] == lax.broadcasted_iota(jnp.int32, (pairs, half), 1)
@@ -313,11 +319,11 @@
         place = lax.broadcasted_iota(jnp.int32, (half, scen), 0)
         out = place < 0
         for t in range(owned):
-            r = scal_ref[1 + t]
+            r = row_ref[t]
             fresh = 1.0
             for u in range(t):
-                fresh = fresh * jnp.where(scal_ref[1 + u] == r, 0.0, 1.0)
-            own = pl.ds(scal_ref[0] + t, 1)
+                fresh = fresh * jnp.where(row_ref[u] == r, 0.0, 1.0)
+            own = pl.ds(here()[0] * group + here()[2] * owned + t, 1)
             every_ref[own, :] = every_ref[own, :] + fresh * total[pl.ds(r, 1), :]
             out = out | (place == r)
         adj_ref[...] = jnp.where(out, 0.0, summed).T.astype(BF16)
@@ -327,7 +333,7 @@
         middle, [sds((scen, half), BF16), sds((scen, conts), F32)], [SM] + [VM] * 10, "penalty",
         [pltpu.VMEM((conts, scen), F32), pltpu.VMEM((half, scen), F32)],
     )(
-        scal, mine, theirs, outage, limits[:, None], entry_row[:, None], entry_row[None, :],
+        outage_row, mine, theirs, outage, limits[:, None], entry_row[:, None], entry_row[None, :],
         contingency[:, None], contingency[None, :], outage_factor[:, None], limits[None, :],
     )
     other_t = swap(adj_t)
@@ -340,14 +346,13 @@
     def backward(name, adj, messages, plain, us=3.0, fine=None):
         wanted = [b for m in messages for b in m] + plain
         n = len(wanted)
-        scal = jnp.stack([core, *[block(k, line) for k, line in wanted]]).astype(jnp.int32)
-
-        def body(scal_ref, f_ref, a_ref, b_ref, *refs):
+
+        def body(f_ref, a_ref, b_ref, *refs):
             outs, (buf, adj, sem) = refs[:-3], refs[-3:]
             more, outs = (outs[0][...], outs[1:]) if fine is not None else (None, outs)
-            copies = columns(f_ref, buf, sem, scal_ref, range(1, n + 1), width)
-            adj[:, pl.ds(pl.multiple_of(scal_ref[0] * half, half), half)] = a_ref[...]
-            adj[:, pl.ds(pl.multiple_of((1 - scal_ref[0]) * half, half), half)] = b_ref[...]
+            copies = columns(f_ref, buf, sem, wanted, width)
+            adj[:, at(here()[2], half)] = a_ref[...]
+            adj[:, at(1 - here()[2], half)] = b_ref[...]
 
             def grad(g):
                 copies[g].wait()
@@ -363,10 +368,10 @@
 
         return call(
             body, [message(len(m), fine is not None) for m in messages] + [grad_block] * len(plain),
-            [SM, HB] + [VM] * (2 if fine is None else 3), name,
+            [HB] + [VM] * (2 if fine is None else 3), name,
             [pltpu.VMEM((n, rows, width), BF16), pltpu.VMEM((scen, rows), BF16), DMA((n,))],
             us=us,
-        )(scal, factors, *adj, *([] if fine is None else [fine]))
+        )(factors, *adj, *([] if fine is None else [fine]))
 
     def add(name, *terms):
         flat = [t[0] if isinstance(t, tuple) else t for t in terms]
@@ -380,52 +385,54 @@
 
         return call(body, message(1), [VM] * len(flat), name, us=0.01)(*flat)
 
-    def shifted(v, core_ref, on_0, on_1):
+    def shifted(v, on_0, on_1):
         return jnp.where(
-            jnp.full(v.shape, core_ref[0]) == 0,
+            jnp.full(v.shape, here()[2]) == 0,
             pltpu.roll(v, LANES - on_0 * line_conts, 1),
             pltpu.roll(v, LANES - on_1 * line_conts, 1),
         )
 
-    def sum_3(core_ref, p_ref, a_ref, e_ref, b_ref, t_ref):
-        t_ref[...] = e_ref[...] + shifted(get_fine(a_ref), core_ref, 1, 2)
+    def sum_3(p_ref, a_ref, e_ref, b_ref, t_ref):
+        t_ref[...] = e_ref[...] + shifted(get_fine(a_ref), 1, 2)
         put_coded(b_ref, [p_ref[...] + get_coded(a_ref, 0, width)], t_ref[...])
 
-    def sum_z3(core_ref, p_ref, a_ref, b_ref, t_ref, z_ref, e_ref):
-        e_ref[...] = (t_ref[...] + shifted(get_fine(b_ref), core_ref, 2, 1)).T[:line_conts, :]
+    def sum_z3(p_ref, a_ref, b_ref, t_ref, z_ref, e_ref):
+        e_ref[...] = (t_ref[...] + shifted(get_fine(b_ref), 2, 1)).T[:line_conts, :]
         put_coded(z_ref, [p_ref[...] + get_coded(a_ref, 1, width) + get_coded(b_ref, 0, width)])
 
-    core_1 = core[None].astype(jnp.int32)
     adj = (adj_t, other_t)
-    (a3,) = backward("backward_3a", adj, [[(3, 3), (3, first)]], [], us=2.6, fine=every)
+    (a3,) = backward("backward_3a", adj, [[(3, 3), (3, "a")]], [], us=2.6, fine=every)
     a3_got = send_first(a3)
     adj = (tie(adj_t, a3), other_t)
-    a2, p3s, p3 = backward("backward_3b", adj, [[(2, 3), (2, first)]], [(3, second), (3, 0)], us=3.3)
+    a2, p3s, p3 = backward("backward_3b", adj, [[(2, 3), (2, "a")]], [(3, "b"), (3, 0)], us=3.3)
     a2_got = send_first(a2)
     b3, every = call(
-        sum_3, [message(1, True), sds((scen, conts), F32)], [SM] + [VM] * 3, "sum_3", us=0.3
-    )(core_1, tie(p3s, a2), a3_got, every)
+        sum_3, [message(1, True), sds((scen, conts), F32)], [VM] * 3, "sum_3", us=0.3
+    )(tie(p3s, a2), a3_got, every)
     b3_got = send_second(b3)
     adj = (tie(adj_t, b3), other_t)
-    a1, p2s, p2 = backward("backward_2", adj, [[(1, 3), (1, first)]], [(2, second), (2, 0)], us=3.5)
+    wanted = [(2, "b"), (2, 0), (1, "b"), (1, 0)]
+    a1, p2s, p2, p1s, p1 = backward("backward_2", adj, [[(1, 3), (1, "a")]], wanted, us=3.5)
     a1_got = send_first(a1)
     z3, every = call(
-        sum_z3, [message(1), sds((line_conts, scen), F32)], [SM] + [VM] * 4, "sum_z3", us=0.3
-    )(core_1, tie(p3, a1), a3_got, b3_got, every)
+        sum_z3, [message(1), sds((line_conts, scen), F32)], [VM] * 4, "sum_z3", us=0.3
+    )(tie(p3, a1), a3_got, b3_got, every)
     every = every + send(every, 1) + send(every, 2) + send(every, 3)
     every = every + swap(every)
     z3_got = send(z3, 3)
     b2 = add("sum_2", tie(p2s, z3), (a2_got, 0))
     b2_got = send_second(b2)
-
-    adj = (tie(adj_t, b2), other_t)
-    p1s, p1, p0d, p0f, p0s, p0 = backward("backward_0", adj, [], [(1, second), (1, 0), (0, 3), (0, first), (0, second), (0, 0)], us=0.01)
-    scal = jnp.stack([spot ^ line for line in lines]).astype(jnp.int32)
-
-    def outaged(scal_ref, e_ref, so_ref, p0_ref, ps_ref, pd_ref, pf_ref, a_ref, s_ref, o_ref, whole):
+    b1 = add("sum_1", tie(p1s, b2), (a1_got, 0))
+    b1_got = send_second(b1)
+
+
+    def outaged(f_ref, a_ref, b_ref, e_ref, so_ref, out_ref, s_ref, o_ref, buf, adj, more, sem):
+        copies = columns(f_ref, buf, sem, [(0, line) for line in (3, "a", "b", 0)], width)
+        adj[:, at(here()[2], half)] = a_ref[...]
+        adj[:, at(1 - here()[2], half)] = b_ref[...]
         marks = so_ref[:, plane:].astype(F32)
-        number = marks[:, :1] * 16.0 + marks[:, 1:2]
-        wide = jnp.broadcast_to(number, (line_conts, LANES))
+        row = marks[:, :1] * 16.0 + marks[:, 1:2]
+        wide = jnp.broadcast_to(row, (line_conts, LANES))
         across = jnp.concatenate([wide] * (LANES // line_conts), axis=0).T[:line_conts, :line_conts]
         one = lax.broadcasted_iota(jnp.int32, (line_conts, line_conts), 0)
         two = lax.broadcasted_iota(jnp.int32, (line_conts, line_conts), 1)
@@ -433,33 +440,33 @@
         earlier = jnp.sum(jnp.where(same & (two < one), 1.0, 0.0), axis=1, keepdims=True)
         merged = pick(one_hot(same), e_ref[...])
         final = jnp.where(earlier > 0.0, 0.0, merged).astype(BF16)
-        whole[...] = lax.dot_general(final, so_ref[:, :plane], (((0,), (0,)), ((), ())), preferred_element_type=F32)
-
-        def of(g):
-            return whole[:, pl.ds(pl.multiple_of(scal_ref[g] * width, width), width)]
-
-        put_coded(a_ref, [pd_ref[...] + of(3), pf_ref[...] + of(1)])
-        s_ref[...] = ps_ref[...] + of(2)
-        o_ref[...] = p0_ref[...] + of(0)
+        more[...] = lax.dot_general(final, so_ref[:, :plane], (((0,), (0,)), ((), ())), preferred_element_type=F32)
+
+        def grad(g, line):
+            copies[g].wait()
+            return jnp.dot(adj[...], buf[g], preferred_element_type=F32) + more[:, at(spot_of(line), width)]
+
+        put_coded(out_ref, [grad(0, 3), grad(1, "a")])
+        s_ref[...] = grad(2, "b")
+        o_ref[...] = grad(3, 0)
 
     a0, p0s, p0 = call(
-        outaged, [message(2), grad_block, grad_block], [SM] + [VM] * 6, "outaged_rows", [pltpu.VMEM((scen, plane), F32)], us=0.01
-    )(scal, every, out_factors, p0, p0s, p0d, p0f)
+        outaged, [message(2), grad_block, grad_block], [HB] + [VM] * 4, "backward_0",
+        [pltpu.VMEM((4, rows, width), BF16), pltpu.VMEM((scen, rows), BF16), pltpu.VMEM((scen, plane), F32), DMA((4,))],
+        us=0.01,
+    )(factors, tie(adj_t, b1), other_t, every, out_factors)
     a0_got = send_first(a0)
-    z2 = add("sum_z2", tie(p2, a0), (a2_got, 1), (b2_got, 0))
-    z2_got = send(z2, 2)
-    b1 = add("sum_1", tie(p1s, z2), (a1_got, 0))
-    b1_got = send_second(b1)
-
     def gather(p_ref, z3_ref, out_ref):
         out_ref[...] = p_ref[...] + get_coded(z3_ref, 0, width)
 
-    p0 = call(gather, grad_block, [VM] * 2, "gradient_z", us=12)(tie(p0, b1), z3_got)
-    b0 = add("sum_0", tie(p0s, b1, p0), (a0_got, 0))
+    p0 = call(gather, grad_block, [VM] * 2, "gradient_z", us=12)(tie(p0, a0), z3_got)
+    z2 = add("sum_z2", tie(p2, p0), (a2_got, 1), (b2_got, 0))
+    z2_got = send(z2, 2)
+    z1 = add("sum_z1", tie(p1, z2), (a1_got, 1), (b1_got, 0))
+    z1_got = send(z1, 1)
+
+    b0 = add("sum_0", tie(p0s, z1), (a0_got, 0))
     b0_got = send_second(b0)
-    z1 = add("sum_z1", tie(p1, b0), (a1_got, 1), (b1_got, 0))
-    z1_got = send(z1, 1)
-
     def last(p_ref, a_ref, b_ref, z1_ref, z2_ref, out_ref):
         total = p_ref[...] + get_coded(a_ref, 1, width)
         for ref in (b_ref, z2_ref, z1_ref):

time: 113 us -> 106 us (0.938)
  Pallas kernels: 41.1 us -> 32.3 us
  starting transfers between devices: 41.5 us -> 43.5 us
  other arithmetic: 1.3 us -> 0.12 us
    pallas_call x4 -> x3, Pallas kernels: 13.4 us -> 8.62 us  [backward(): call(body, [message(len(m), fine is not None) for m in messages] + [grad_...]
    pallas_call x10 -> x8, Pallas kernels: 23 us -> 19.4 us  [the longest x3 12.7 us: forward(): call(body, [sds((half, scen), F32)] * 2 if parted else sds((rows, scen),...]
    ppermute x16, starting transfers between devices: 24.2 us -> 26.6 us  [send(): return lax.ppermute(v, 'br', to(dz, ds))]
    ppermute x8, waiting for transfers between devices: 8.9 us -> 7.15 us  [send_first(): return lax.ppermute(v, both, split((1, 2)))]
    ppermute x8, starting transfers between devices: 9.04 us -> 7.32 us  [send_first(): return lax.ppermute(v, both, split((1, 2)))]
    ppermute x8 -> x9, starting transfers between devices: 7.84 us -> 9.18 us  [send_second(): return lax.ppermute(v, both, split((2, 1)))]
    ppermute x8 -> x9, waiting for transfers between devices: 3.59 us -> 4.66 us  [send_second(): return lax.ppermute(v, both, split((2, 1)))]
  transfers between devices with their start and end apart: 37 -> 38, of which waited for: 12 -> 15; matrix products, arithmetic and copies ran while one was open for 2% -> 1% of each run, Pallas kernels for 32% -> 26%
where the time goes in v3:
time: 106 us; the launch traced here: 105 us
  starting transfers between devices  43.5 us (41%)
  Pallas kernels  32.3 us (30%)
  waiting for transfers between devices  27.8 us (26%)
  local copies, waits for them, and re-layouts  1.24 us (1%)
    ppermute x16, starting transfers between devices, send(): return lax.ppermute(v, 'br', to(dz, ds))  26.6 us
    ppermute x16, waiting for transfers between devices, send(): return lax.ppermute(v, 'br', to(dz, ds))  12.8 us
    pallas_call x3, Pallas kernels, forward(): call(body, [sds((half, scen), F32)] * 2 if parted else sds((rows, scen),...  12.7 us
    ppermute x9, starting transfers between devices, send_second(): return lax.ppermute(v, both, split((2, 1)))  9.18 us
    pallas_call x3, Pallas kernels, backward(): call(body, [message(len(m), fine is not None) for m in messages] + [grad_...  8.62 us
    ppermute x8, starting transfers between devices, send_first(): return lax.ppermute(v, both, split((1, 2)))  7.32 us
    ppermute x8, waiting for transfers between devices, send_first(): return lax.ppermute(v, both, split((1, 2)))  7.15 us
    ppermute x9, waiting for transfers between devices, send_second(): return lax.ppermute(v, both, split((2, 1)))  4.66 us
  transfers between devices with their start and end apart: 38, of which 15 were waited for; matrix products, arithmetic and copies ran while one was open for 1% of the time, Pallas kernels for 26%

profile of v3, /device:TPU:0, one launch (start us, length us, event | category | flops | bytes accessed | tf_op | source)
XLA Modules:
  0.0 105.3 jit_solution(14493715682732019791)
XLA Ops:
  0.0 3.0 %collective-permute-start.11 = (bf16[640,128]{1,0:T(8,128)(2,1)}, bf16[640,128]{1,0:T(8,128)(2,1)S(1)}, u32[]{:S(2)}, u32[]{:S(2)}) collective-permute-start(bf16[640,128]{1,0:T(8,128)(2,1)} %refs_4_.1), channel_id=1, source_target_pairs={{0,8},{2,10},{4,12},{6,14},{8,0},{10,2},{12,4},{14,6},{16,24},{18,... | collective-permute-start | bytes 491528 | tf_op jit(solution)/shard_map/ppermute | solution.py:202
  7.3 2.5 %collective-permute-start.13 = (bf16[640,128]{1,0:T(8,128)(2,1)}, bf16[640,128]{1,0:T(8,128)(2,1)S(1)}, u32[]{:S(2)}, u32[]{:S(2)}) collective-permute-start(bf16[640,128]{1,0:T(8,128)(2,1)} %refs_4_.1), channel_id=1, source_target_pairs={{0,24},{2,26},{4,28},{6,30},{8,16},{10,18},{12,20},{14,22},{16,8},... | collective-permute-start | bytes 491528 | tf_op jit(solution)/shard_map/ppermute | solution.py:202
  11.1 2.8 %outage_rows.1 = (bf16[8,2688]{1,0:T(8,128)(2,1)S(1)}, bf16[8,2688]{1,0:T(8,128)(2,1)S(1)}, bf16[8,2688]{1,0:T(8,128)(2,1)S(1)}, bf16[8,2688]{1,0:T(8,128)(2,1)S(1)}) custom-call(s32[4]{0:T(128)S(1)} %copy-done.2, s32[4]{0:T(128)S(1)} %collective-permute-done.other_ref, bf16[768,10240]{1,0:T(8,128)(2,1)} %f_ref.14), custom_call_target="tpu_custom_call" | custom-call | flops 3449999872 | bytes 1 | tf_op jit(solution)/shard_map/outage_rows/pallas_call | solution.py:260
  13.9 1.9 %collective-permute-start.7 = (bf16[8,2688]{1,0:T(8,128)(2,1)S(1)}, bf16[8,2688]{1,0:T(8,128)(2,1)S(1)}, u32[]{:S(2)}, u32[]{:S(2)}) collective-permute-start(bf16[8,2688]{1,0:T(8,128)(2,1)S(1)} %get-tuple-element.53), channel_id=1, source_target_pairs={{0,8},{2,10},{4,12},{6,14},{8,0},{10,2},{12,4},{14,6},{16,24},{18,... | collective-permute-start | bytes 129032 | tf_op jit(solution)/shard_map/ppermute | solution.py:202
  16.3 2.3 %collective-permute-start.8 = (bf16[8,2688]{1,0:T(8,128)(2,1)S(1)}, bf16[8,2688]{1,0:T(8,128)(2,1)S(1)}, u32[]{:S(2)}, u32[]{:S(2)}) collective-permute-start(bf16[8,2688]{1,0:T(8,128)(2,1)S(1)} %get-tuple-element.54), channel_id=1, source_target_pairs={{0,16},{2,18},{4,20},{6,22},{8,24},{10,26},{12,28},{14,30},{16,0},... | collective-permute-start | bytes 129032 | tf_op jit(solution)/shard_map/ppermute | solution.py:202
  19.5 3.1 %collective-permute-done.4.refs_3_.refs_7_ = bf16[640,128]{1,0:T(8,128)(2,1)S(1)} collective-permute-done((bf16[640,128]{1,0:T(8,128)(2,1)S(1)}, bf16[640,128]{1,0:T(8,128)(2,1)S(1)}, u32[]{:S(2)}, u32[]{:S(2)}) %collective-permute-start.4) | collective-permute-done | bytes 163872 | tf_op jit(solution)/shard_map/ppermute | solution.py:211
  22.7 3.5 %forward_own.1.refs_8_ = f32[768,128]{1,0:T(8,128)S(1)} custom-call(bf16[768,10240]{1,0:T(8,128)(2,1)} %f_ref.14, bf16[640,128]{1,0:T(8,128)(2,1)S(1)} %copy-done, bf16[640,128]{1,0:T(8,128)(2,1)S(1)} %collective-permute-done.2.refs_1_.refs_5_, bf16[640,128]{1,0:T(8,128)(2,1)S(1)} %collective-permute-done.3.refs_2_.refs_6_, ...), custom_call_target="tpu_custom_call" | custom-call | flops 4024999936 | bytes 1 | tf_op jit(solution)/shard_map/forward_own/pallas_call | solution.py:166
  26.5 2.7 %collective-permute-start.9 = (bf16[8,2688]{1,0:T(8,128)(2,1)S(1)}, bf16[8,2688]{1,0:T(8,128)(2,1)S(1)}, u32[]{:S(2)}, u32[]{:S(2)}) collective-permute-start(bf16[8,2688]{1,0:T(8,128)(2,1)S(1)} %get-tuple-element.55), channel_id=1, source_target_pairs={{0,24},{2,26},{4,28},{6,30},{8,16},{10,18},{12,20},{14,22},{16,8},... | collective-permute-start | bytes 129032 | tf_op jit(solution)/shard_map/ppermute | solution.py:202
  33.7 2.7 %collective-permute-done.10 = f32[32,128]{1,0:T(8,128)S(1)} collective-permute-done((f32[32,128]{1,0:T(8,128)S(1)}, f32[32,128]{1,0:T(8,128)S(1)}, u32[]{:S(2)}, u32[]{:S(2)}) %collective-permute-start.10) | collective-permute-done | bytes 16416 | tf_op jit(solution)/shard_map/ppermute | solution.py:202
  37.8 3.2 %collective-permute-done.15 = f32[32,128]{1,0:T(8,128)S(1)} collective-permute-done((f32[32,128]{1,0:T(8,128)S(1)}, f32[32,128]{1,0:T(8,128)S(1)}, u32[]{:S(2)}, u32[]{:S(2)}) %collective-permute-start.15) | collective-permute-done | bytes 16416 | tf_op jit(solution)/shard_map/ppermute | solution.py:202
  41.2 1.8 %collective-permute-start.6 = (bf16[1280,128]{1,0:T(8,128)(2,1)S(1)}, bf16[1280,128]{1,0:T(8,128)(2,1)S(1)}, u32[]{:S(2)}, u32[]{:S(2)}) collective-permute-start(bf16[1280,128]{1,0:T(8,128)(2,1)S(1)} %pad_maximum_fusion), channel_id=1, source_target_pairs={{0,4},{2,6},{4,0},{6,2},{8,12},{10,14},{12,8},{14,10},{16,20},{18,... | collective-permute-start | bytes 983048 | tf_op jit(solution)/shard_map/ppermute | solution.py:211
  44.6 6.9 %forward_most.1.refs_1_ = f32[768,128]{1,0:T(8,128)S(1)} custom-call(bf16[768,10240]{1,0:T(8,128)(2,1)} %f_ref.14, bf16[640,128]{1,0:T(8,128)(2,1)S(1)} %collective-permute-done.11.refs_0_, bf16[640,128]{1,0:T(8,128)(2,1)S(1)} %collective-permute-done.12.refs_1_, bf16[1280,128]{1,0:T(8,128)(2,1)S(1)} %collective-permute-done.16.refs_2_, ...), custom_call_target="tpu_custom_call" | custom-call | flops 6899999744 | bytes 1 | tf_op jit(solution)/shard_map/forward_most/pallas_call | solution.py:166
  52.7 2.4 %forward_last.1 = (f32[384,128]{1,0:T(8,128)S(1)}, f32[384,128]{1,0:T(8,128)S(1)}) custom-call(bf16[768,10240]{1,0:T(8,128)(2,1)} %f_ref.14, bf16[1280,128]{1,0:T(8,128)(2,1)S(1)} %collective-permute-done.6.refs_0_, f32[768,128]{1,0:T(8,128)S(1)} %forward_most.1.refs_1_), custom_call_target="tpu_custom_call" | custom-call | flops 2760000000 | bytes 1 | tf_op jit(solution)/shard_map/forward_last/pallas_call | solution.py:166
  56.6 1.7 %penalty.1 = (bf16[128,384]{1,0:T(8,128)(2,1)S(1)}, f32[128,128]{1,0:T(8,128)S(1)}) custom-call(s32[4]{0:T(128)S(1)} %copy-done.3, f32[384,128]{1,0:T(8,128)S(1)} %get-tuple-element.60.mine_ref, f32[384,128]{1,0:T(8,128)S(1)} %collective-permute-done.19.theirs_ref, f32[128,128]{1,0:T(8,128)S(1)} %pad_maximum_fusion.3.out_ref, ...), custom_call_target="tpu_custom_call" | custom-call | flops 575000000 | bytes 1 | tf_op jit(solution)/shard_map/penalty/pallas_call | solution.py:332
  59.7 2.1 %backward_3a.1 = s16[128,1664]{1,0:T(8,128)(2,1)S(1)} custom-call(bf16[768,10240]{1,0:T(8,128)(2,1)} %f_ref.14, bf16[128,384]{1,0:T(8,128)(2,1)S(1)} %get-tuple-element.81.a_ref, bf16[128,384]{1,0:T(8,128)(2,1)S(1)} %collective-permute-done.22.b_ref, f32[128,128]{1,0:T(8,128)S(1)} %get-tuple-element.65.refs_0_.e_ref), custom_call_target="tpu_custom_call" | custom-call | flops 2990000128 | bytes 1 | tf_op jit(solution)/shard_map/backward_3a/pallas_call | solution.py:369
  62.5 2.8 %backward_3b.1 = (s16[128,1408]{1,0:T(8,128)(2,1)S(1)}, f32[128,640]{1,0:T(8,128)S(1)}, f32[128,640]{1,0:T(8,128)S(1)}) custom-call(bf16[768,10240]{1,0:T(8,128)(2,1)} %f_ref.14, bf16[128,384]{1,0:T(8,128)(2,1)S(1)} %get-tuple-element.81.a_ref, bf16[128,384]{1,0:T(8,128)(2,1)S(1)} %collective-permute-done.22.b_ref), custom_call_target="tpu_custom_call" | custom-call | flops 3795000064 | bytes 1 | tf_op jit(solution)/shard_map/backward_3b/pallas_call | solution.py:369
  66.8 3.2 %collective-permute-done.23.a_ref = s16[128,1664]{1,0:T(8,128)(2,1)S(1)} collective-permute-done((s16[128,1664]{1,0:T(8,128)(2,1)S(1)}, s16[128,1664]{1,0:T(8,128)(2,1)S(1)}, u32[]{:S(2)}, u32[]{:S(2)}) %collective-permute-start.23) | collective-permute-done | bytes 426016 | tf_op jit(solution)/shard_map/ppermute | solution.py:208
  71.3 3.7 %backward_2.1 = (s16[128,1408]{1,0:T(8,128)(2,1)S(1)}, f32[128,640]{1,0:T(8,128)S(1)}, f32[128,640]{1,0:T(8,128)S(1)}, f32[128,640]{1,0:T(8,128)S(1)}, f32[128,640]{1,0:T(8,128)S(1)}) custom-call(bf16[768,10240]{1,0:T(8,128)(2,1)} %f_ref.14, bf16[128,384]{1,0:T(8,128)(2,1)S(1)} %get-tuple-element.81.a_ref, bf16[128,384]{1,0:T(8,128)(2,1)S(1)} %collective-permute-done.22.b_ref), custom_call_target="tpu_custom_call" | custom-call | flops 4024999936 | bytes 1 | tf_op jit(solution)/shard_map/backward_2/pallas_call | solution.py:369
  77.4 2.0 %collective-permute-start.29 = (f32[32,128]{1,0:T(8,128)S(1)}, f32[32,128]{1,0:T(8,128)S(1)}, u32[]{:S(2)}, u32[]{:S(2)}) collective-permute-start(f32[32,128]{1,0:T(8,128)S(1)} %get-tuple-element.82), channel_id=1, source_target_pairs={{0,24},{2,26},{4,28},{6,30},{8,16},{10,18},{12,20},{14,22},{16,8},... | collective-permute-start | bytes 49160 | tf_op jit(solution)/shard_map/ppermute | solution.py:202
  79.4 2.5 %collective-permute-start.27 = (f32[32,128]{1,0:T(8,128)S(1)}, f32[32,128]{1,0:T(8,128)S(1)}, u32[]{:S(2)}, u32[]{:S(2)}) collective-permute-start(f32[32,128]{1,0:T(8,128)S(1)} %get-tuple-element.82), channel_id=1, source_target_pairs={{0,8},{2,10},{4,12},{6,14},{8,0},{10,2},{12,4},{14,6},{16,24},{18,... | collective-permute-start | bytes 49160 | tf_op jit(solution)/shard_map/ppermute | solution.py:202
  83.0 1.9 %collective-permute-start.31 = (s16[128,768]{1,0:T(8,128)(2,1)S(1)}, s16[128,768]{1,0:T(8,128)(2,1)S(1)}, u32[]{:S(2)}, u32[]{:S(2)}) collective-permute-start(s16[128,768]{1,0:T(8,128)(2,1)S(1)} %get-tuple-element.78), channel_id=1, source_target_pairs={{0,24},{2,26},{4,28},{6,30},{8,16},{10,18},{12,20},{14,22},{16,8},... | collective-permute-start | bytes 589832 | tf_op jit(solution)/shard_map/ppermute | solution.py:202
  87.7 3.1 %backward_0.1 = (s16[128,1408]{1,0:T(8,128)(2,1)S(1)}, f32[128,640]{1,0:T(8,128)S(1)}, f32[128,640]{1,0:T(8,128)S(1)}) custom-call(bf16[768,10240]{1,0:T(8,128)(2,1)} %f_ref.14, bf16[128,384]{1,0:T(8,128)(2,1)S(1)} %get-tuple-element.81.a_ref, bf16[128,384]{1,0:T(8,128)(2,1)S(1)} %collective-permute-done.22.b_ref, f32[32,128]{1,0:T(8,128)S(1)} %add.48.e_ref, ...), custom_call_target="tpu_custom_call" | custom-call | flops 11500000 | bytes 1 | tf_op jit(solution)/shard_map/backward_0/pallas_call | solution.py:453
  94.4 3.9 %collective-permute-done.32.refs_1_.a_ref = s16[128,1408]{1,0:T(8,128)(2,1)S(1)} collective-permute-done((s16[128,1408]{1,0:T(8,128)(2,1)S(1)}, s16[128,1408]{1,0:T(8,128)(2,1)S(1)}, u32[]{:S(2)}, u32[]{:S(2)}) %collective-permute-start.32) | collective-permute-done | bytes 360480 | tf_op jit(solution)/shard_map/ppermute | solution.py:208
  99.6 4.4 %collective-permute-done.37.z2_ref = s16[128,768]{1,0:T(8,128)(2,1)S(1)} collective-permute-done((s16[128,768]{1,0:T(8,128)(2,1)S(1)}, s16[128,768]{1,0:T(8,128)(2,1)S(1)}, u32[]{:S(2)}, u32[]{:S(2)}) %collective-permute-start.37) | collective-permute-done | bytes 196640 | tf_op jit(solution)/shard_map/ppermute | solution.py:202
  (103 shorter events, 34.8 us)
Async XLA Ops:
  0.0 9.9 %collective-permute-start.11 = (bf16[640,128]{1,0:T(8,128)(2,1)}, bf16[640,128]{1,0:T(8,128)(2,1)S(1)}, u32[]{:S(2)}, u32[]{:S(2)}) collective-permute-start(bf16[640,128]{1,0:T(8,128)(2,1)} %refs_4_.1), channel_id=1, source_target_pairs={{0,8},{2,10},{4,12},{6,14},{8,0},{10,2},{12,4},{14,6},{16,24},{18,... | collective-permute-start | bytes 491528 | tf_op jit(solution)/shard_map/ppermute | solution.py:202
  3.0 13.3 %collective-permute-start.3 = (bf16[640,128]{1,0:T(8,128)(2,1)}, bf16[640,128]{1,0:T(8,128)(2,1)S(1)}, u32[]{:S(2)}, u32[]{:S(2)}) collective-permute-start(bf16[640,128]{1,0:T(8,128)(2,1)} %refs_4_.1), channel_id=1, source_target_pairs={{0,4},{2,6},{4,0},{6,2},{8,12},{10,14},{12,8},{14,10},{16,20},{18,... | collective-permute-start | bytes 491528 | tf_op jit(solution)/shard_map/ppermute | solution.py:211
  4.5 9.3 %collective-permute-start.2 = (bf16[640,128]{1,0:T(8,128)(2,1)}, bf16[640,128]{1,0:T(8,128)(2,1)S(1)}, u32[]{:S(2)}, u32[]{:S(2)}) collective-permute-start(bf16[640,128]{1,0:T(8,128)(2,1)} %refs_4_.1), channel_id=1, source_target_pairs={{0,2},{2,0},{4,6},{6,4},{8,10},{10,8},{12,14},{14,12},{16,18},{18,... | collective-permute-start | bytes 491528 | tf_op jit(solution)/shard_map/ppermute | solution.py:208
  7.3 11.3 %collective-permute-start.13 = (bf16[640,128]{1,0:T(8,128)(2,1)}, bf16[640,128]{1,0:T(8,128)(2,1)S(1)}, u32[]{:S(2)}, u32[]{:S(2)}) collective-permute-start(bf16[640,128]{1,0:T(8,128)(2,1)} %refs_4_.1), channel_id=1, source_target_pairs={{0,24},{2,26},{4,28},{6,30},{8,16},{10,18},{12,20},{14,22},{16,8},... | collective-permute-start | bytes 491528 | tf_op jit(solution)/shard_map/ppermute | solution.py:202
  9.8 16.7 %collective-permute-start.1 = (bf16[640,128]{1,0:T(8,128)(2,1)}, bf16[640,128]{1,0:T(8,128)(2,1)S(1)}, u32[]{:S(2)}, u32[]{:S(2)}) collective-permute-start(bf16[640,128]{1,0:T(8,128)(2,1)} %refs_4_.1), channel_id=1, source_target_pairs={{0,16},{2,18},{4,20},{6,22},{8,24},{10,26},{12,28},{14,30},{16,0},... | collective-permute-start | bytes 491528 | tf_op jit(solution)/shard_map/ppermute | solution.py:202
  13.9 16.6 %collective-permute-start.7 = (bf16[8,2688]{1,0:T(8,128)(2,1)S(1)}, bf16[8,2688]{1,0:T(8,128)(2,1)S(1)}, u32[]{:S(2)}, u32[]{:S(2)}) collective-permute-start(bf16[8,2688]{1,0:T(8,128)(2,1)S(1)} %get-tuple-element.53), channel_id=1, source_target_pairs={{0,8},{2,10},{4,12},{6,14},{8,0},{10,2},{12,4},{14,6},{16,24},{18,... | collective-permute-start | bytes 129032 | tf_op jit(solution)/shard_map/ppermute | solution.py:202
  15.8 6.9 %collective-permute-start.4 = (bf16[640,128]{1,0:T(8,128)(2,1)S(1)}, bf16[640,128]{1,0:T(8,128)(2,1)S(1)}, u32[]{:S(2)}, u32[]{:S(2)}) collective-permute-start(bf16[640,128]{1,0:T(8,128)(2,1)S(1)} %collective-permute-done.2.refs_1_.refs_5_), channel_id=1, source_target_pairs={{0,4},{2,6},{4,0},{6,2},{8,12},{10,14},{12,8},{14,10},{16,20},{18,... | collective-permute-start | bytes 491528 | tf_op jit(solution)/shard_map/ppermute | solution.py:211
  16.3 15.2 %collective-permute-start.8 = (bf16[8,2688]{1,0:T(8,128)(2,1)S(1)}, bf16[8,2688]{1,0:T(8,128)(2,1)S(1)}, u32[]{:S(2)}, u32[]{:S(2)}) collective-permute-start(bf16[8,2688]{1,0:T(8,128)(2,1)S(1)} %get-tuple-element.54), channel_id=1, source_target_pairs={{0,16},{2,18},{4,20},{6,22},{8,24},{10,26},{12,28},{14,30},{16,0},... | collective-permute-start | bytes 129032 | tf_op jit(solution)/shard_map/ppermute | solution.py:202
  18.6 10.6 %collective-permute-start.14 = (bf16[640,128]{1,0:T(8,128)(2,1)S(1)}, bf16[640,128]{1,0:T(8,128)(2,1)S(1)}, u32[]{:S(2)}, u32[]{:S(2)}) collective-permute-start(bf16[640,128]{1,0:T(8,128)(2,1)S(1)} %collective-permute-done.13.refs_3_), channel_id=1, source_target_pairs={{0,2},{2,0},{4,6},{6,4},{8,10},{10,8},{12,14},{14,12},{16,18},{18,... | collective-permute-start | bytes 491528 | tf_op jit(solution)/shard_map/ppermute | solution.py:208
  22.7 18.4 %collective-permute-start.16 = (bf16[1280,128]{1,0:T(8,128)(2,1)S(1)}, bf16[1280,128]{1,0:T(8,128)(2,1)S(1)}, u32[]{:S(2)}, u32[]{:S(2)}) collective-permute-start(bf16[1280,128]{1,0:T(8,128)(2,1)S(1)} %pad_maximum_fusion.1), channel_id=1, source_target_pairs={{0,4},{2,6},{4,0},{6,2},{8,12},{10,14},{12,8},{14,10},{16,20},{18,... | collective-permute-start | bytes 983048 | tf_op jit(solution)/shard_map/ppermute | solution.py:211
  29.2 11.9 %collective-permute-start.5 = (bf16[640,128]{1,0:T(8,128)(2,1)S(1)}, bf16[640,128]{1,0:T(8,128)(2,1)S(1)}, u32[]{:S(2)}, u32[]{:S(2)}) collective-permute-start(bf16[640,128]{1,0:T(8,128)(2,1)S(1)} %collective-permute-done.1.refs_6_), channel_id=1, source_target_pairs={{0,2},{2,0},{4,6},{6,4},{8,10},{10,8},{12,14},{14,12},{16,18},{18,... | collective-permute-start | bytes 491528 | tf_op jit(solution)/shard_map/ppermute | solution.py:208
  30.5 12.7 %collective-permute-start.18 = (bf16[1280,128]{1,0:T(8,128)(2,1)S(1)}, bf16[1280,128]{1,0:T(8,128)(2,1)S(1)}, u32[]{:S(2)}, u32[]{:S(2)}) collective-permute-start(bf16[1280,128]{1,0:T(8,128)(2,1)S(1)} %pad_maximum_fusion.2), channel_id=1, source_target_pairs={{0,4},{2,6},{4,0},{6,2},{8,12},{10,14},{12,8},{14,10},{16,20},{18,... | collective-permute-start | bytes 983048 | tf_op jit(solution)/shard_map/ppermute | solution.py:211
  41.2 11.5 %collective-permute-start.6 = (bf16[1280,128]{1,0:T(8,128)(2,1)S(1)}, bf16[1280,128]{1,0:T(8,128)(2,1)S(1)}, u32[]{:S(2)}, u32[]{:S(2)}) collective-permute-start(bf16[1280,128]{1,0:T(8,128)(2,1)S(1)} %pad_maximum_fusion), channel_id=1, source_target_pairs={{0,4},{2,6},{4,0},{6,2},{8,12},{10,14},{12,8},{14,10},{16,20},{18,... | collective-permute-start | bytes 983048 | tf_op jit(solution)/shard_map/ppermute | solution.py:211
  43.1 8.4 %collective-permute-start.20 = (f32[32,128]{1,0:T(8,128)S(1)}, f32[32,128]{1,0:T(8,128)S(1)}, u32[]{:S(2)}, u32[]{:S(2)}) collective-permute-start(f32[32,128]{1,0:T(8,128)S(1)} %add.40), channel_id=1, source_target_pairs={{0,2},{2,0},{4,6},{6,4},{8,10},{10,8},{12,14},{14,12},{16,18},{18,... | collective-permute-start | bytes 49160 | tf_op jit(solution)/shard_map/ppermute | solution.py:202
  61.8 8.2 %collective-permute-start.23 = (s16[128,1664]{1,0:T(8,128)(2,1)S(1)}, s16[128,1664]{1,0:T(8,128)(2,1)S(1)}, u32[]{:S(2)}, u32[]{:S(2)}) collective-permute-start(s16[128,1664]{1,0:T(8,128)(2,1)S(1)} %backward_3a.1), channel_id=1, source_target_pairs={{0,2},{2,0},{4,6},{6,4},{8,10},{10,8},{12,14},{14,12},{16,18},{18,... | collective-permute-start | bytes 1277960 | tf_op jit(solution)/shard_map/ppermute | solution.py:208
  65.3 19.8 %collective-permute-start.25 = (s16[128,1408]{1,0:T(8,128)(2,1)S(1)}, s16[128,1408]{1,0:T(8,128)(2,1)S(1)}, u32[]{:S(2)}, u32[]{:S(2)}) collective-permute-start(s16[128,1408]{1,0:T(8,128)(2,1)S(1)} %get-tuple-element.68), channel_id=1, source_target_pairs={{0,2},{2,0},{4,6},{6,4},{8,10},{10,8},{12,14},{14,12},{16,18},{18,... | collective-permute-start | bytes 1081352 | tf_op jit(solution)/shard_map/ppermute | solution.py:208
  70.3 6.8 %collective-permute-start.24 = (s16[128,1024]{1,0:T(8,128)(2,1)S(1)}, s16[128,1024]{1,0:T(8,128)(2,1)S(1)}, u32[]{:S(2)}, u32[]{:S(2)}) collective-permute-start(s16[128,1024]{1,0:T(8,128)(2,1)S(1)} %get-tuple-element.70), channel_id=1, source_target_pairs={{0,4},{2,6},{4,0},{6,2},{8,12},{10,14},{12,8},{14,10},{16,20},{18,... | collective-permute-start | bytes 786440 | tf_op jit(solution)/shard_map/ppermute | solution.py:211
  75.0 11.3 %collective-permute-start.26 = (s16[128,1408]{1,0:T(8,128)(2,1)S(1)}, s16[128,1408]{1,0:T(8,128)(2,1)S(1)}, u32[]{:S(2)}, u32[]{:S(2)}) collective-permute-start(s16[128,1408]{1,0:T(8,128)(2,1)S(1)} %get-tuple-element.75), channel_id=1, source_target_pairs={{0,2},{2,0},{4,6},{6,4},{8,10},{10,8},{12,14},{14,12},{16,18},{18,... | collective-permute-start | bytes 1081352 | tf_op jit(solution)/shard_map/ppermute | solution.py:208
  83.0 8.1 %collective-permute-start.31 = (s16[128,768]{1,0:T(8,128)(2,1)S(1)}, s16[128,768]{1,0:T(8,128)(2,1)S(1)}, u32[]{:S(2)}, u32[]{:S(2)}) collective-permute-start(s16[128,768]{1,0:T(8,128)(2,1)S(1)} %get-tuple-element.78), channel_id=1, source_target_pairs={{0,24},{2,26},{4,28},{6,30},{8,16},{10,18},{12,20},{14,22},{16,8},... | collective-permute-start | bytes 589832 | tf_op jit(solution)/shard_map/ppermute | solution.py:202
  85.3 6.0 %collective-permute-start.33 = (s16[128,768]{1,0:T(8,128)(2,1)S(1)}, s16[128,768]{1,0:T(8,128)(2,1)S(1)}, u32[]{:S(2)}, u32[]{:S(2)}) collective-permute-start(s16[128,768]{1,0:T(8,128)(2,1)S(1)} %sum_2.1), channel_id=1, source_target_pairs={{0,4},{2,6},{4,0},{6,2},{8,12},{10,14},{12,8},{14,10},{16,20},{18,... | collective-permute-start | bytes 589832 | tf_op jit(solution)/shard_map/ppermute | solution.py:211
  86.6 6.7 %collective-permute-start.34 = (s16[128,768]{1,0:T(8,128)(2,1)S(1)}, s16[128,768]{1,0:T(8,128)(2,1)S(1)}, u32[]{:S(2)}, u32[]{:S(2)}) collective-permute-start(s16[128,768]{1,0:T(8,128)(2,1)S(1)} %sum_1.1), channel_id=1, source_target_pairs={{0,4},{2,6},{4,0},{6,2},{8,12},{10,14},{12,8},{14,10},{16,20},{18,... | collective-permute-start | bytes 589832 | tf_op jit(solution)/shard_map/ppermute | solution.py:211
  90.8 7.5 %collective-permute-start.32 = (s16[128,1408]{1,0:T(8,128)(2,1)S(1)}, s16[128,1408]{1,0:T(8,128)(2,1)S(1)}, u32[]{:S(2)}, u32[]{:S(2)}) collective-permute-start(s16[128,1408]{1,0:T(8,128)(2,1)S(1)} %get-tuple-element.85), channel_id=1, source_target_pairs={{0,2},{2,0},{4,6},{6,4},{8,10},{10,8},{12,14},{14,12},{16,18},{18,... | collective-permute-start | bytes 1081352 | tf_op jit(solution)/shard_map/ppermute | solution.py:208
  91.5 12.5 %collective-permute-start.37 = (s16[128,768]{1,0:T(8,128)(2,1)S(1)}, s16[128,768]{1,0:T(8,128)(2,1)S(1)}, u32[]{:S(2)}, u32[]{:S(2)}) collective-permute-start(s16[128,768]{1,0:T(8,128)(2,1)S(1)} %sum_z2.1), channel_id=1, source_target_pairs={{0,16},{2,18},{4,20},{6,22},{8,24},{10,26},{12,28},{14,30},{16,0},... | collective-permute-start | bytes 589832 | tf_op jit(solution)/shard_map/ppermute | solution.py:202
  93.5 10.6 %collective-permute-start.36 = (s16[128,768]{1,0:T(8,128)(2,1)S(1)}, s16[128,768]{1,0:T(8,128)(2,1)S(1)}, u32[]{:S(2)}, u32[]{:S(2)}) collective-permute-start(s16[128,768]{1,0:T(8,128)(2,1)S(1)} %sum_z1.1), channel_id=1, source_target_pairs={{0,8},{2,10},{4,12},{6,14},{8,0},{10,2},{12,4},{14,6},{16,24},{18,... | collective-permute-start | bytes 589832 | tf_op jit(solution)/shard_map/ppermute | solution.py:202
  (22 other events, 152.3 us)

commit v4 on v3

--- a/solution.py
+++ b/solution.py
@@ -131,12 +131,13 @@
     copies = []
     for g, (k, line) in enumerate(wanted):
         place = (here()[0] ^ k) * 4 + spot_of(line)
-        copies.append(pltpu.make_async_copy(f_ref.at[:, at(place, width)], buf.at[g], sem.at[g]))
+        into = buf[g] if isinstance(buf, (tuple, list)) else buf.at[g]
+        copies.append(pltpu.make_async_copy(f_ref.at[:, at(place, width)], into, sem.at[g]))
         copies[-1].start()
     return copies
 
 
-def forward(factors, shards, wanted, total, name, parted=False, us=1.0):
+def forward(factors, shards, wanted, total, name, parted=False, us=1.0, ready=(), ahead=()):
     rows = factors.shape[0]
     width, scen = factors.shape[1] // (4 * 4), shards[0].shape[1]
     n, half = len(wanted), rows // 2
@@ -146,13 +147,16 @@
     def body(f_ref, *refs):
         ins, refs = refs[: len(shards)], refs[len(shards) :]
         tot_ref, refs = (refs[0], refs[1:]) if keep else (None, refs)
-        outs, (buf, acc, sem) = refs[:-3], refs[-3:]
-        copies = columns(f_ref, buf, sem, wanted, width)
+        blocks, refs = refs[: len(ready)], refs[len(ready) :]
+        outs, (buf, acc, sem, later) = refs[:-4], refs[-4:]
+        copies = [] if ready else columns(f_ref, buf, sem, wanted, width)
+        extra = columns(f_ref, outs[len(outs) - len(ahead) :], later, ahead, width)
         dst = acc if parted else outs[0]
         for g in range(n):
-            copies[g].wait()
+            if copies:
+                copies[g].wait()
             i, r = spots[g]
-            part = jnp.dot(buf[g], ins[i][r : r + width, :], preferred_element_type=F32)
+            part = jnp.dot(blocks[g][...] if ready else buf[g], ins[i][r : r + width, :], preferred_element_type=F32)
             if g:
                 dst[...] += part
             else:
@@ -161,14 +165,19 @@
             core = here()[2]
             outs[0][...] = acc[at(core, half), :]
             outs[1][...] = acc[at(1 - core, half), :]
-
-    ops = [factors, *shards] + ([total] if keep else [])
+        for copy in extra:
+            copy.wait()
+
+    ops = [factors, *shards] + ([total] if keep else []) + list(ready)
+    shapes = [sds((half, scen), F32)] * 2 if parted else [sds((rows, scen), F32)]
+    shapes += [sds((rows, width), BF16)] * len(ahead)
     return call(
         body,
-        [sds((half, scen), F32)] * 2 if parted else sds((rows, scen), F32),
+        shapes if len(shapes) > 1 else shapes[0],
         [HB] + [VM] * (len(ops) - 1),
         name,
-        [pltpu.VMEM((n, rows, width), BF16), pltpu.VMEM((rows if parted else 8, scen), F32), DMA((n,))],
+        [pltpu.VMEM((1 if ready else n, rows, width), BF16), pltpu.VMEM((rows if parted else 8, scen), F32), DMA((n,)),
+         DMA((max(1, len(ahead)),))],
         us=us,
     )(*ops)
 
@@ -287,8 +296,8 @@
     outage = tie(outage, shards[1][1], shards[3][1])
     outage = outage + send(outage, 2)
     outage = tie(outage, shards[2][1], shards[1][2])
+    summed = outage
     outage = outage + swap(outage)
-    summed = outage
     outage = tie(outage, shards[3][2])
     outage = jnp.concatenate([outage, send(outage, 0, 1)], axis=0)
     wanted = [(k, line) for k in (1, 3) for line in lines] + [(2, line) for line in lines[:2]]
@@ -299,7 +308,9 @@
     contingency = jnp.bitwise_xor(owner % 4, spot) * line_conts + (owner // 4) * group + entry_slot
 
     wanted = [(2, line) for line in lines[2:]]
-    mine, theirs = forward(factors, shards[2][2:], wanted, part, "forward_last", True, us=2.4)
+    mine, theirs, *ready = forward(
+        factors, shards[2][2:], wanted, part, "forward_last", True, us=2.4, ahead=[(3, 3), (3, "a")]
+    )
     theirs = swap(theirs)
 
     def middle(row_ref, mine_ref, theirs_ref, out_ref, lim_ref, er_ref, ert_ref, ct_ref, ctt_ref, f_ref, limr_ref,
@@ -343,20 +354,22 @@
 
     grad_block = sds((scen, width), F32)
 
-    def backward(name, adj, messages, plain, us=3.0, fine=None):
+    def backward(name, adj, messages, plain, us=3.0, fine=None, ready=()):
         wanted = [b for m in messages for b in m] + plain
         n = len(wanted)
 
         def body(f_ref, a_ref, b_ref, *refs):
             outs, (buf, adj, sem) = refs[:-3], refs[-3:]
             more, outs = (outs[0][...], outs[1:]) if fine is not None else (None, outs)
-            copies = columns(f_ref, buf, sem, wanted, width)
+            blocks, outs = outs[: len(ready)], outs[len(ready) :]
+            copies = [] if ready else columns(f_ref, buf, sem, wanted, width)
             adj[:, at(here()[2], half)] = a_ref[...]
             adj[:, at(1 - here()[2], half)] = b_ref[...]
 
             def grad(g):
-                copies[g].wait()
-                return jnp.dot(adj[...], buf[g], preferred_element_type=F32)
+                if copies:
+                    copies[g].wait()
+                return jnp.dot(adj[...], blocks[g][...] if ready else buf[g], preferred_element_type=F32)
 
             g = 0
             for ref, m in zip(outs, messages):
@@ -368,10 +381,10 @@
 
         return call(
             body, [message(len(m), fine is not None) for m in messages] + [grad_block] * len(plain),
-            [HB] + [VM] * (2 if fine is None else 3), name,
-            [pltpu.VMEM((n, rows, width), BF16), pltpu.VMEM((scen, rows), BF16), DMA((n,))],
+            [HB] + [VM] * ((2 if fine is None else 3) + len(ready)), name,
+            [pltpu.VMEM((1 if ready else n, rows, width), BF16), pltpu.VMEM((scen, rows), BF16), DMA((n,))],
             us=us,
-        )(factors, *adj, *([] if fine is None else [fine]))
+        )(factors, *adj, *([] if fine is None else [fine]), *ready)
 
     def add(name, *terms):
         flat = [t[0] if isinstance(t, tuple) else t for t in terms]
@@ -401,24 +414,26 @@
         put_coded(z_ref, [p_ref[...] + get_coded(a_ref, 1, width) + get_coded(b_ref, 0, width)])
 
     adj = (adj_t, other_t)
-    (a3,) = backward("backward_3a", adj, [[(3, 3), (3, "a")]], [], us=2.6, fine=every)
+    (a3,) = backward("backward_3a", adj, [[(3, 3), (3, "a")]], [], us=1.5, fine=every, ready=ready)
     a3_got = send_first(a3)
     adj = (tie(adj_t, a3), other_t)
     a2, p3s, p3 = backward("backward_3b", adj, [[(2, 3), (2, "a")]], [(3, "b"), (3, 0)], us=3.3)
     a2_got = send_first(a2)
+    adj = (tie(adj_t, a2), other_t)
+    wanted = [(2, "b"), (2, 0), (1, "b"), (1, 0)]
+    a1, p2s, p2, p1s, p1 = backward("backward_2", adj, [[(1, 3), (1, "a")]], wanted, us=3.5)
     b3, every = call(
         sum_3, [message(1, True), sds((scen, conts), F32)], [VM] * 3, "sum_3", us=0.3
-    )(tie(p3s, a2), a3_got, every)
+    )(tie(p3s, a1), a3_got, every)
     b3_got = send_second(b3)
     adj = (tie(adj_t, b3), other_t)
-    wanted = [(2, "b"), (2, 0), (1, "b"), (1, 0)]
-    a1, p2s, p2, p1s, p1 = backward("backward_2", adj, [[(1, 3), (1, "a")]], wanted, us=3.5)
-    a1_got = send_first(a1)
+    p0d, p0f, p0s, p0 = backward("backward_0", adj, [], [(0, 3), (0, "a"), (0, "b"), (0, 0)], us=3)
     z3, every = call(
         sum_z3, [message(1), sds((line_conts, scen), F32)], [VM] * 4, "sum_z3", us=0.3
-    )(tie(p3, a1), a3_got, b3_got, every)
+    )(tie(p3, p0), a3_got, b3_got, every)
     every = every + send(every, 1) + send(every, 2) + send(every, 3)
     every = every + swap(every)
+    a1_got = send_first(tie(a1, z3))
     z3_got = send(z3, 3)
     b2 = add("sum_2", tie(p2s, z3), (a2_got, 0))
     b2_got = send_second(b2)
@@ -426,10 +441,7 @@
     b1_got = send_second(b1)
 
 
-    def outaged(f_ref, a_ref, b_ref, e_ref, so_ref, out_ref, s_ref, o_ref, buf, adj, more, sem):
-        copies = columns(f_ref, buf, sem, [(0, line) for line in (3, "a", "b", 0)], width)
-        adj[:, at(here()[2], half)] = a_ref[...]
-        adj[:, at(1 - here()[2], half)] = b_ref[...]
+    def outaged(d_ref, f_ref, p_ref, q_ref, e_ref, so_ref, out_ref, s_ref, o_ref, more):
         marks = so_ref[:, plane:].astype(F32)
         row = marks[:, :1] * 16.0 + marks[:, 1:2]
         wide = jnp.broadcast_to(row, (line_conts, LANES))
@@ -442,27 +454,25 @@
         final = jnp.where(earlier > 0.0, 0.0, merged).astype(BF16)
         more[...] = lax.dot_general(final, so_ref[:, :plane], (((0,), (0,)), ((), ())), preferred_element_type=F32)
 
-        def grad(g, line):
-            copies[g].wait()
-            return jnp.dot(adj[...], buf[g], preferred_element_type=F32) + more[:, at(spot_of(line), width)]
-
-        put_coded(out_ref, [grad(0, 3), grad(1, "a")])
-        s_ref[...] = grad(2, "b")
-        o_ref[...] = grad(3, 0)
+        def grad(ref, line):
+            return ref[...] + more[:, at(spot_of(line), width)]
+
+        put_coded(out_ref, [grad(d_ref, 3), grad(f_ref, "a")])
+        s_ref[...] = grad(p_ref, "b")
+        o_ref[...] = grad(q_ref, 0)
 
     a0, p0s, p0 = call(
-        outaged, [message(2), grad_block, grad_block], [HB] + [VM] * 4, "backward_0",
-        [pltpu.VMEM((4, rows, width), BF16), pltpu.VMEM((scen, rows), BF16), pltpu.VMEM((scen, plane), F32), DMA((4,))],
-        us=0.01,
-    )(factors, tie(adj_t, b1), other_t, every, out_factors)
+        outaged, [message(2), grad_block, grad_block], [VM] * 6, "outaged_rows", [pltpu.VMEM((scen, plane), F32)], us=0.01
+    )(tie(p0d, b1), p0f, p0s, p0, every, out_factors)
     a0_got = send_first(a0)
+
     def gather(p_ref, z3_ref, out_ref):
         out_ref[...] = p_ref[...] + get_coded(z3_ref, 0, width)
 
     p0 = call(gather, grad_block, [VM] * 2, "gradient_z", us=12)(tie(p0, a0), z3_got)
-    z2 = add("sum_z2", tie(p2, p0), (a2_got, 1), (b2_got, 0))
+    z2 = add("sum_z2", tie(p2, a0), (a2_got, 1), (b2_got, 0))
     z2_got = send(z2, 2)
-    z1 = add("sum_z1", tie(p1, z2), (a1_got, 1), (b1_got, 0))
+    z1 = add("sum_z1", tie(p1, z2, p0), (a1_got, 1), (b1_got, 0))
     z1_got = send(z1, 1)
 
     b0 = add("sum_0", tie(p0s, z1), (a0_got, 0))

time: 106 us -> 105 us (level)
  waiting for transfers between devices: 27.8 us -> 25.6 us
  other arithmetic: 0.12 us -> 1.51 us
    ppermute x8, waiting for transfers between devices: 7.15 us -> 2.32 us  [send_first(): return lax.ppermute(v, both, split((1, 2)))]
    ppermute x9, waiting for transfers between devices: 4.66 us -> 7.21 us  [send_second(): return lax.ppermute(v, both, split((2, 1)))]
    pallas_call x4, Pallas kernels: 15.9 us -> 13.8 us  [the longest x3 12.8 us: forward(): call(body, shapes if len(shapes) > 1 else shapes[0], [HB] + [VM] * (len(o...]
    pallas_call x3 -> x4, Pallas kernels: 8.62 us -> 9.82 us  [backward(): call(body, [message(len(m), fine is not None) for m in messages] + [grad_...]
    ppermute x8, starting transfers between devices: 7.32 us -> 8.42 us  [send_first(): return lax.ppermute(v, both, split((1, 2)))]
  transfers between devices with their start and end apart: 38 -> 38, of which waited for: 15 -> 14; matrix products, arithmetic and copies ran while one was open for 1% -> 2% of each run, Pallas kernels for 26% -> 27%
where the time goes in v4:
time: 105 us
  starting transfers between devices  43.9 us (42%)
  Pallas kernels  31.9 us (30%)
  waiting for transfers between devices  25.6 us (24%)
  other arithmetic  1.51 us (1%)
  local copies, waits for them, and re-layouts  1.24 us (1%)
    ppermute x16, starting transfers between devices, send(): return lax.ppermute(v, 'br', to(dz, ds))  25.6 us
    pallas_call x3, Pallas kernels, forward(): call(body, shapes if len(shapes) > 1 else shapes[0], [HB] + [VM] * (len(o...  12.8 us
    ppermute x16, waiting for transfers between devices, send(): return lax.ppermute(v, 'br', to(dz, ds))  12.6 us
    pallas_call x4, Pallas kernels, backward(): call(body, [message(len(m), fine is not None) for m in messages] + [grad_...  9.82 us
    ppermute x9, starting transfers between devices, send_second(): return lax.ppermute(v, both, split((2, 1)))  9.2 us
    ppermute x8, starting transfers between devices, send_first(): return lax.ppermute(v, both, split((1, 2)))  8.42 us
    ppermute x9, waiting for transfers between devices, send_second(): return lax.ppermute(v, both, split((2, 1)))  7.21 us
    ppermute x5, waiting for transfers between devices, swap(): return lax.ppermute(v, 'bus', [(0, 1), (1, 0)])  3.48 us
  transfers between devices with their start and end apart: 38, of which 14 were waited for; matrix products, arithmetic and copies ran while one was open for 2% of the time, Pallas kernels for 27%

profile of v4, /device:TPU:0, one launch (start us, length us, event | category | flops | bytes accessed | tf_op | source)
XLA Modules:
  0.0 104.5 jit_solution(14474940129468847717)
XLA Ops:
  0.0 3.0 %collective-permute-start.11 = (bf16[640,128]{1,0:T(8,128)(2,1)}, bf16[640,128]{1,0:T(8,128)(2,1)S(1)}, u32[]{:S(2)}, u32[]{:S(2)}) collective-permute-start(bf16[640,128]{1,0:T(8,128)(2,1)} %refs_4_.1), channel_id=1, source_target_pairs={{0,8},{2,10},{4,12},{6,14},{8,0},{10,2},{12,4},{14,6},{16,24},{18,... | collective-permute-start | bytes 491528 | tf_op jit(solution)/shard_map/ppermute | solution.py:211
  3.0 1.5 %collective-permute-start.3 = (bf16[640,128]{1,0:T(8,128)(2,1)}, bf16[640,128]{1,0:T(8,128)(2,1)S(1)}, u32[]{:S(2)}, u32[]{:S(2)}) collective-permute-start(bf16[640,128]{1,0:T(8,128)(2,1)} %refs_4_.1), channel_id=1, source_target_pairs={{0,4},{2,6},{4,0},{6,2},{8,12},{10,14},{12,8},{14,10},{16,20},{18,... | collective-permute-start | bytes 491528 | tf_op jit(solution)/shard_map/ppermute | solution.py:220
  7.3 2.5 %collective-permute-start.13 = (bf16[640,128]{1,0:T(8,128)(2,1)}, bf16[640,128]{1,0:T(8,128)(2,1)S(1)}, u32[]{:S(2)}, u32[]{:S(2)}) collective-permute-start(bf16[640,128]{1,0:T(8,128)(2,1)} %refs_4_.1), channel_id=1, source_target_pairs={{0,24},{2,26},{4,28},{6,30},{8,16},{10,18},{12,20},{14,22},{16,8},... | collective-permute-start | bytes 491528 | tf_op jit(solution)/shard_map/ppermute | solution.py:211
  11.1 2.8 %outage_rows.1 = (bf16[8,2688]{1,0:T(8,128)(2,1)S(1)}, bf16[8,2688]{1,0:T(8,128)(2,1)S(1)}, bf16[8,2688]{1,0:T(8,128)(2,1)S(1)}, bf16[8,2688]{1,0:T(8,128)(2,1)S(1)}) custom-call(s32[4]{0:T(128)S(1)} %copy-done.2, s32[4]{0:T(128)S(1)} %collective-permute-done.other_ref, bf16[768,10240]{1,0:T(8,128)(2,1)} %f_ref.14), custom_call_target="tpu_custom_call" | custom-call | flops 3449999872 | bytes 1 | tf_op jit(solution)/shard_map/outage_rows/pallas_call | solution.py:269
  13.9 1.8 %collective-permute-start.7 = (bf16[8,2688]{1,0:T(8,128)(2,1)S(1)}, bf16[8,2688]{1,0:T(8,128)(2,1)S(1)}, u32[]{:S(2)}, u32[]{:S(2)}) collective-permute-start(bf16[8,2688]{1,0:T(8,128)(2,1)S(1)} %get-tuple-element.61), channel_id=1, source_target_pairs={{0,8},{2,10},{4,12},{6,14},{8,0},{10,2},{12,4},{14,6},{16,24},{18,... | collective-permute-start | bytes 129032 | tf_op jit(solution)/shard_map/ppermute | solution.py:211
  16.3 2.3 %collective-permute-start.8 = (bf16[8,2688]{1,0:T(8,128)(2,1)S(1)}, bf16[8,2688]{1,0:T(8,128)(2,1)S(1)}, u32[]{:S(2)}, u32[]{:S(2)}) collective-permute-start(bf16[8,2688]{1,0:T(8,128)(2,1)S(1)} %get-tuple-element.62), channel_id=1, source_target_pairs={{0,16},{2,18},{4,20},{6,22},{8,24},{10,26},{12,28},{14,30},{16,0},... | collective-permute-start | bytes 129032 | tf_op jit(solution)/shard_map/ppermute | solution.py:211
  19.5 3.1 %collective-permute-done.4.refs_3_.refs_7_ = bf16[640,128]{1,0:T(8,128)(2,1)S(1)} collective-permute-done((bf16[640,128]{1,0:T(8,128)(2,1)S(1)}, bf16[640,128]{1,0:T(8,128)(2,1)S(1)}, u32[]{:S(2)}, u32[]{:S(2)}) %collective-permute-start.4) | collective-permute-done | bytes 163872 | tf_op jit(solution)/shard_map/ppermute | solution.py:220
  22.7 3.5 %forward_own.1.refs_8_ = f32[768,128]{1,0:T(8,128)S(1)} custom-call(bf16[768,10240]{1,0:T(8,128)(2,1)} %f_ref.14, bf16[640,128]{1,0:T(8,128)(2,1)S(1)} %copy-done, bf16[640,128]{1,0:T(8,128)(2,1)S(1)} %collective-permute-done.2.refs_1_.refs_5_, bf16[640,128]{1,0:T(8,128)(2,1)S(1)} %collective-permute-done.3.refs_2_.refs_6_, ...), custom_call_target="tpu_custom_call" | custom-call | flops 4024999936 | bytes 1 | tf_op jit(solution)/shard_map/forward_own/pallas_call | solution.py:174
  26.5 2.7 %collective-permute-start.9 = (bf16[8,2688]{1,0:T(8,128)(2,1)S(1)}, bf16[8,2688]{1,0:T(8,128)(2,1)S(1)}, u32[]{:S(2)}, u32[]{:S(2)}) collective-permute-start(bf16[8,2688]{1,0:T(8,128)(2,1)S(1)} %get-tuple-element.63), channel_id=1, source_target_pairs={{0,24},{2,26},{4,28},{6,30},{8,16},{10,18},{12,20},{14,22},{16,8},... | collective-permute-start | bytes 129032 | tf_op jit(solution)/shard_map/ppermute | solution.py:211
  33.7 2.7 %collective-permute-done.10 = f32[32,128]{1,0:T(8,128)S(1)} collective-permute-done((f32[32,128]{1,0:T(8,128)S(1)}, f32[32,128]{1,0:T(8,128)S(1)}, u32[]{:S(2)}, u32[]{:S(2)}) %collective-permute-start.10) | collective-permute-done | bytes 16416 | tf_op jit(solution)/shard_map/ppermute | solution.py:211
  37.8 3.2 %collective-permute-done.15 = f32[32,128]{1,0:T(8,128)S(1)} collective-permute-done((f32[32,128]{1,0:T(8,128)S(1)}, f32[32,128]{1,0:T(8,128)S(1)}, u32[]{:S(2)}, u32[]{:S(2)}) %collective-permute-start.15) | collective-permute-done | bytes 16416 | tf_op jit(solution)/shard_map/ppermute | solution.py:211
  41.2 1.8 %collective-permute-start.6 = (bf16[1280,128]{1,0:T(8,128)(2,1)S(1)}, bf16[1280,128]{1,0:T(8,128)(2,1)S(1)}, u32[]{:S(2)}, u32[]{:S(2)}) collective-permute-start(bf16[1280,128]{1,0:T(8,128)(2,1)S(1)} %pad_maximum_fusion), channel_id=1, source_target_pairs={{0,4},{2,6},{4,0},{6,2},{8,12},{10,14},{12,8},{14,10},{16,20},{18,... | collective-permute-start | bytes 983048 | tf_op jit(solution)/shard_map/ppermute | solution.py:220
  44.6 6.9 %forward_most.1.refs_1_ = f32[768,128]{1,0:T(8,128)S(1)} custom-call(bf16[768,10240]{1,0:T(8,128)(2,1)} %f_ref.14, bf16[640,128]{1,0:T(8,128)(2,1)S(1)} %collective-permute-done.11.refs_0_, bf16[640,128]{1,0:T(8,128)(2,1)S(1)} %collective-permute-done.12.refs_1_, bf16[1280,128]{1,0:T(8,128)(2,1)S(1)} %collective-permute-done.16.refs_2_, ...), custom_call_target="tpu_custom_call" | custom-call | flops 6899999744 | bytes 1 | tf_op jit(solution)/shard_map/forward_most/pallas_call | solution.py:174
  53.2 2.5 %forward_last.1 = (f32[384,128]{1,0:T(8,128)S(1)}, f32[384,128]{1,0:T(8,128)S(1)}, bf16[768,640]{1,0:T(8,128)(2,1)S(1)}, bf16[768,640]{1,0:T(8,128)(2,1)S(1)}) custom-call(bf16[768,10240]{1,0:T(8,128)(2,1)} %f_ref.14, bf16[1280,128]{1,0:T(8,128)(2,1)S(1)} %collective-permute-done.6.refs_0_, f32[768,128]{1,0:T(8,128)S(1)} %forward_most.1.refs_1_), custom_call_target="tpu_custom_call" | custom-call | flops 2760000000 | bytes 1 | tf_op jit(solution)/shard_map/forward_last/pallas_call | solution.py:174
  57.3 2.1 %penalty.1 = (bf16[128,384]{1,0:T(8,128)(2,1)S(1)}, f32[128,128]{1,0:T(8,128)S(1)}) custom-call(s32[4]{0:T(128)S(1)} %copy-done.3, f32[384,128]{1,0:T(8,128)S(1)} %get-tuple-element.68.mine_ref, f32[384,128]{1,0:T(8,128)} %collective-permute-done.18.theirs_ref, f32[128,128]{1,0:T(8,128)S(1)} %pad_maximum_fusion.3.out_ref, ...), custom_call_target="tpu_custom_call" | custom-call | flops 575000000 | bytes 1 | tf_op jit(solution)/shard_map/penalty/pallas_call | solution.py:343
  62.2 2.8 %backward_3b.1 = (s16[128,1408]{1,0:T(8,128)(2,1)S(1)}, f32[128,640]{1,0:T(8,128)S(1)}, f32[128,640]{1,0:T(8,128)S(1)}) custom-call(bf16[768,10240]{1,0:T(8,128)(2,1)} %f_ref.14, bf16[128,384]{1,0:T(8,128)(2,1)S(1)} %get-tuple-element.83.a_ref, bf16[128,384]{1,0:T(8,128)(2,1)S(1)} %collective-permute-done.22.b_ref), custom_call_target="tpu_custom_call" | custom-call | flops 3795000064 | bytes 1 | tf_op jit(solution)/shard_map/backward_3b/pallas_call | solution.py:382
  66.5 3.7 %backward_2.1 = (s16[128,1408]{1,0:T(8,128)(2,1)S(1)}, f32[128,640]{1,0:T(8,128)S(1)}, f32[128,640]{1,0:T(8,128)S(1)}, f32[128,640]{1,0:T(8,128)S(1)}, f32[128,640]{1,0:T(8,128)S(1)}) custom-call(bf16[768,10240]{1,0:T(8,128)(2,1)} %f_ref.14, bf16[128,384]{1,0:T(8,128)(2,1)S(1)} %get-tuple-element.83.a_ref, bf16[128,384]{1,0:T(8,128)(2,1)S(1)} %collective-permute-done.22.b_ref), custom_call_target="tpu_custom_call" | custom-call | flops 4024999936 | bytes 1 | tf_op jit(solution)/shard_map/backward_2/pallas_call | solution.py:382
  71.6 2.7 %backward_0.1 = (f32[128,640]{1,0:T(8,128)S(1)}, f32[128,640]{1,0:T(8,128)S(1)}, f32[128,640]{1,0:T(8,128)S(1)}, f32[128,640]{1,0:T(8,128)S(1)}) custom-call(bf16[768,10240]{1,0:T(8,128)(2,1)} %f_ref.14, bf16[128,384]{1,0:T(8,128)(2,1)S(1)} %get-tuple-element.83.a_ref, bf16[128,384]{1,0:T(8,128)(2,1)S(1)} %collective-permute-done.22.b_ref), custom_call_target="tpu_custom_call" | custom-call | flops 3449999872 | bytes 1 | tf_op jit(solution)/shard_map/backward_0/pallas_call | solution.py:382
  74.2 2.7 %collective-permute-done.24.b_ref = s16[128,1024]{1,0:T(8,128)(2,1)S(1)} collective-permute-done((s16[128,1024]{1,0:T(8,128)(2,1)S(1)}, s16[128,1024]{1,0:T(8,128)(2,1)S(1)}, u32[]{:S(2)}, u32[]{:S(2)}) %collective-permute-start.24) | collective-permute-done | bytes 262176 | tf_op jit(solution)/shard_map/ppermute | solution.py:220
  78.0 1.9 %collective-permute-start.29 = (f32[32,128]{1,0:T(8,128)S(1)}, f32[32,128]{1,0:T(8,128)S(1)}, u32[]{:S(2)}, u32[]{:S(2)}) collective-permute-start(f32[32,128]{1,0:T(8,128)S(1)} %get-tuple-element.98), channel_id=1, source_target_pairs={{0,24},{2,26},{4,28},{6,30},{8,16},{10,18},{12,20},{14,22},{16,8},... | collective-permute-start | bytes 49160 | tf_op jit(solution)/shard_map/ppermute | solution.py:211
  79.9 2.5 %collective-permute-start.27 = (f32[32,128]{1,0:T(8,128)S(1)}, f32[32,128]{1,0:T(8,128)S(1)}, u32[]{:S(2)}, u32[]{:S(2)}) collective-permute-start(f32[32,128]{1,0:T(8,128)S(1)} %get-tuple-element.98), channel_id=1, source_target_pairs={{0,8},{2,10},{4,12},{6,14},{8,0},{10,2},{12,4},{14,6},{16,24},{18,... | collective-permute-start | bytes 49160 | tf_op jit(solution)/shard_map/ppermute | solution.py:211
  82.4 1.9 %collective-permute-start.31 = (s16[128,768]{1,0:T(8,128)(2,1)S(1)}, s16[128,768]{1,0:T(8,128)(2,1)S(1)}, u32[]{:S(2)}, u32[]{:S(2)}) collective-permute-start(s16[128,768]{1,0:T(8,128)(2,1)S(1)} %get-tuple-element.91), channel_id=1, source_target_pairs={{0,24},{2,26},{4,28},{6,30},{8,16},{10,18},{12,20},{14,22},{16,8},... | collective-permute-start | bytes 589832 | tf_op jit(solution)/shard_map/ppermute | solution.py:211
  94.4 2.3 %collective-permute-done.32.refs_1_.a_ref = s16[128,1408]{1,0:T(8,128)(2,1)S(1)} collective-permute-done((s16[128,1408]{1,0:T(8,128)(2,1)S(1)}, s16[128,1408]{1,0:T(8,128)(2,1)S(1)}, u32[]{:S(2)}, u32[]{:S(2)}) %collective-permute-start.32) | collective-permute-done | bytes 360480 | tf_op jit(solution)/shard_map/ppermute | solution.py:217
  98.0 4.6 %collective-permute-done.37.z2_ref = s16[128,768]{1,0:T(8,128)(2,1)S(1)} collective-permute-done((s16[128,768]{1,0:T(8,128)(2,1)S(1)}, s16[128,768]{1,0:T(8,128)(2,1)S(1)}, u32[]{:S(2)}, u32[]{:S(2)}) %collective-permute-start.37) | collective-permute-done | bytes 196640 | tf_op jit(solution)/shard_map/ppermute | solution.py:211
  (104 shorter events, 36.5 us)
Async XLA Ops:
  0.0 9.9 %collective-permute-start.11 = (bf16[640,128]{1,0:T(8,128)(2,1)}, bf16[640,128]{1,0:T(8,128)(2,1)S(1)}, u32[]{:S(2)}, u32[]{:S(2)}) collective-permute-start(bf16[640,128]{1,0:T(8,128)(2,1)} %refs_4_.1), channel_id=1, source_target_pairs={{0,8},{2,10},{4,12},{6,14},{8,0},{10,2},{12,4},{14,6},{16,24},{18,... | collective-permute-start | bytes 491528 | tf_op jit(solution)/shard_map/ppermute | solution.py:211
  3.0 13.3 %collective-permute-start.3 = (bf16[640,128]{1,0:T(8,128)(2,1)}, bf16[640,128]{1,0:T(8,128)(2,1)S(1)}, u32[]{:S(2)}, u32[]{:S(2)}) collective-permute-start(bf16[640,128]{1,0:T(8,128)(2,1)} %refs_4_.1), channel_id=1, source_target_pairs={{0,4},{2,6},{4,0},{6,2},{8,12},{10,14},{12,8},{14,10},{16,20},{18,... | collective-permute-start | bytes 491528 | tf_op jit(solution)/shard_map/ppermute | solution.py:220
  4.5 9.4 %collective-permute-start.2 = (bf16[640,128]{1,0:T(8,128)(2,1)}, bf16[640,128]{1,0:T(8,128)(2,1)S(1)}, u32[]{:S(2)}, u32[]{:S(2)}) collective-permute-start(bf16[640,128]{1,0:T(8,128)(2,1)} %refs_4_.1), channel_id=1, source_target_pairs={{0,2},{2,0},{4,6},{6,4},{8,10},{10,8},{12,14},{14,12},{16,18},{18,... | collective-permute-start | bytes 491528 | tf_op jit(solution)/shard_map/ppermute | solution.py:217
  7.3 11.3 %collective-permute-start.13 = (bf16[640,128]{1,0:T(8,128)(2,1)}, bf16[640,128]{1,0:T(8,128)(2,1)S(1)}, u32[]{:S(2)}, u32[]{:S(2)}) collective-permute-start(bf16[640,128]{1,0:T(8,128)(2,1)} %refs_4_.1), channel_id=1, source_target_pairs={{0,24},{2,26},{4,28},{6,30},{8,16},{10,18},{12,20},{14,22},{16,8},... | collective-permute-start | bytes 491528 | tf_op jit(solution)/shard_map/ppermute | solution.py:211
  9.8 16.7 %collective-permute-start.1 = (bf16[640,128]{1,0:T(8,128)(2,1)}, bf16[640,128]{1,0:T(8,128)(2,1)S(1)}, u32[]{:S(2)}, u32[]{:S(2)}) collective-permute-start(bf16[640,128]{1,0:T(8,128)(2,1)} %refs_4_.1), channel_id=1, source_target_pairs={{0,16},{2,18},{4,20},{6,22},{8,24},{10,26},{12,28},{14,30},{16,0},... | collective-permute-start | bytes 491528 | tf_op jit(solution)/shard_map/ppermute | solution.py:211
  13.9 16.5 %collective-permute-start.7 = (bf16[8,2688]{1,0:T(8,128)(2,1)S(1)}, bf16[8,2688]{1,0:T(8,128)(2,1)S(1)}, u32[]{:S(2)}, u32[]{:S(2)}) collective-permute-start(bf16[8,2688]{1,0:T(8,128)(2,1)S(1)} %get-tuple-element.61), channel_id=1, source_target_pairs={{0,8},{2,10},{4,12},{6,14},{8,0},{10,2},{12,4},{14,6},{16,24},{18,... | collective-permute-start | bytes 129032 | tf_op jit(solution)/shard_map/ppermute | solution.py:211
  15.8 6.9 %collective-permute-start.4 = (bf16[640,128]{1,0:T(8,128)(2,1)S(1)}, bf16[640,128]{1,0:T(8,128)(2,1)S(1)}, u32[]{:S(2)}, u32[]{:S(2)}) collective-permute-start(bf16[640,128]{1,0:T(8,128)(2,1)S(1)} %collective-permute-done.2.refs_1_.refs_5_), channel_id=1, source_target_pairs={{0,4},{2,6},{4,0},{6,2},{8,12},{10,14},{12,8},{14,10},{16,20},{18,... | collective-permute-start | bytes 491528 | tf_op jit(solution)/shard_map/ppermute | solution.py:220
  16.3 15.2 %collective-permute-start.8 = (bf16[8,2688]{1,0:T(8,128)(2,1)S(1)}, bf16[8,2688]{1,0:T(8,128)(2,1)S(1)}, u32[]{:S(2)}, u32[]{:S(2)}) collective-permute-start(bf16[8,2688]{1,0:T(8,128)(2,1)S(1)} %get-tuple-element.62), channel_id=1, source_target_pairs={{0,16},{2,18},{4,20},{6,22},{8,24},{10,26},{12,28},{14,30},{16,0},... | collective-permute-start | bytes 129032 | tf_op jit(solution)/shard_map/ppermute | solution.py:211
  18.6 10.6 %collective-permute-start.14 = (bf16[640,128]{1,0:T(8,128)(2,1)S(1)}, bf16[640,128]{1,0:T(8,128)(2,1)S(1)}, u32[]{:S(2)}, u32[]{:S(2)}) collective-permute-start(bf16[640,128]{1,0:T(8,128)(2,1)S(1)} %collective-permute-done.13.refs_3_), channel_id=1, source_target_pairs={{0,2},{2,0},{4,6},{6,4},{8,10},{10,8},{12,14},{14,12},{16,18},{18,... | collective-permute-start | bytes 491528 | tf_op jit(solution)/shard_map/ppermute | solution.py:217
  22.7 18.4 %collective-permute-start.16 = (bf16[1280,128]{1,0:T(8,128)(2,1)S(1)}, bf16[1280,128]{1,0:T(8,128)(2,1)S(1)}, u32[]{:S(2)}, u32[]{:S(2)}) collective-permute-start(bf16[1280,128]{1,0:T(8,128)(2,1)S(1)} %pad_maximum_fusion.1), channel_id=1, source_target_pairs={{0,4},{2,6},{4,0},{6,2},{8,12},{10,14},{12,8},{14,10},{16,20},{18,... | collective-permute-start | bytes 983048 | tf_op jit(solution)/shard_map/ppermute | solution.py:220
  29.2 11.9 %collective-permute-start.5 = (bf16[640,128]{1,0:T(8,128)(2,1)S(1)}, bf16[640,128]{1,0:T(8,128)(2,1)S(1)}, u32[]{:S(2)}, u32[]{:S(2)}) collective-permute-start(bf16[640,128]{1,0:T(8,128)(2,1)S(1)} %collective-permute-done.1.refs_6_), channel_id=1, source_target_pairs={{0,2},{2,0},{4,6},{6,4},{8,10},{10,8},{12,14},{14,12},{16,18},{18,... | collective-permute-start | bytes 491528 | tf_op jit(solution)/shard_map/ppermute | solution.py:217
  30.5 12.6 %collective-permute-start.17 = (bf16[1280,128]{1,0:T(8,128)(2,1)S(1)}, bf16[1280,128]{1,0:T(8,128)(2,1)S(1)}, u32[]{:S(2)}, u32[]{:S(2)}) collective-permute-start(bf16[1280,128]{1,0:T(8,128)(2,1)S(1)} %pad_maximum_fusion.2), channel_id=1, source_target_pairs={{0,4},{2,6},{4,0},{6,2},{8,12},{10,14},{12,8},{14,10},{16,20},{18,... | collective-permute-start | bytes 983048 | tf_op jit(solution)/shard_map/ppermute | solution.py:220
  41.2 12.0 %collective-permute-start.6 = (bf16[1280,128]{1,0:T(8,128)(2,1)S(1)}, bf16[1280,128]{1,0:T(8,128)(2,1)S(1)}, u32[]{:S(2)}, u32[]{:S(2)}) collective-permute-start(bf16[1280,128]{1,0:T(8,128)(2,1)S(1)} %pad_maximum_fusion), channel_id=1, source_target_pairs={{0,4},{2,6},{4,0},{6,2},{8,12},{10,14},{12,8},{14,10},{16,20},{18,... | collective-permute-start | bytes 983048 | tf_op jit(solution)/shard_map/ppermute | solution.py:220
  43.1 8.4 %collective-permute-start.20 = (f32[32,128]{1,0:T(8,128)S(1)}, f32[32,128]{1,0:T(8,128)S(1)}, u32[]{:S(2)}, u32[]{:S(2)}) collective-permute-start(f32[32,128]{1,0:T(8,128)S(1)} %add.40), channel_id=1, source_target_pairs={{0,2},{2,0},{4,6},{6,4},{8,10},{10,8},{12,14},{14,12},{16,18},{18,... | collective-permute-start | bytes 49160 | tf_op jit(solution)/shard_map/ppermute | solution.py:211
  61.5 8.7 %collective-permute-start.23 = (s16[128,1664]{1,0:T(8,128)(2,1)S(1)}, s16[128,1664]{1,0:T(8,128)(2,1)S(1)}, u32[]{:S(2)}, u32[]{:S(2)}) collective-permute-start(s16[128,1664]{1,0:T(8,128)(2,1)S(1)} %backward_3a.1), channel_id=1, source_target_pairs={{0,2},{2,0},{4,6},{6,4},{8,10},{10,8},{12,14},{14,12},{16,18},{18,... | collective-permute-start | bytes 1277960 | tf_op jit(solution)/shard_map/ppermute | solution.py:217
  65.0 17.4 %collective-permute-start.25 = (s16[128,1408]{1,0:T(8,128)(2,1)S(1)}, s16[128,1408]{1,0:T(8,128)(2,1)S(1)}, u32[]{:S(2)}, u32[]{:S(2)}) collective-permute-start(s16[128,1408]{1,0:T(8,128)(2,1)S(1)} %get-tuple-element.78), channel_id=1, source_target_pairs={{0,2},{2,0},{4,6},{6,4},{8,10},{10,8},{12,14},{14,12},{16,18},{18,... | collective-permute-start | bytes 1081352 | tf_op jit(solution)/shard_map/ppermute | solution.py:217
  70.5 6.4 %collective-permute-start.24 = (s16[128,1024]{1,0:T(8,128)(2,1)S(1)}, s16[128,1024]{1,0:T(8,128)(2,1)S(1)}, u32[]{:S(2)}, u32[]{:S(2)}) collective-permute-start(s16[128,1024]{1,0:T(8,128)(2,1)S(1)} %get-tuple-element.82), channel_id=1, source_target_pairs={{0,4},{2,6},{4,0},{6,2},{8,12},{10,14},{12,8},{14,10},{16,20},{18,... | collective-permute-start | bytes 786440 | tf_op jit(solution)/shard_map/ppermute | solution.py:220
  77.4 9.6 %collective-permute-start.26 = (s16[128,1408]{1,0:T(8,128)(2,1)S(1)}, s16[128,1408]{1,0:T(8,128)(2,1)S(1)}, u32[]{:S(2)}, u32[]{:S(2)}) collective-permute-start(s16[128,1408]{1,0:T(8,128)(2,1)S(1)} %get-tuple-element.94), channel_id=1, source_target_pairs={{0,2},{2,0},{4,6},{6,4},{8,10},{10,8},{12,14},{14,12},{16,18},{18,... | collective-permute-start | bytes 1081352 | tf_op jit(solution)/shard_map/ppermute | solution.py:217
  78.0 6.5 %collective-permute-start.29 = (f32[32,128]{1,0:T(8,128)S(1)}, f32[32,128]{1,0:T(8,128)S(1)}, u32[]{:S(2)}, u32[]{:S(2)}) collective-permute-start(f32[32,128]{1,0:T(8,128)S(1)} %get-tuple-element.98), channel_id=1, source_target_pairs={{0,24},{2,26},{4,28},{6,30},{8,16},{10,18},{12,20},{14,22},{16,8},... | collective-permute-start | bytes 49160 | tf_op jit(solution)/shard_map/ppermute | solution.py:211
  82.4 9.7 %collective-permute-start.31 = (s16[128,768]{1,0:T(8,128)(2,1)S(1)}, s16[128,768]{1,0:T(8,128)(2,1)S(1)}, u32[]{:S(2)}, u32[]{:S(2)}) collective-permute-start(s16[128,768]{1,0:T(8,128)(2,1)S(1)} %get-tuple-element.91), channel_id=1, source_target_pairs={{0,24},{2,26},{4,28},{6,30},{8,16},{10,18},{12,20},{14,22},{16,8},... | collective-permute-start | bytes 589832 | tf_op jit(solution)/shard_map/ppermute | solution.py:211
  89.2 7.5 %collective-permute-start.32 = (s16[128,1408]{1,0:T(8,128)(2,1)S(1)}, s16[128,1408]{1,0:T(8,128)(2,1)S(1)}, u32[]{:S(2)}, u32[]{:S(2)}) collective-permute-start(s16[128,1408]{1,0:T(8,128)(2,1)S(1)} %get-tuple-element.101), channel_id=1, source_target_pairs={{0,2},{2,0},{4,6},{6,4},{8,10},{10,8},{12,14},{14,12},{16,18},{18,... | collective-permute-start | bytes 1081352 | tf_op jit(solution)/shard_map/ppermute | solution.py:217
  90.9 11.7 %collective-permute-start.37 = (s16[128,768]{1,0:T(8,128)(2,1)S(1)}, s16[128,768]{1,0:T(8,128)(2,1)S(1)}, u32[]{:S(2)}, u32[]{:S(2)}) collective-permute-start(s16[128,768]{1,0:T(8,128)(2,1)S(1)} %sum_z2.1), channel_id=1, source_target_pairs={{0,16},{2,18},{4,20},{6,22},{8,24},{10,26},{12,28},{14,30},{16,0},... | collective-permute-start | bytes 589832 | tf_op jit(solution)/shard_map/ppermute | solution.py:211
  93.8 9.6 %collective-permute-start.36 = (s16[128,768]{1,0:T(8,128)(2,1)S(1)}, s16[128,768]{1,0:T(8,128)(2,1)S(1)}, u32[]{:S(2)}, u32[]{:S(2)}) collective-permute-start(s16[128,768]{1,0:T(8,128)(2,1)S(1)} %sum_z1.1), channel_id=1, source_target_pairs={{0,8},{2,10},{4,12},{6,14},{8,0},{10,2},{12,4},{14,6},{16,24},{18,... | collective-permute-start | bytes 589832 | tf_op jit(solution)/shard_map/ppermute | solution.py:211
  96.9 6.5 %collective-permute-start.35 = (s16[128,768]{1,0:T(8,128)(2,1)S(1)}, s16[128,768]{1,0:T(8,128)(2,1)S(1)}, u32[]{:S(2)}, u32[]{:S(2)}) collective-permute-start(s16[128,768]{1,0:T(8,128)(2,1)S(1)} %sum_0.1), channel_id=1, source_target_pairs={{0,4},{2,6},{4,0},{6,2},{8,12},{10,14},{12,8},{14,10},{16,20},{18,... | collective-permute-start | bytes 589832 | tf_op jit(solution)/shard_map/ppermute | solution.py:220
  (22 other events, 157.9 us)

commit v5 on v4

--- a/solution.py
+++ b/solution.py
@@ -19,7 +19,7 @@
 LANES = 128
 
 
-def call(body, out_shape, in_specs, name, scratch=(), us=0.5, limit=24):
+def call(body, out_shape, in_specs, name, scratch=(), us=0.5, limit=16):
     many = isinstance(out_shape, (tuple, list))
     return pl.pallas_call(
         body,

time: 105 us -> 105 us (level)
  no operation moved by 1% of the time
where the time goes in v5:
time: 105 us
  starting transfers between devices  43.9 us (42%)
  Pallas kernels  31.9 us (30%)
  waiting for transfers between devices  25.6 us (24%)
  other arithmetic  1.51 us (1%)
  local copies, waits for them, and re-layouts  1.24 us (1%)
    ppermute x16, starting transfers between devices, send(): return lax.ppermute(v, 'br', to(dz, ds))  25.6 us
    pallas_call x3, Pallas kernels, forward(): call(body, shapes if len(shapes) > 1 else shapes[0], [HB] + [VM] * (len(o...  12.8 us
    ppermute x16, waiting for transfers between devices, send(): return lax.ppermute(v, 'br', to(dz, ds))  12.6 us
    pallas_call x4, Pallas kernels, backward(): call(body, [message(len(m), fine is not None) for m in messages] + [grad_...  9.82 us
    ppermute x9, starting transfers between devices, send_second(): return lax.ppermute(v, both, split((2, 1)))  9.22 us
    ppermute x8, starting transfers between devices, send_first(): return lax.ppermute(v, both, split((1, 2)))  8.43 us
    ppermute x9, waiting for transfers between devices, send_second(): return lax.ppermute(v, both, split((2, 1)))  7.21 us
    ppermute x5, waiting for transfers between devices, swap(): return lax.ppermute(v, 'bus', [(0, 1), (1, 0)])  3.48 us
  transfers between devices with their start and end apart: 38, of which 14 were waited for; matrix products, arithmetic and copies ran while one was open for 2% of the time, Pallas kernels for 27%

profile of v5, /device:TPU:0, one launch (start us, length us, event | category | flops | bytes accessed | tf_op | source)
XLA Modules:
  0.0 104.5 jit_solution(12110929183749456584)
XLA Ops:
  0.0 3.0 %collective-permute-start.11 = (bf16[640,128]{1,0:T(8,128)(2,1)}, bf16[640,128]{1,0:T(8,128)(2,1)S(1)}, u32[]{:S(2)}, u32[]{:S(2)}) collective-permute-start(bf16[640,128]{1,0:T(8,128)(2,1)} %refs_4_.1), channel_id=1, source_target_pairs={{0,8},{2,10},{4,12},{6,14},{8,0},{10,2},{12,4},{14,6},{16,24},{18,... | collective-permute-start | bytes 491528 | tf_op jit(solution)/shard_map/ppermute | solution.py:211
  3.0 1.5 %collective-permute-start.3 = (bf16[640,128]{1,0:T(8,128)(2,1)}, bf16[640,128]{1,0:T(8,128)(2,1)S(1)}, u32[]{:S(2)}, u32[]{:S(2)}) collective-permute-start(bf16[640,128]{1,0:T(8,128)(2,1)} %refs_4_.1), channel_id=1, source_target_pairs={{0,4},{2,6},{4,0},{6,2},{8,12},{10,14},{12,8},{14,10},{16,20},{18,... | collective-permute-start | bytes 491528 | tf_op jit(solution)/shard_map/ppermute | solution.py:220
  7.3 2.5 %collective-permute-start.13 = (bf16[640,128]{1,0:T(8,128)(2,1)}, bf16[640,128]{1,0:T(8,128)(2,1)S(1)}, u32[]{:S(2)}, u32[]{:S(2)}) collective-permute-start(bf16[640,128]{1,0:T(8,128)(2,1)} %refs_4_.1), channel_id=1, source_target_pairs={{0,24},{2,26},{4,28},{6,30},{8,16},{10,18},{12,20},{14,22},{16,8},... | collective-permute-start | bytes 491528 | tf_op jit(solution)/shard_map/ppermute | solution.py:211
  11.1 2.8 %outage_rows.1 = (bf16[8,2688]{1,0:T(8,128)(2,1)S(1)}, bf16[8,2688]{1,0:T(8,128)(2,1)S(1)}, bf16[8,2688]{1,0:T(8,128)(2,1)S(1)}, bf16[8,2688]{1,0:T(8,128)(2,1)S(1)}) custom-call(s32[4]{0:T(128)S(1)} %copy-done.2, s32[4]{0:T(128)S(1)} %collective-permute-done.other_ref, bf16[768,10240]{1,0:T(8,128)(2,1)} %f_ref.14), custom_call_target="tpu_custom_call" | custom-call | flops 3449999872 | bytes 1 | tf_op jit(solution)/shard_map/outage_rows/pallas_call | solution.py:269
  13.9 1.9 %collective-permute-start.7 = (bf16[8,2688]{1,0:T(8,128)(2,1)S(1)}, bf16[8,2688]{1,0:T(8,128)(2,1)S(1)}, u32[]{:S(2)}, u32[]{:S(2)}) collective-permute-start(bf16[8,2688]{1,0:T(8,128)(2,1)S(1)} %get-tuple-element.61), channel_id=1, source_target_pairs={{0,8},{2,10},{4,12},{6,14},{8,0},{10,2},{12,4},{14,6},{16,24},{18,... | collective-permute-start | bytes 129032 | tf_op jit(solution)/shard_map/ppermute | solution.py:211
  16.3 2.3 %collective-permute-start.8 = (bf16[8,2688]{1,0:T(8,128)(2,1)S(1)}, bf16[8,2688]{1,0:T(8,128)(2,1)S(1)}, u32[]{:S(2)}, u32[]{:S(2)}) collective-permute-start(bf16[8,2688]{1,0:T(8,128)(2,1)S(1)} %get-tuple-element.62), channel_id=1, source_target_pairs={{0,16},{2,18},{4,20},{6,22},{8,24},{10,26},{12,28},{14,30},{16,0},... | collective-permute-start | bytes 129032 | tf_op jit(solution)/shard_map/ppermute | solution.py:211
  19.5 3.1 %collective-permute-done.4.refs_3_.refs_7_ = bf16[640,128]{1,0:T(8,128)(2,1)S(1)} collective-permute-done((bf16[640,128]{1,0:T(8,128)(2,1)S(1)}, bf16[640,128]{1,0:T(8,128)(2,1)S(1)}, u32[]{:S(2)}, u32[]{:S(2)}) %collective-permute-start.4) | collective-permute-done | bytes 163872 | tf_op jit(solution)/shard_map/ppermute | solution.py:220
  22.7 3.5 %forward_own.1.refs_8_ = f32[768,128]{1,0:T(8,128)S(1)} custom-call(bf16[768,10240]{1,0:T(8,128)(2,1)} %f_ref.14, bf16[640,128]{1,0:T(8,128)(2,1)S(1)} %copy-done, bf16[640,128]{1,0:T(8,128)(2,1)S(1)} %collective-permute-done.2.refs_1_.refs_5_, bf16[640,128]{1,0:T(8,128)(2,1)S(1)} %collective-permute-done.3.refs_2_.refs_6_, ...), custom_call_target="tpu_custom_call" | custom-call | flops 4024999936 | bytes 1 | tf_op jit(solution)/shard_map/forward_own/pallas_call | solution.py:174
  26.5 2.7 %collective-permute-start.9 = (bf16[8,2688]{1,0:T(8,128)(2,1)S(1)}, bf16[8,2688]{1,0:T(8,128)(2,1)S(1)}, u32[]{:S(2)}, u32[]{:S(2)}) collective-permute-start(bf16[8,2688]{1,0:T(8,128)(2,1)S(1)} %get-tuple-element.63), channel_id=1, source_target_pairs={{0,24},{2,26},{4,28},{6,30},{8,16},{10,18},{12,20},{14,22},{16,8},... | collective-permute-start | bytes 129032 | tf_op jit(solution)/shard_map/ppermute | solution.py:211
  33.7 2.7 %collective-permute-done.10 = f32[32,128]{1,0:T(8,128)S(1)} collective-permute-done((f32[32,128]{1,0:T(8,128)S(1)}, f32[32,128]{1,0:T(8,128)S(1)}, u32[]{:S(2)}, u32[]{:S(2)}) %collective-permute-start.10) | collective-permute-done | bytes 16416 | tf_op jit(solution)/shard_map/ppermute | solution.py:211
  37.8 3.2 %collective-permute-done.15 = f32[32,128]{1,0:T(8,128)S(1)} collective-permute-done((f32[32,128]{1,0:T(8,128)S(1)}, f32[32,128]{1,0:T(8,128)S(1)}, u32[]{:S(2)}, u32[]{:S(2)}) %collective-permute-start.15) | collective-permute-done | bytes 16416 | tf_op jit(solution)/shard_map/ppermute | solution.py:211
  41.2 1.8 %collective-permute-start.6 = (bf16[1280,128]{1,0:T(8,128)(2,1)S(1)}, bf16[1280,128]{1,0:T(8,128)(2,1)S(1)}, u32[]{:S(2)}, u32[]{:S(2)}) collective-permute-start(bf16[1280,128]{1,0:T(8,128)(2,1)S(1)} %pad_maximum_fusion), channel_id=1, source_target_pairs={{0,4},{2,6},{4,0},{6,2},{8,12},{10,14},{12,8},{14,10},{16,20},{18,... | collective-permute-start | bytes 983048 | tf_op jit(solution)/shard_map/ppermute | solution.py:220
  44.6 6.9 %forward_most.1.refs_1_ = f32[768,128]{1,0:T(8,128)S(1)} custom-call(bf16[768,10240]{1,0:T(8,128)(2,1)} %f_ref.14, bf16[640,128]{1,0:T(8,128)(2,1)S(1)} %collective-permute-done.11.refs_0_, bf16[640,128]{1,0:T(8,128)(2,1)S(1)} %collective-permute-done.12.refs_1_, bf16[1280,128]{1,0:T(8,128)(2,1)S(1)} %collective-permute-done.16.refs_2_, ...), custom_call_target="tpu_custom_call" | custom-call | flops 6899999744 | bytes 1 | tf_op jit(solution)/shard_map/forward_most/pallas_call | solution.py:174
  53.2 2.5 %forward_last.1 = (f32[384,128]{1,0:T(8,128)S(1)}, f32[384,128]{1,0:T(8,128)S(1)}, bf16[768,640]{1,0:T(8,128)(2,1)S(1)}, bf16[768,640]{1,0:T(8,128)(2,1)S(1)}) custom-call(bf16[768,10240]{1,0:T(8,128)(2,1)} %f_ref.14, bf16[1280,128]{1,0:T(8,128)(2,1)S(1)} %collective-permute-done.6.refs_0_, f32[768,128]{1,0:T(8,128)S(1)} %forward_most.1.refs_1_), custom_call_target="tpu_custom_call" | custom-call | flops 2760000000 | bytes 1 | tf_op jit(solution)/shard_map/forward_last/pallas_call | solution.py:174
  57.3 2.1 %penalty.1 = (bf16[128,384]{1,0:T(8,128)(2,1)S(1)}, f32[128,128]{1,0:T(8,128)S(1)}) custom-call(s32[4]{0:T(128)S(1)} %copy-done.3, f32[384,128]{1,0:T(8,128)S(1)} %get-tuple-element.68.mine_ref, f32[384,128]{1,0:T(8,128)} %collective-permute-done.18.theirs_ref, f32[128,128]{1,0:T(8,128)S(1)} %pad_maximum_fusion.3.out_ref, ...), custom_call_target="tpu_custom_call" | custom-call | flops 575000000 | bytes 1 | tf_op jit(solution)/shard_map/penalty/pallas_call | solution.py:343
  62.2 2.8 %backward_3b.1 = (s16[128,1408]{1,0:T(8,128)(2,1)S(1)}, f32[128,640]{1,0:T(8,128)S(1)}, f32[128,640]{1,0:T(8,128)S(1)}) custom-call(bf16[768,10240]{1,0:T(8,128)(2,1)} %f_ref.14, bf16[128,384]{1,0:T(8,128)(2,1)S(1)} %get-tuple-element.83.a_ref, bf16[128,384]{1,0:T(8,128)(2,1)S(1)} %collective-permute-done.22.b_ref), custom_call_target="tpu_custom_call" | custom-call | flops 3795000064 | bytes 1 | tf_op jit(solution)/shard_map/backward_3b/pallas_call | solution.py:382
  66.5 3.7 %backward_2.1 = (s16[128,1408]{1,0:T(8,128)(2,1)S(1)}, f32[128,640]{1,0:T(8,128)S(1)}, f32[128,640]{1,0:T(8,128)S(1)}, f32[128,640]{1,0:T(8,128)S(1)}, f32[128,640]{1,0:T(8,128)S(1)}) custom-call(bf16[768,10240]{1,0:T(8,128)(2,1)} %f_ref.14, bf16[128,384]{1,0:T(8,128)(2,1)S(1)} %get-tuple-element.83.a_ref, bf16[128,384]{1,0:T(8,128)(2,1)S(1)} %collective-permute-done.22.b_ref), custom_call_target="tpu_custom_call" | custom-call | flops 4024999936 | bytes 1 | tf_op jit(solution)/shard_map/backward_2/pallas_call | solution.py:382
  71.6 2.7 %backward_0.1 = (f32[128,640]{1,0:T(8,128)S(1)}, f32[128,640]{1,0:T(8,128)S(1)}, f32[128,640]{1,0:T(8,128)S(1)}, f32[128,640]{1,0:T(8,128)S(1)}) custom-call(bf16[768,10240]{1,0:T(8,128)(2,1)} %f_ref.14, bf16[128,384]{1,0:T(8,128)(2,1)S(1)} %get-tuple-element.83.a_ref, bf16[128,384]{1,0:T(8,128)(2,1)S(1)} %collective-permute-done.22.b_ref), custom_call_target="tpu_custom_call" | custom-call | flops 3449999872 | bytes 1 | tf_op jit(solution)/shard_map/backward_0/pallas_call | solution.py:382
  74.2 2.7 %collective-permute-done.24.b_ref = s16[128,1024]{1,0:T(8,128)(2,1)S(1)} collective-permute-done((s16[128,1024]{1,0:T(8,128)(2,1)S(1)}, s16[128,1024]{1,0:T(8,128)(2,1)S(1)}, u32[]{:S(2)}, u32[]{:S(2)}) %collective-permute-start.24) | collective-permute-done | bytes 262176 | tf_op jit(solution)/shard_map/ppermute | solution.py:220
  78.0 1.9 %collective-permute-start.29 = (f32[32,128]{1,0:T(8,128)S(1)}, f32[32,128]{1,0:T(8,128)S(1)}, u32[]{:S(2)}, u32[]{:S(2)}) collective-permute-start(f32[32,128]{1,0:T(8,128)S(1)} %get-tuple-element.98), channel_id=1, source_target_pairs={{0,24},{2,26},{4,28},{6,30},{8,16},{10,18},{12,20},{14,22},{16,8},... | collective-permute-start | bytes 49160 | tf_op jit(solution)/shard_map/ppermute | solution.py:211
  79.9 2.5 %collective-permute-start.27 = (f32[32,128]{1,0:T(8,128)S(1)}, f32[32,128]{1,0:T(8,128)S(1)}, u32[]{:S(2)}, u32[]{:S(2)}) collective-permute-start(f32[32,128]{1,0:T(8,128)S(1)} %get-tuple-element.98), channel_id=1, source_target_pairs={{0,8},{2,10},{4,12},{6,14},{8,0},{10,2},{12,4},{14,6},{16,24},{18,... | collective-permute-start | bytes 49160 | tf_op jit(solution)/shard_map/ppermute | solution.py:211
  82.4 1.9 %collective-permute-start.31 = (s16[128,768]{1,0:T(8,128)(2,1)S(1)}, s16[128,768]{1,0:T(8,128)(2,1)S(1)}, u32[]{:S(2)}, u32[]{:S(2)}) collective-permute-start(s16[128,768]{1,0:T(8,128)(2,1)S(1)} %get-tuple-element.91), channel_id=1, source_target_pairs={{0,24},{2,26},{4,28},{6,30},{8,16},{10,18},{12,20},{14,22},{16,8},... | collective-permute-start | bytes 589832 | tf_op jit(solution)/shard_map/ppermute | solution.py:211
  94.4 2.3 %collective-permute-done.32.refs_1_.a_ref = s16[128,1408]{1,0:T(8,128)(2,1)S(1)} collective-permute-done((s16[128,1408]{1,0:T(8,128)(2,1)S(1)}, s16[128,1408]{1,0:T(8,128)(2,1)S(1)}, u32[]{:S(2)}, u32[]{:S(2)}) %collective-permute-start.32) | collective-permute-done | bytes 360480 | tf_op jit(solution)/shard_map/ppermute | solution.py:217
  98.0 4.6 %collective-permute-done.37.z2_ref = s16[128,768]{1,0:T(8,128)(2,1)S(1)} collective-permute-done((s16[128,768]{1,0:T(8,128)(2,1)S(1)}, s16[128,768]{1,0:T(8,128)(2,1)S(1)}, u32[]{:S(2)}, u32[]{:S(2)}) %collective-permute-start.37) | collective-permute-done | bytes 196640 | tf_op jit(solution)/shard_map/ppermute | solution.py:211
  (104 shorter events, 36.5 us)
Async XLA Ops:
  0.0 9.9 %collective-permute-start.11 = (bf16[640,128]{1,0:T(8,128)(2,1)}, bf16[640,128]{1,0:T(8,128)(2,1)S(1)}, u32[]{:S(2)}, u32[]{:S(2)}) collective-permute-start(bf16[640,128]{1,0:T(8,128)(2,1)} %refs_4_.1), channel_id=1, source_target_pairs={{0,8},{2,10},{4,12},{6,14},{8,0},{10,2},{12,4},{14,6},{16,24},{18,... | collective-permute-start | bytes 491528 | tf_op jit(solution)/shard_map/ppermute | solution.py:211
  3.0 13.3 %collective-permute-start.3 = (bf16[640,128]{1,0:T(8,128)(2,1)}, bf16[640,128]{1,0:T(8,128)(2,1)S(1)}, u32[]{:S(2)}, u32[]{:S(2)}) collective-permute-start(bf16[640,128]{1,0:T(8,128)(2,1)} %refs_4_.1), channel_id=1, source_target_pairs={{0,4},{2,6},{4,0},{6,2},{8,12},{10,14},{12,8},{14,10},{16,20},{18,... | collective-permute-start | bytes 491528 | tf_op jit(solution)/shard_map/ppermute | solution.py:220
  4.5 9.3 %collective-permute-start.2 = (bf16[640,128]{1,0:T(8,128)(2,1)}, bf16[640,128]{1,0:T(8,128)(2,1)S(1)}, u32[]{:S(2)}, u32[]{:S(2)}) collective-permute-start(bf16[640,128]{1,0:T(8,128)(2,1)} %refs_4_.1), channel_id=1, source_target_pairs={{0,2},{2,0},{4,6},{6,4},{8,10},{10,8},{12,14},{14,12},{16,18},{18,... | collective-permute-start | bytes 491528 | tf_op jit(solution)/shard_map/ppermute | solution.py:217
  7.3 11.3 %collective-permute-start.13 = (bf16[640,128]{1,0:T(8,128)(2,1)}, bf16[640,128]{1,0:T(8,128)(2,1)S(1)}, u32[]{:S(2)}, u32[]{:S(2)}) collective-permute-start(bf16[640,128]{1,0:T(8,128)(2,1)} %refs_4_.1), channel_id=1, source_target_pairs={{0,24},{2,26},{4,28},{6,30},{8,16},{10,18},{12,20},{14,22},{16,8},... | collective-permute-start | bytes 491528 | tf_op jit(solution)/shard_map/ppermute | solution.py:211
  9.8 16.7 %collective-permute-start.1 = (bf16[640,128]{1,0:T(8,128)(2,1)}, bf16[640,128]{1,0:T(8,128)(2,1)S(1)}, u32[]{:S(2)}, u32[]{:S(2)}) collective-permute-start(bf16[640,128]{1,0:T(8,128)(2,1)} %refs_4_.1), channel_id=1, source_target_pairs={{0,16},{2,18},{4,20},{6,22},{8,24},{10,26},{12,28},{14,30},{16,0},... | collective-permute-start | bytes 491528 | tf_op jit(solution)/shard_map/ppermute | solution.py:211
  13.9 16.6 %collective-permute-start.7 = (bf16[8,2688]{1,0:T(8,128)(2,1)S(1)}, bf16[8,2688]{1,0:T(8,128)(2,1)S(1)}, u32[]{:S(2)}, u32[]{:S(2)}) collective-permute-start(bf16[8,2688]{1,0:T(8,128)(2,1)S(1)} %get-tuple-element.61), channel_id=1, source_target_pairs={{0,8},{2,10},{4,12},{6,14},{8,0},{10,2},{12,4},{14,6},{16,24},{18,... | collective-permute-start | bytes 129032 | tf_op jit(solution)/shard_map/ppermute | solution.py:211
  15.8 6.9 %collective-permute-start.4 = (bf16[640,128]{1,0:T(8,128)(2,1)S(1)}, bf16[640,128]{1,0:T(8,128)(2,1)S(1)}, u32[]{:S(2)}, u32[]{:S(2)}) collective-permute-start(bf16[640,128]{1,0:T(8,128)(2,1)S(1)} %collective-permute-done.2.refs_1_.refs_5_), channel_id=1, source_target_pairs={{0,4},{2,6},{4,0},{6,2},{8,12},{10,14},{12,8},{14,10},{16,20},{18,... | collective-permute-start | bytes 491528 | tf_op jit(solution)/shard_map/ppermute | solution.py:220
  16.3 15.2 %collective-permute-start.8 = (bf16[8,2688]{1,0:T(8,128)(2,1)S(1)}, bf16[8,2688]{1,0:T(8,128)(2,1)S(1)}, u32[]{:S(2)}, u32[]{:S(2)}) collective-permute-start(bf16[8,2688]{1,0:T(8,128)(2,1)S(1)} %get-tuple-element.62), channel_id=1, source_target_pairs={{0,16},{2,18},{4,20},{6,22},{8,24},{10,26},{12,28},{14,30},{16,0},... | collective-permute-start | bytes 129032 | tf_op jit(solution)/shard_map/ppermute | solution.py:211
  18.6 10.6 %collective-permute-start.14 = (bf16[640,128]{1,0:T(8,128)(2,1)S(1)}, bf16[640,128]{1,0:T(8,128)(2,1)S(1)}, u32[]{:S(2)}, u32[]{:S(2)}) collective-permute-start(bf16[640,128]{1,0:T(8,128)(2,1)S(1)} %collective-permute-done.13.refs_3_), channel_id=1, source_target_pairs={{0,2},{2,0},{4,6},{6,4},{8,10},{10,8},{12,14},{14,12},{16,18},{18,... | collective-permute-start | bytes 491528 | tf_op jit(solution)/shard_map/ppermute | solution.py:217
  22.7 18.4 %collective-permute-start.16 = (bf16[1280,128]{1,0:T(8,128)(2,1)S(1)}, bf16[1280,128]{1,0:T(8,128)(2,1)S(1)}, u32[]{:S(2)}, u32[]{:S(2)}) collective-permute-start(bf16[1280,128]{1,0:T(8,128)(2,1)S(1)} %pad_maximum_fusion.1), channel_id=1, source_target_pairs={{0,4},{2,6},{4,0},{6,2},{8,12},{10,14},{12,8},{14,10},{16,20},{18,... | collective-permute-start | bytes 983048 | tf_op jit(solution)/shard_map/ppermute | solution.py:220
  29.2 11.9 %collective-permute-start.5 = (bf16[640,128]{1,0:T(8,128)(2,1)S(1)}, bf16[640,128]{1,0:T(8,128)(2,1)S(1)}, u32[]{:S(2)}, u32[]{:S(2)}) collective-permute-start(bf16[640,128]{1,0:T(8,128)(2,1)S(1)} %collective-permute-done.1.refs_6_), channel_id=1, source_target_pairs={{0,2},{2,0},{4,6},{6,4},{8,10},{10,8},{12,14},{14,12},{16,18},{18,... | collective-permute-start | bytes 491528 | tf_op jit(solution)/shard_map/ppermute | solution.py:217
  30.5 12.6 %collective-permute-start.17 = (bf16[1280,128]{1,0:T(8,128)(2,1)S(1)}, bf16[1280,128]{1,0:T(8,128)(2,1)S(1)}, u32[]{:S(2)}, u32[]{:S(2)}) collective-permute-start(bf16[1280,128]{1,0:T(8,128)(2,1)S(1)} %pad_maximum_fusion.2), channel_id=1, source_target_pairs={{0,4},{2,6},{4,0},{6,2},{8,12},{10,14},{12,8},{14,10},{16,20},{18,... | collective-permute-start | bytes 983048 | tf_op jit(solution)/shard_map/ppermute | solution.py:220
  41.2 12.0 %collective-permute-start.6 = (bf16[1280,128]{1,0:T(8,128)(2,1)S(1)}, bf16[1280,128]{1,0:T(8,128)(2,1)S(1)}, u32[]{:S(2)}, u32[]{:S(2)}) collective-permute-start(bf16[1280,128]{1,0:T(8,128)(2,1)S(1)} %pad_maximum_fusion), channel_id=1, source_target_pairs={{0,4},{2,6},{4,0},{6,2},{8,12},{10,14},{12,8},{14,10},{16,20},{18,... | collective-permute-start | bytes 983048 | tf_op jit(solution)/shard_map/ppermute | solution.py:220
  43.1 8.4 %collective-permute-start.20 = (f32[32,128]{1,0:T(8,128)S(1)}, f32[32,128]{1,0:T(8,128)S(1)}, u32[]{:S(2)}, u32[]{:S(2)}) collective-permute-start(f32[32,128]{1,0:T(8,128)S(1)} %add.40), channel_id=1, source_target_pairs={{0,2},{2,0},{4,6},{6,4},{8,10},{10,8},{12,14},{14,12},{16,18},{18,... | collective-permute-start | bytes 49160 | tf_op jit(solution)/shard_map/ppermute | solution.py:211
  61.5 8.7 %collective-permute-start.23 = (s16[128,1664]{1,0:T(8,128)(2,1)S(1)}, s16[128,1664]{1,0:T(8,128)(2,1)S(1)}, u32[]{:S(2)}, u32[]{:S(2)}) collective-permute-start(s16[128,1664]{1,0:T(8,128)(2,1)S(1)} %backward_3a.1), channel_id=1, source_target_pairs={{0,2},{2,0},{4,6},{6,4},{8,10},{10,8},{12,14},{14,12},{16,18},{18,... | collective-permute-start | bytes 1277960 | tf_op jit(solution)/shard_map/ppermute | solution.py:217
  65.0 17.4 %collective-permute-start.25 = (s16[128,1408]{1,0:T(8,128)(2,1)S(1)}, s16[128,1408]{1,0:T(8,128)(2,1)S(1)}, u32[]{:S(2)}, u32[]{:S(2)}) collective-permute-start(s16[128,1408]{1,0:T(8,128)(2,1)S(1)} %get-tuple-element.78), channel_id=1, source_target_pairs={{0,2},{2,0},{4,6},{6,4},{8,10},{10,8},{12,14},{14,12},{16,18},{18,... | collective-permute-start | bytes 1081352 | tf_op jit(solution)/shard_map/ppermute | solution.py:217
  70.5 6.4 %collective-permute-start.24 = (s16[128,1024]{1,0:T(8,128)(2,1)S(1)}, s16[128,1024]{1,0:T(8,128)(2,1)S(1)}, u32[]{:S(2)}, u32[]{:S(2)}) collective-permute-start(s16[128,1024]{1,0:T(8,128)(2,1)S(1)} %get-tuple-element.82), channel_id=1, source_target_pairs={{0,4},{2,6},{4,0},{6,2},{8,12},{10,14},{12,8},{14,10},{16,20},{18,... | collective-permute-start | bytes 786440 | tf_op jit(solution)/shard_map/ppermute | solution.py:220
  77.4 9.6 %collective-permute-start.26 = (s16[128,1408]{1,0:T(8,128)(2,1)S(1)}, s16[128,1408]{1,0:T(8,128)(2,1)S(1)}, u32[]{:S(2)}, u32[]{:S(2)}) collective-permute-start(s16[128,1408]{1,0:T(8,128)(2,1)S(1)} %get-tuple-element.94), channel_id=1, source_target_pairs={{0,2},{2,0},{4,6},{6,4},{8,10},{10,8},{12,14},{14,12},{16,18},{18,... | collective-permute-start | bytes 1081352 | tf_op jit(solution)/shard_map/ppermute | solution.py:217
  78.0 6.5 %collective-permute-start.29 = (f32[32,128]{1,0:T(8,128)S(1)}, f32[32,128]{1,0:T(8,128)S(1)}, u32[]{:S(2)}, u32[]{:S(2)}) collective-permute-start(f32[32,128]{1,0:T(8,128)S(1)} %get-tuple-element.98), channel_id=1, source_target_pairs={{0,24},{2,26},{4,28},{6,30},{8,16},{10,18},{12,20},{14,22},{16,8},... | collective-permute-start | bytes 49160 | tf_op jit(solution)/shard_map/ppermute | solution.py:211
  82.4 9.7 %collective-permute-start.31 = (s16[128,768]{1,0:T(8,128)(2,1)S(1)}, s16[128,768]{1,0:T(8,128)(2,1)S(1)}, u32[]{:S(2)}, u32[]{:S(2)}) collective-permute-start(s16[128,768]{1,0:T(8,128)(2,1)S(1)} %get-tuple-element.91), channel_id=1, source_target_pairs={{0,24},{2,26},{4,28},{6,30},{8,16},{10,18},{12,20},{14,22},{16,8},... | collective-permute-start | bytes 589832 | tf_op jit(solution)/shard_map/ppermute | solution.py:211
  89.2 7.5 %collective-permute-start.32 = (s16[128,1408]{1,0:T(8,128)(2,1)S(1)}, s16[128,1408]{1,0:T(8,128)(2,1)S(1)}, u32[]{:S(2)}, u32[]{:S(2)}) collective-permute-start(s16[128,1408]{1,0:T(8,128)(2,1)S(1)} %get-tuple-element.101), channel_id=1, source_target_pairs={{0,2},{2,0},{4,6},{6,4},{8,10},{10,8},{12,14},{14,12},{16,18},{18,... | collective-permute-start | bytes 1081352 | tf_op jit(solution)/shard_map/ppermute | solution.py:217
  90.9 11.7 %collective-permute-start.37 = (s16[128,768]{1,0:T(8,128)(2,1)S(1)}, s16[128,768]{1,0:T(8,128)(2,1)S(1)}, u32[]{:S(2)}, u32[]{:S(2)}) collective-permute-start(s16[128,768]{1,0:T(8,128)(2,1)S(1)} %sum_z2.1), channel_id=1, source_target_pairs={{0,16},{2,18},{4,20},{6,22},{8,24},{10,26},{12,28},{14,30},{16,0},... | collective-permute-start | bytes 589832 | tf_op jit(solution)/shard_map/ppermute | solution.py:211
  93.8 9.6 %collective-permute-start.36 = (s16[128,768]{1,0:T(8,128)(2,1)S(1)}, s16[128,768]{1,0:T(8,128)(2,1)S(1)}, u32[]{:S(2)}, u32[]{:S(2)}) collective-permute-start(s16[128,768]{1,0:T(8,128)(2,1)S(1)} %sum_z1.1), channel_id=1, source_target_pairs={{0,8},{2,10},{4,12},{6,14},{8,0},{10,2},{12,4},{14,6},{16,24},{18,... | collective-permute-start | bytes 589832 | tf_op jit(solution)/shard_map/ppermute | solution.py:211
  96.9 6.5 %collective-permute-start.35 = (s16[128,768]{1,0:T(8,128)(2,1)S(1)}, s16[128,768]{1,0:T(8,128)(2,1)S(1)}, u32[]{:S(2)}, u32[]{:S(2)}) collective-permute-start(s16[128,768]{1,0:T(8,128)(2,1)S(1)} %sum_0.1), channel_id=1, source_target_pairs={{0,4},{2,6},{4,0},{6,2},{8,12},{10,14},{12,8},{14,10},{16,20},{18,... | collective-permute-start | bytes 589832 | tf_op jit(solution)/shard_map/ppermute | solution.py:220
  (22 other events, 157.9 us)
